TPU v7x, 128 devices: a whole 4x4x4 slice. The times are simulated.
128 devices in a mesh: rows: 32 (over x, y, core), cols: 4 (over z).
Axes of the slice: x: 4, y: 4, z: 4, core: 2. Of those that a mesh axis runs over, the one named last changes fastest.
Arguments:
- features: bfloat16 [4, 128, 512, 256], P(None, 'rows', 'cols'), may hold values from -450 to 450
- conv_weight: bfloat16 [3, 3, 256, 512], replicated, may hold values from -0.125 to 0.125
- bn_gain: float32 [512], replicated, may hold values from 0.1 to 1.9
- bn_bias: float32 [512], replicated, may hold values from -3 to 3
- head_weight: bfloat16 [512, 4], replicated, may hold values from -0.25 to 0.25
- labels: int32 [4, 128, 512], P(None, 'rows', 'cols'), may hold values from 0 to 3
- raster: int32 [4, 128, 512], P(None, 'rows', 'cols'), may hold values 0 or 1
Outputs:
- grad_weight: float32 [3, 3, 256, 512], P(None, None, None, 'cols')
- grad_gain: float32 [512], P('cols')
- grad_bias: float32 [512], P('cols')
- grad_head: float32 [512, 4], P('cols')
- grad_input: float32 [4, 128, 512, 256], P(None, 'rows', 'cols')
All inputs are finite; a program needn't handle non-finite values. No bound on the sum of `raster` on one device may be relied on, other than what follows from the above.
Results may differ from a plain program's by a relative error of at most 0.009.
Values may be sent and summed in bfloat16 or wider, within the bound.
A program may use at most 192 MiB of HBM per device.

v0:
```python
import jax
import jax.numpy as jnp
from jax import lax
from jax.sharding import PartitionSpec as P


def with_halo(block, sides, width):
    for axis, dim in sides:
        count = lax.axis_size(axis)
        forward = [(i, i + 1) for i in range(count - 1)]
        backward = [(target, source) for source, target in forward]
        low = lax.ppermute(
            lax.slice_in_dim(block, block.shape[dim] - width, None, axis=dim), axis, forward
        )
        high = lax.ppermute(lax.slice_in_dim(block, 0, width, axis=dim), axis, backward)
        block = jnp.concatenate([low, block, high], axis=dim)
    return block


def shifted_conv(padded, kernel):
    height = padded.shape[1] - 2
    width = padded.shape[2] - 2
    total = None
    for offset_row in range(3):
        for offset_col in range(3):
            window = padded[:, offset_row : offset_row + height, offset_col : offset_col + width]
            term = jnp.einsum(
                "bhwc,co->bhwo",
                window,
                kernel[offset_row, offset_col],
                preferred_element_type=jnp.float32,
            )
            total = term if total is None else total + term
    return total


def back_conv(padded_grad, kernel):
    height = padded_grad.shape[1] - 2
    width = padded_grad.shape[2] - 2
    total = None
    for offset_row in range(3):
        for offset_col in range(3):
            window = padded_grad[
                :, 2 - offset_row : 2 - offset_row + height, 2 - offset_col : 2 - offset_col + width
            ]
            term = jnp.einsum(
                "bhwo,co->bhwc",
                window,
                kernel[offset_row, offset_col],
                preferred_element_type=jnp.float32,
            )
            total = term if total is None else total + term
    return total


def kernel_grad(padded, grad):
    height = grad.shape[1]
    width = grad.shape[2]
    layers = []
    for offset_row in range(3):
        line = []
        for offset_col in range(3):
            window = padded[:, offset_row : offset_row + height, offset_col : offset_col + width]
            line.append(
                jnp.einsum("bhwc,bhwo->co", window, grad, preferred_element_type=jnp.float32)
            )
        layers.append(jnp.stack(line))
    return jnp.stack(layers)


def per_device(features, conv_weight, bn_gain, bn_bias, head_weight, labels, raster):
    batch, rows_here, cols_here, channels = features.shape
    n_rows = lax.axis_size("rows")
    n_cols = lax.axis_size("cols")
    count = float(batch * rows_here * n_rows * cols_here * n_cols)
    share = conv_weight.shape[3] // n_cols
    first = lax.axis_index("cols") * share
    padded = with_halo(features, (("rows", 1), ("cols", 2)), 1)

    def reduce_all(values):
        return lax.psum(values, ("rows", "cols"))

    conv = shifted_conv(padded, conv_weight)
    mean = reduce_all(jnp.sum(conv, axis=(0, 1, 2))) / count
    var = reduce_all(jnp.sum((conv - mean) ** 2, axis=(0, 1, 2))) / count
    rstd = lax.rsqrt(var + 1e-05)
    normed = (conv - mean) * rstd
    preact = bn_gain * normed + bn_bias
    act = jnp.maximum(preact, 0.0).astype(jnp.bfloat16)
    partial_logits = jnp.einsum(
        "bhwo,oq->bhwq", act, head_weight, preferred_element_type=jnp.float32
    )
    expo = jnp.exp(partial_logits)
    probs = expo / jnp.sum(expo, axis=-1, keepdims=True)
    onehot = (labels[..., None] == jnp.arange(partial_logits.shape[-1], dtype=jnp.int32)).astype(
        jnp.float32
    )
    pixel_weight = (1 + raster).astype(jnp.float32)
    score_grad = (pixel_weight[..., None] * (probs - onehot) / float(batch)).astype(jnp.bfloat16)
    head_part = jnp.einsum("bhwo,bhwq->oq", act, score_grad, preferred_element_type=jnp.float32)
    act_grad = jnp.einsum(
        "bhwq,oq->bhwo", score_grad, head_weight, preferred_element_type=jnp.float32
    )
    pre_grad = jnp.where(preact > 0, act_grad, 0.0)
    head_total, bias_total, gain_total = reduce_all(
        (head_part, jnp.sum(pre_grad, axis=(0, 1, 2)), jnp.sum(pre_grad * normed, axis=(0, 1, 2)))
    )
    conv_grad = (
        bn_gain * rstd * (pre_grad - bias_total / count - normed * gain_total / count)
    ).astype(jnp.bfloat16)
    weight_part = kernel_grad(padded, conv_grad)
    padded_grad = with_halo(conv_grad, (("rows", 1), ("cols", 2)), 1)
    grad_input = back_conv(padded_grad, conv_weight)
    weight_total = lax.psum(weight_part, ("rows", "cols"))
    grad_weight = lax.dynamic_slice_in_dim(weight_total, first, share, 3)
    grad_gain = lax.dynamic_slice_in_dim(gain_total, first, share, 0)
    grad_bias = lax.dynamic_slice_in_dim(bias_total, first, share, 0)
    grad_head = lax.dynamic_slice_in_dim(head_total, first, share, 0)
    return (grad_weight, grad_gain, grad_bias, grad_head, grad_input)


def solution(mesh):
    in_specs = (
        P(None, "rows", "cols", None),
        P(),
        P(),
        P(),
        P(),
        P(None, "rows", "cols"),
        P(None, "rows", "cols"),
    )
    out_specs = (
        P(None, None, None, "cols"),
        P("cols"),
        P("cols"),
        P("cols", None),
        P(None, "rows", "cols", None),
    )
    return jax.shard_map(
        per_device, mesh=mesh, in_specs=in_specs, out_specs=out_specs, check_vma=False
    )
```

profile of v0, /device:TPU:1, one launch (start us, length us, event | category | flops | bytes accessed | tf_op | source)
XLA Modules:
  0.0 445.7 jit_solution(14480637846800466050)
XLA Ops:
  7.2 0.0 copy-start
  7.2 0.0 all-reduce.3.cloned.1.call-start
  7.2 1.9 fusion.112
  9.1 4.6 %collective-permute-start = (bf16[4,1,128,256]{3,2,1,0:T(8,128)(2,1)S(1)}, bf16[4,1,128,256]{3,2,1,0:T(8,128)(2,1)S(1)}, u32[]{:S(2)}, u32[]{:S(2)}) collective-permute-start(bf16[4,1,128,256]{3,2,1,0:T(8,128)(2,1)S(1)} %get-tuple-element.21), channel_id=1, source_target_pairs={{0,4},{4,8},{8,12},{12,16},{16,20},{20,24},{24,28},{28,32},{32,36}... | collective-permute-start | bytes 786440 | tf_op jit(solution)/shard_map/ppermute | solution.py:12
  13.7 1.9 collective-permute-start.1
  15.6 3.6 fusion.48
  19.3 0.0 copy-start.8
  19.3 1.6 constant_dynamic-update-slice_fusion.3
  20.9 0.7 collective-permute-done.1
  21.6 0.0 copy-start.2
  21.7 3.5 collective-permute-start.2
  25.2 1.3 collective-permute-start.3
  26.6 2.6 fusion.39
  29.2 2.6 fusion.57
  31.8 0.7 fusion.51
  32.6 0.7 fusion.60
  33.3 0.7 fusion.54
  34.0 2.7 fusion.44
  36.7 2.7 fusion.30
  39.4 9.7 %fusion.113 = (f32[512]{0:T(512)S(1)}, f32[4,4,128,512]{3,2,1,0:T(8,128)}) fusion(bf16[3,3,256,512]{3,2,1,0:T(8,128)(2,1)} %param.8, bf16[4,6,1,256]{3,2,1,0:T(2,128)(2,1)S(1)} %collective-permute-done.3, bf16[4,6,128,256]{3,2,1,0:T(8,128)(2,1)S(1)} %get-tuple-element.25, f32[4,4,128,512]{3,2,1,0:T(8,128)} %fusion.39, f32[4,4,128,512]{3,2,1,0:T(8,128)} %fusion.30, ...), kind=kOutput, calls=%fused_computation.154 | convolution fusion | flops 548404736 | bytes 39598080 | tf_op jit(solution)/shard_map/bhwc,co->bhwo/dot_general | solution.py:27
  49.1 68.7 %psum.42 = f32[512]{0:T(512)S(1)} all-reduce(f32[512]{0:T(512)S(1)} %get-tuple-element.29), channel_id=1, replica_groups=mesh['rows'=32,'cols'=4] {'rows','cols'}, use_global_device_ids=true, to_apply=%region_1.0 | all-reduce | flops 512 | bytes 4096 | tf_op jit(solution)/shard_map/psum | solution.py:81
  117.8 2.7 multiply_reduce_fusion.1
  120.5 63.7 %psum.43 = f32[512]{0:T(512)S(1)} all-reduce(f32[512]{0:T(512)S(1)} %multiply_reduce_fusion.1), channel_id=1, replica_groups=mesh['rows'=32,'cols'=4] {'rows','cols'}, use_global_device_ids=true, to_apply=%region_3.0 | all-reduce | flops 512 | bytes 4096 | tf_op jit(solution)/shard_map/psum | solution.py:81
  184.2 3.1 convolution_exponential_fusion
  187.3 3.1 convolution_bitcast_fusion.9
  190.4 5.7 %fusion.109 = (f32[512]{0:T(512)S(1)}, f32[512]{0:T(512)S(1)}, f32[4,4,128,512]{3,2,1,0:T(8,128)}) fusion(f32[512]{0:T(512)S(1)} %get-tuple-element.28, f32[4,4,128,512]{3,2,1,0:T(8,128)} %get-tuple-element.30, f32[512]{0:T(512)S(1)} %broadcast_multiply_fusion.1, bf16[512,4]{0,1:T(4,128)(2,1)S(1)} %copy-done, ...), kind=kOutput, calls=%fused_computation.150 | convolution fusion | flops 17884164 | bytes 8454144 | tf_op jit(solution)/shard_map/bhwq,oq->bhwo/dot_general | solution.py:101
  196.1 63.0 %all-reduce = (f32[512]{0:T(512)S(1)}, f32[512]{0:T(512)S(1)}, f32[512,4]{0,1:T(4,128)S(1)}) all-reduce(f32[512]{0:T(512)S(1)} %get-tuple-element.6, f32[512]{0:T(512)S(1)} %get-tuple-element.5, f32[512,4]{0,1:T(4,128)S(1)} %convolution_bitcast_fusion.9), channel_id=1, replica_groups=mesh['rows'=32,'cols'=4] {'rows','cols'}, use_global_device_ids=true, to_apply=%region_8.9 | all-reduce | flops 3072 | bytes 24576 | tf_op jit(solution)/shard_map/psum | solution.py:81
  259.1 4.6 %multiply_convert_fusion = bf16[4,4,128,512]{3,2,1,0:T(8,128)(2,1)S(1)} fusion(f32[4,4,128,512]{3,2,1,0:T(8,128)} %get-tuple-element.31, f32[4,4,128,512]{3,2,1,0:T(8,128)} %get-tuple-element.30, f32[512]{0:T(512)S(1)} %get-tuple-element.7, f32[512]{0:T(512)S(1)} %broadcast_multiply_fusion, f32[512]{0:T(512)S(1)} %get-tuple-element.28, ...), kind=kLoop, calls=%fused_computation.2 | loop fusion | flops 8388608 | bytes 10496000 | tf_op jit(solution)/shard_map/convert_element_type | solution.py:110
  263.7 1.0 fusion.110
  264.8 0.6 copy-done.5
  265.4 0.7 convolution_bitcast_fusion.1
  266.2 0.5 copy-done.7
  266.7 0.8 convolution_bitcast_fusion.5
  267.4 0.7 convolution_bitcast_fusion
  268.1 2.5 collective-permute-start.5
  270.7 3.2 collective-permute-start.4
  274.0 0.7 convolution_bitcast_fusion.3
  274.7 0.7 convolution_bitcast_fusion.2
  275.5 0.1 maximum_bitcast_fusion.2
  275.6 0.7 convolution_bitcast_fusion.6
  276.3 0.7 convolution_bitcast_fusion.4
  277.1 0.7 convolution_bitcast_fusion.8
  277.8 0.7 convolution_bitcast_fusion.7
  278.6 0.3 maximum_bitcast_fusion
  278.9 2.7 pad_maximum_fusion
  281.6 0.6 dynamic_slice.13
  282.2 0.6 dynamic_slice.14
  282.8 0.0 all-reduce.3.cloned.1.call-update
  282.8 0.6 constant_dynamic-slice_fusion
  283.4 1.7 fusion.46
  285.1 0.1 pad_maximum_fusion.10
  285.2 1.4 collective-permute-start.6
  286.6 4.0 collective-permute-start.7
  290.6 0.7 fusion.1
  291.4 0.7 fusion.5
  292.1 1.5 maximum_maximum_fusion
  293.7 0.8 fusion.11
  294.4 0.8 fusion.15
  295.2 0.7 fusion.13
  295.9 0.7 fusion.17
  296.7 0.8 fusion.19
  297.5 2.4 add_add_fusion.1
  299.8 136.7 %all-reduce.3.cloned.1.call-done = f32[3,3,256,512]{3,2,1,0:T(8,128)} async-done(((f32[3,3,256,512]{3,2,1,0:T(8,128)}), f32[3,3,256,512]{3,2,1,0:T(8,128)}) %all-reduce.3.cloned.1.call-update) | async-done | bytes 4718608 | tf_op jit(solution)/shard_map/psum | solution.py:114
  436.5 2.4 constant_dynamic-slice_fusion.1
  (37 shorter events, 0.2 us)
Async XLA Ops:
  7.2 177.0 %copy-start = (bf16[512,4]{0,1:T(4,128)(2,1)S(1)}, bf16[512,4]{0,1:T(4,128)(2,1)}, u32[]{:S(2)}) copy-start(bf16[512,4]{0,1:T(4,128)(2,1)} %param.11) | copy-start | bytes 12292
  7.2 8.4 %copy-start.6 = (bf16[4,4,128,256]{3,2,1,0:T(8,128)(2,1)S(1)}, bf16[4,4,128,256]{3,2,1,0:T(8,128)(2,1)}, u32[]{:S(2)}) copy-start(bf16[4,4,128,256]{3,2,1,0:T(8,128)(2,1)} %param.7) | copy-start | bytes 3145732
  7.2 429.3 %all-reduce.3.cloned.1.call-start = ((), (), s32[]{:S(2)}) async-start(), calls=%async_computation | async-start | bytes 9437184 | tf_op jit(solution)/shard_map/psum | solution.py:114
  9.1 10.1 %collective-permute-start = (bf16[4,1,128,256]{3,2,1,0:T(8,128)(2,1)S(1)}, bf16[4,1,128,256]{3,2,1,0:T(8,128)(2,1)S(1)}, u32[]{:S(2)}, u32[]{:S(2)}) collective-permute-start(bf16[4,1,128,256]{3,2,1,0:T(8,128)(2,1)S(1)} %get-tuple-element.21), channel_id=1, source_target_pairs={{0,4},{4,8},{8,12},{12,16},{16,20},{20,24},{24,28},{28,32},{32,36}... | collective-permute-start | bytes 786440 | tf_op jit(solution)/shard_map/ppermute | solution.py:12
  13.7 5.5 %copy-start.10 = (s32[4,4,128]{2,1,0:T(4,128)S(1)}, s32[4,4,128]{2,1,0:T(4,128)}, u32[]{:S(2)}) copy-start(s32[4,4,128]{2,1,0:T(4,128)} %param.13) | copy-start | bytes 24580
  13.7 7.9 %collective-permute-start.1 = (bf16[4,1,128,256]{3,2,1,0:T(8,128)(2,1)}, bf16[4,1,128,256]{3,2,1,0:T(8,128)(2,1)S(1)}, u32[]{:S(2)}, u32[]{:S(2)}) collective-permute-start(bf16[4,1,128,256]{3,2,1,0:T(8,128)(2,1)} %get-tuple-element.22), channel_id=1, source_target_pairs={{4,0},{8,4},{12,8},{16,12},{20,16},{24,20},{28,24},{32,28},{36,32}... | collective-permute-start | bytes 786440 | tf_op jit(solution)/shard_map/ppermute | solution.py:15
  19.3 7.3 %copy-start.8 = (bf16[3,3,256,512]{3,2,1,0:T(8,128)(2,1)S(1)}, bf16[3,3,256,512]{3,2,1,0:T(8,128)(2,1)}, u32[]{:S(2)}) copy-start(bf16[3,3,256,512]{3,2,1,0:T(8,128)(2,1)} %param.8) | copy-start | bytes 7077892
  20.9 8.3 %copy-start.4 = (bf16[4,5,128,256]{3,2,1,0:T(8,128)(2,1)}, bf16[4,5,128,256]{3,2,1,0:T(8,128)(2,1)S(1)}, u32[]{:S(2)}) copy-start(bf16[4,5,128,256]{3,2,1,0:T(8,128)(2,1)S(1)} %get-tuple-element.18) | copy-start | bytes 3932164
  21.6 17.7 %copy-start.2 = (bf16[4,6,128,256]{3,2,1,0:T(8,128)(2,1)}, bf16[4,6,128,256]{3,2,1,0:T(8,128)(2,1)S(1)}, u32[]{:S(2)}) copy-start(bf16[4,6,128,256]{3,2,1,0:T(8,128)(2,1)S(1)} %get-tuple-element.25) | copy-start | bytes 4718596
  21.7 10.1 %collective-permute-start.2 = (bf16[4,6,1,256]{3,2,1,0:T(2,128)(2,1)S(1)}, bf16[4,6,1,256]{3,2,1,0:T(2,128)(2,1)S(1)}, u32[]{:S(2)}, u32[]{:S(2)}) collective-permute-start(bf16[4,6,1,256]{3,2,1,0:T(2,128)(2,1)S(1)} %get-tuple-element.17), channel_id=1, source_target_pairs={{0,1},{1,2},{2,3},{4,5},{5,6},{6,7},{8,9},{9,10},{10,11},{12,13},{... | collective-permute-start | bytes 36872 | tf_op jit(solution)/shard_map/ppermute | solution.py:12
  25.2 8.0 %collective-permute-start.3 = (bf16[4,6,1,256]{3,2,1,0:T(2,128)(2,1)S(1)}, bf16[4,6,1,256]{3,2,1,0:T(2,128)(2,1)S(1)}, u32[]{:S(2)}, u32[]{:S(2)}) collective-permute-start(bf16[4,6,1,256]{3,2,1,0:T(2,128)(2,1)S(1)} %get-tuple-element.16), channel_id=1, source_target_pairs={{1,0},{2,1},{3,2},{5,4},{6,5},{7,6},{9,8},{10,9},{11,10},{13,12},{... | collective-permute-start | bytes 36872 | tf_op jit(solution)/shard_map/ppermute | solution.py:15
  117.7 66.4 %copy-start.11 = (f32[512]{0:T(512)S(1)}, f32[512]{0:T(512)}, u32[]{:S(2)}) copy-start(f32[512]{0:T(512)} %param.9) | copy-start | bytes 6148
  117.8 66.4 %copy-start.13 = (f32[512]{0:T(512)S(1)}, f32[512]{0:T(512)}, u32[]{:S(2)}) copy-start(f32[512]{0:T(512)} %param.10) | copy-start | bytes 6148
  184.2 3.1 copy-start.12
  263.7 1.7 copy-start.5
  265.4 1.2 copy-start.7
  267.4 6.5 %copy-start.3 = (bf16[4,6,128,256]{3,2,1,0:T(8,128)(2,1)S(1)}, bf16[4,6,128,256]{3,2,1,0:T(8,128)(2,1)}, u32[]{:S(2)}) copy-start(bf16[4,6,128,256]{3,2,1,0:T(8,128)(2,1)} %copy-done.2) | copy-start | bytes 4718596
  268.1 16.9 %collective-permute-start.5 = (bf16[4,1,128,512]{3,2,1,0:T(8,128)(2,1)}, bf16[4,1,128,512]{3,2,1,0:T(8,128)(2,1)S(1)}, u32[]{:S(2)}, u32[]{:S(2)}) collective-permute-start(bf16[4,1,128,512]{3,2,1,0:T(8,128)(2,1)} %get-tuple-element.14), channel_id=1, source_target_pairs={{4,0},{8,4},{12,8},{16,12},{20,16},{24,20},{28,24},{32,28},{36,32}... | collective-permute-start | bytes 1572872 | tf_op jit(solution)/shard_map/ppermute | solution.py:15
  270.7 14.4 %collective-permute-start.4 = (bf16[4,1,128,512]{3,2,1,0:T(8,128)(2,1)}, bf16[4,1,128,512]{3,2,1,0:T(8,128)(2,1)S(1)}, u32[]{:S(2)}, u32[]{:S(2)}) collective-permute-start(bf16[4,1,128,512]{3,2,1,0:T(8,128)(2,1)} %get-tuple-element.15), channel_id=1, source_target_pairs={{0,4},{4,8},{8,12},{12,16},{16,20},{20,24},{24,28},{28,32},{32,36}... | collective-permute-start | bytes 1572872 | tf_op jit(solution)/shard_map/ppermute | solution.py:12
  285.1 5.6 %copy-start.9 = (bf16[3,3,256,512]{3,2,1,0:T(8,128)(2,1)S(1)}, bf16[3,3,256,512]{3,2,1,0:T(8,128)(2,1)}, u32[]{:S(2)}) copy-start(bf16[3,3,256,512]{3,2,1,0:T(8,128)(2,1)} %param.8) | copy-start | bytes 7077892
  285.2 6.9 %collective-permute-start.6 = (bf16[4,6,1,512]{3,2,1,0:T(2,128)(2,1)S(1)}, bf16[4,6,1,512]{3,2,1,0:T(2,128)(2,1)S(1)}, u32[]{:S(2)}, u32[]{:S(2)}) collective-permute-start(bf16[4,6,1,512]{3,2,1,0:T(2,128)(2,1)S(1)} %get-tuple-element.13), channel_id=1, source_target_pairs={{1,0},{2,1},{3,2},{5,4},{6,5},{7,6},{9,8},{10,9},{11,10},{13,12},{... | collective-permute-start | bytes 73736 | tf_op jit(solution)/shard_map/ppermute | solution.py:15
  286.6 5.5 %collective-permute-start.7 = (bf16[4,6,1,512]{3,2,1,0:T(2,128)(2,1)S(1)}, bf16[4,6,1,512]{3,2,1,0:T(2,128)(2,1)S(1)}, u32[]{:S(2)}, u32[]{:S(2)}) collective-permute-start(bf16[4,6,1,512]{3,2,1,0:T(2,128)(2,1)S(1)} %get-tuple-element.12), channel_id=1, source_target_pairs={{0,1},{1,2},{2,3},{4,5},{5,6},{6,7},{8,9},{9,10},{10,11},{12,13},{... | collective-permute-start | bytes 73736 | tf_op jit(solution)/shard_map/ppermute | solution.py:12
  297.4 141.4 %copy-start.1 = (bf16[512,4]{0,1:T(4,128)(2,1)S(1)}, bf16[512,4]{0,1:T(4,128)(2,1)}, u32[]{:S(2)}) copy-start(bf16[512,4]{0,1:T(4,128)(2,1)} %param.11) | copy-start | bytes 12292
Sparse Core Ops, SparseCore 0:
  282.9 153.5 all-reduce.2
where the time goes:
time: 447 us; the launch traced here: 446 us
  blocking collectives  195 us (44%)
  waiting for transfers between devices  137 us (31%)
  matrix products  53.8 us (12%)
  starting transfers between devices  22.6 us (5%)
  between operations  14.5 us (3%)
  other arithmetic  12.1 us (3%)
  local copies, waits for them, and re-layouts  9.92 us (2%)
    psum x3, blocking collectives, reduce_all(): return lax.psum(values, ('rows', 'cols'))  195 us
    psum x1, waiting for transfers between devices, per_device(): weight_total = lax.psum(weight_part, ('rows', 'cols'))  137 us
    dot_general x9, matrix products, shifted_conv(): jnp.einsum('bhwc,co->bhwo', window, kernel[offset_row, offset_col], prefe...  26.1 us
    ppermute x4, starting transfers between devices, with_halo(): lax.ppermute(lax.slice_in_dim(block, block.shape[dim] - width, None, axis...  15.4 us
    dot_general x9, matrix products, back_conv(): jnp.einsum('bhwo,co->bhwc', window, kernel[offset_row, offset_col], prefe...  9.27 us
  transfers between devices with their start and end apart: 9, of which 2 were waited for; matrix products, arithmetic and copies ran while one was open for 7% of the time, Pallas kernels for 0%

commit v1 on v0

v1 whole, which is shorter than its diff:
```python
import jax
import jax.numpy as jnp
from jax import lax
from jax.experimental import pallas as pl
from jax.experimental.pallas import tpu as pltpu
from jax.sharding import PartitionSpec as P

F32 = jnp.float32
BF16 = jnp.bfloat16
MESH = pl.DeviceIdType.MESH

B = 4
H = 4
W = 128
CI = 256
CO = 512
TAPS = 9
PIX = H * W
COUNT = 4.0 * 128.0 * 512.0
EPS = 1e-05
OWN = 1152
PART = 80


def part_start(j):
    return pl.multiple_of(((9 * j) // 2) * 16, 16)


def kernel(
    feat,
    wgt_hbm,
    gain_ref,
    bias_ref,
    head_ref,
    labels_ref,
    raster_ref,
    gw_out,
    gg_out,
    gb_out,
    gh_out,
    gi_out,
    wgt,
    wgt_t,
    xl,
    xc,
    xr,
    xt,
    conv,
    pgs,
    act,
    sgs,
    onehot,
    pixw,
    head_pad,
    head_tile,
    head_t,
    gl,
    gc,
    gr,
    xrow,
    xedge_out,
    xedge_in,
    grow,
    gedge_f,
    gedge_out,
    gedge_in,
    st_local,
    st8,
    st16,
    tot8,
    tot16,
    hd8,
    hd16,
    head_all,
    part,
    send_a,
    recv_a,
    send_b,
    recv_b,
    sum_c,
    send_c,
    recv_c,
    gath,
    gath_other,
    wsem,
    xrow_s,
    xrow_r,
    xedge_s,
    xedge_r,
    grow_s,
    grow_r,
    gedge_s,
    gedge_r,
    s8_s,
    s8_r,
    s16_s,
    s16_r,
    t8_s,
    t8_r,
    t16_s,
    t16_r,
    h8_s,
    h8_r,
    h16_s,
    h16_r,
    a_s,
    a_r,
    b_s,
    b_r,
    c_s,
    c_r,
    g_s,
    g_r,
    o_s,
    o_r,
):
    me = lax.axis_index("rows")
    z = lax.axis_index("cols")
    core = lax.rem(me, 2)
    chip = me // 2
    rank8 = z * 2 + core

    def dev8(j):
        return (chip * 2 + lax.rem(j, 2), j // 2)

    def dev16(j):
        return (j * 2 + core, z)

    other = (chip * 2 + 1 - core, z)
    up = lax.rem(me + 31, 32)
    down = lax.rem(me + 1, 32)
    west = lax.rem(z + 3, 4)
    east = lax.rem(z + 1, 4)
    beyond = lax.rem(me + 31 + 2 * core, 32)

    barrier = pltpu.get_barrier_semaphore()

    def greet(device):
        pl.semaphore_signal(barrier, inc=1, device_id=device, device_id_type=MESH)

    for k in range(1, 8):
        greet(dev8(lax.rem(rank8 + k, 8)))
    for col in (west, z, east):
        greet((beyond, col))

    def greet16(k, carry):
        greet(dev16(lax.rem(chip + k, 16)))
        return carry

    lax.fori_loop(1, 16, greet16, 0)

    wcopy = pltpu.make_async_copy(wgt_hbm, wgt, wsem)
    wcopy.start()

    row_id = lax.broadcasted_iota(jnp.int32, (16, CI), 0)
    left_edge = jnp.zeros((16, CI), F32)
    right_edge = jnp.zeros((16, CI), F32)
    for b in range(B):
        for h in range(H):
            low = feat[b, h, 0:16, :].astype(F32)[0:1, :]
            top = feat[b, h, W - 16 : W, :].astype(F32)[15:16, :]
            here = row_id == b * H + h
            left_edge = jnp.where(here, low, left_edge)
            right_edge = jnp.where(here, top, right_edge)
    xedge_out[0] = right_edge.astype(BF16)
    xedge_out[1] = left_edge.astype(BF16)

    pl.semaphore_wait(barrier, 25)

    def remote(src, dst, ssem, rsem, device):
        return pltpu.make_async_remote_copy(
            src_ref=src,
            dst_ref=dst,
            send_sem=ssem,
            recv_sem=rsem,
            device_id=device,
            device_id_type=MESH,
        )

    def row_sends(first, last, land, ssem, rsem):
        return [
            remote(last, land.at[0], ssem.at[0], rsem.at[0], (down, z)),
            remote(first, land.at[1], ssem.at[1], rsem.at[1], (up, z)),
        ]

    def edge_sends(out, land, ssem, rsem):
        copies = []
        for side, col in ((0, east), (1, west)):
            for slot, row in ((0, down), (1, me), (2, up)):
                index = side * 3 + slot
                copies.append(
                    remote(
                        out.at[side], land.at[index], ssem.at[index], rsem.at[index], (row, col)
                    )
                )
        return copies

    xrow_copies = row_sends(feat.at[:, 0], feat.at[:, H - 1], xrow, xrow_s, xrow_r)
    for copy in xrow_copies:
        copy.start()
    xedge_copies = edge_sends(xedge_out, xedge_in, xedge_s, xedge_r)
    for copy in xedge_copies:
        copy.start()

    head_pad[...] = jnp.zeros((CO, 128), F32)
    head_pad[:, 0:4] = head_ref[...].astype(F32)
    spread = head_pad[...]
    head_t[...] = jnp.transpose(spread).astype(BF16)
    for step in (4, 8, 16, 32, 64):
        spread = spread + pltpu.roll(spread, step, 1)
    head_tile[...] = spread.astype(BF16)

    west_ok = jnp.where(z > 0, 1.0, 0.0).astype(F32)
    east_ok = jnp.where(z < 3, 1.0, 0.0).astype(F32)
    up_ok = jnp.where(me > 0, 1.0, 0.0).astype(F32)
    down_ok = jnp.where(me < 31, 1.0, 0.0).astype(F32)

    def pick_row(ref, slot, index):
        block = ref[slot].astype(F32)
        ids = lax.broadcasted_iota(jnp.int32, block.shape, 0)
        return jnp.sum(jnp.where(ids == index, block, 0.0), axis=0, keepdims=True)

    def shifted(value, before, after):
        ids = lax.broadcasted_iota(jnp.int32, value.shape, 0)
        left = jnp.where(ids == 0, before, pltpu.roll(value, 1, 0))
        right = jnp.where(ids == W - 1, after, pltpu.roll(value, W - 1, 0))
        return left.astype(BF16), right.astype(BF16)

    for copy in xedge_copies:
        copy.wait_recv()

    def build_x(i, carry):
        b = i // H
        h = lax.rem(i, H)
        value = feat[b, h].astype(F32)
        left, right = shifted(
            value,
            pick_row(xedge_in, 1, i) * west_ok,
            pick_row(xedge_in, 4, i) * east_ok,
        )
        xl[b, h + 1] = left
        xc[b, h + 1] = feat[b, h]
        xr[b, h + 1] = right
        return carry

    lax.fori_loop(0, B * H, build_x, 0)

    for copy in xrow_copies:
        copy.wait_recv()

    def build_halo(land, edge_in, left_ref, mid_ref, right_ref):
        def body(b, carry):
            for side, line, ok, src in ((0, 0, up_ok, H - 1), (1, H + 1, down_ok, 0)):
                value = land[side, b].astype(F32) * ok
                slot = 2 * side
                left, right = shifted(
                    value,
                    pick_row(edge_in, slot, b * H + src) * (west_ok * ok),
                    pick_row(edge_in, slot + 3, b * H + src) * (east_ok * ok),
                )
                left_ref[b, line] = left
                mid_ref[b, line] = value.astype(BF16)
                right_ref[b, line] = right
            return carry

        lax.fori_loop(0, B, body, 0)

    build_halo(xrow, xedge_in, xl, xc, xr)
    wcopy.wait()

    def forward(b, carry):
        lhs = jnp.concatenate(
            [
                ref[b, r : r + H].reshape(PIX, CI)
                for r in range(3)
                for ref in (xl, xc, xr)
            ],
            axis=1,
        )
        value = jnp.dot(lhs, wgt[...], preferred_element_type=F32)
        conv[b] = value
        mid = jnp.sum(value, axis=0, keepdims=True) * (1.0 / PIX)
        st_local[b, 0:1] = mid
        st_local[b, 1:2] = jnp.sum((value - mid) ** 2, axis=0, keepdims=True)
        return carry

    lax.fori_loop(0, B, forward, 0)

    def combine(parts, count):
        total = parts[0][0:1]
        for item in parts[1:]:
            total = total + item[0:1]
        mid = total * (1.0 / len(parts))
        spread_sum = None
        for item in parts:
            term = item[1:2] + count * (item[0:1] - mid) ** 2
            spread_sum = term if spread_sum is None else spread_sum + term
        return mid, spread_sum

    def exchange(buf, rank, size, dev, ssem, rsem):
        def copy_to(k):
            return remote(
                buf.at[rank],
                buf.at[rank],
                ssem.at[k],
                rsem.at[rank],
                dev(lax.rem(rank + k, size)),
            )

        def start():
            def body(k, carry):
                copy_to(k).start()
                return carry

            lax.fori_loop(1, size, body, 0)

        def wait():
            def body(k, carry):
                j = lax.rem(rank + k, size)
                remote(buf.at[j], buf.at[j], ssem.at[k], rsem.at[j], dev(j)).wait_recv()
                return carry

            lax.fori_loop(1, size, body, 0)

        def finish():
            def body(k, carry):
                copy_to(k).wait_send()
                return carry

            lax.fori_loop(1, size, body, 0)

        return start, wait, finish

    st8_x = exchange(st8, rank8, 8, dev8, s8_s, s8_r)
    st16_x = exchange(st16, chip, 16, dev16, s16_s, s16_r)
    tot8_x = exchange(tot8, rank8, 8, dev8, t8_s, t8_r)
    tot16_x = exchange(tot16, chip, 16, dev16, t16_s, t16_r)
    hd8_x = exchange(hd8, rank8, 8, dev8, h8_s, h8_r)
    hd16_x = exchange(hd16, chip, 16, dev16, h16_s, h16_r)

    mid, m2 = combine([st_local[b] for b in range(B)], float(PIX))
    st8[rank8, 0:1] = mid
    st8[rank8, 1:2] = m2
    st8_x[0]()

    def transpose_x(i, carry):
        b = i // (H + 2)
        h = lax.rem(i, H + 2)
        for c, ref in enumerate((xl, xc, xr)):
            xt[b, h, c * CI : (c + 1) * CI, :] = jnp.transpose(ref[b, h])
        return carry

    lax.fori_loop(0, B * (H + 2), transpose_x, 0)

    st8_x[1]()
    mid, m2 = combine([st8[j] for j in range(8)], float(B * PIX))
    st16[chip, 0:1] = mid
    st16[chip, 1:2] = m2
    st16_x[0]()

    def transpose_w(t, carry):
        wgt_t[pl.ds(pl.multiple_of(t * CO, CO), CO), :] = jnp.transpose(
            wgt[pl.ds(pl.multiple_of((TAPS - 1 - t) * CI, CI), CI), :]
        )
        return carry

    lax.fori_loop(0, TAPS, transpose_w, 0)

    lane_class = lax.rem(lax.broadcasted_iota(jnp.int32, (W, 128), 1), 4).astype(F32)
    for b in range(B):
        for h in range(H):
            label = labels_ref[b, h : h + 1, :].astype(F32)
            weight = raster_ref[b, h : h + 1, :].astype(F32)
            label_t = jnp.transpose(jnp.broadcast_to(label, (128, W)))
            weight_t = jnp.transpose(jnp.broadcast_to(weight, (128, W)))
            onehot[b, h * W : (h + 1) * W] = jnp.where(label_t == lane_class, 1.0, 0.0)
            pixw[b, h * W : (h + 1) * W] = (1.0 + weight_t) * 0.25

    st16_x[1]()
    mean, m2 = combine([st16[j] for j in range(16)], float(8 * B * PIX))
    rstd = lax.rsqrt(m2 * (1.0 / COUNT) + EPS)
    gain = gain_ref[...]
    bias = bias_ref[...]
    scale = gain * rstd

    def middle(b, carry):
        sum_g, sum_gn = carry
        away = conv[b] - mean
        pre = away * scale + bias
        acted = jnp.maximum(pre, 0.0).astype(BF16)
        act[b] = acted
        logits = jnp.dot(acted, head_tile[...], preferred_element_type=F32)
        expo = jnp.exp(logits)
        total = expo + pltpu.roll(expo, 1, 1)
        total = total + pltpu.roll(total, 2, 1)
        score = (pixw[b] * (expo / total - onehot[b])).astype(BF16)
        sgs[b] = score
        act_grad = jnp.dot(score, head_t[...], preferred_element_type=F32)
        pre_grad = jnp.where(pre > 0.0, act_grad, 0.0)
        pgs[b] = pre_grad
        sum_g = sum_g + jnp.sum(pre_grad, axis=0, keepdims=True)
        sum_gn = sum_gn + jnp.sum(pre_grad * away, axis=0, keepdims=True)
        return sum_g, sum_gn

    zero_row = jnp.zeros((1, CO), F32)
    sum_g, sum_gn = lax.fori_loop(0, B, middle, (zero_row, zero_row))

    def add_up(buf, size):
        total = buf[0]
        for j in range(1, size):
            total = total + buf[j]
        return total

    tot8[rank8, 0:1] = sum_g
    tot8[rank8, 1:2] = sum_gn * rstd
    tot8_x[0]()

    def head_part(b, total):
        return total + lax.dot_general(
            sgs[b], act[b], (((0,), (0,)), ((), ())), preferred_element_type=F32
        )

    head_sum = lax.fori_loop(0, B, head_part, jnp.zeros((128, CO), F32))

    tot8_x[1]()
    tot16[chip] = add_up(tot8, 8)
    tot16_x[0]()
    hd8[rank8] = head_sum[0:4, :]
    hd8_x[0]()
    tot16_x[1]()
    totals = add_up(tot16, 16)
    off = totals[0:1] * (1.0 / COUNT)
    slope = rstd * totals[1:2] * (1.0 / COUNT)
    st_local[0] = totals
    gb_out[...] = st_local[0, 0:1, pl.ds(pl.multiple_of(z * 128, 128), 128)]
    gg_out[...] = st_local[0, 1:2, pl.ds(pl.multiple_of(z * 128, 128), 128)]

    def conv_grad(i, carry):
        b = lax.rem(i, B)
        h = lax.rem(3 * (i // B), H)
        spot = pl.ds(pl.multiple_of(h * W, W), W)
        away = conv[b, spot] - mean
        value = scale * (pgs[b, spot] - off - away * slope)
        gc[b, h + 1] = value.astype(BF16)
        gedge_f[0, pl.ds(b * H + h, 1)] = value[W - 1 : W, :]
        gedge_f[1, pl.ds(b * H + h, 1)] = value[0:1, :]
        return carry

    lax.fori_loop(0, 2 * B, conv_grad, 0)
    grow_copies = row_sends(gc.at[:, 1], gc.at[:, H], grow, grow_s, grow_r)
    for copy in grow_copies:
        copy.start()
    lax.fori_loop(2 * B, 4 * B, conv_grad, 0)
    gedge_out[...] = gedge_f[...].astype(BF16)
    gedge_copies = edge_sends(gedge_out, gedge_in, gedge_s, gedge_r)
    for copy in gedge_copies:
        copy.start()

    mine = pl.ds(pl.multiple_of(core * 128, 128), 128)
    theirs = pl.ds(pl.multiple_of((1 - core) * 128, 128), 128)
    a_copies = [remote(send_a.at[r], recv_a.at[r], a_s.at[r], a_r.at[r], other) for r in range(3)]

    def kernel_grad(r):
        lhs = jnp.concatenate([xt[b, h + r] for b in range(B) for h in range(H)], axis=1)
        grad = gc[:, 1 : H + 1].reshape(B * PIX, CO)
        part[r] = jnp.dot(lhs, grad, preferred_element_type=F32).reshape(3, CI, CO)
        send_a[r] = part[r, :, theirs, :].astype(BF16)
        a_copies[r].start()

    def b_copy(r, k):
        j = lax.rem(z + k, 4)
        return remote(send_b.at[r, j], recv_b.at[r, z], b_s.at[r, k], b_r.at[r, z], (me, j))

    def b_arrival(r, k):
        j = lax.rem(z + k, 4)
        return remote(send_b.at[r, j], recv_b.at[r, j], b_s.at[r, k], b_r.at[r, j], (me, j))

    def stage_b(r):
        a_copies[r].wait_recv()
        value = part[r, :, mine, :] + recv_a[r].astype(F32)
        part[r, :, mine, :] = value
        for j in range(4):
            send_b[r, j] = value[:, :, j * 128 : (j + 1) * 128].reshape(384, 128).astype(BF16)
        for k in range(1, 4):
            b_copy(r, k).start()

    kernel_grad(0)
    hd8_x[1]()
    hd16[chip] = add_up(hd8, 8)
    hd16_x[0]()
    kernel_grad(1)
    stage_b(0)
    kernel_grad(2)
    stage_b(1)

    for copy in gedge_copies:
        copy.wait_recv()

    def build_g(i, carry):
        b = i // H
        h = lax.rem(i, H)
        left, right = shifted(
            gc[b, h + 1].astype(F32),
            pick_row(gedge_in, 1, i) * west_ok,
            pick_row(gedge_in, 4, i) * east_ok,
        )
        gl[b, h + 1] = left
        gr[b, h + 1] = right
        return carry

    lax.fori_loop(0, B * H, build_g, 0)
    stage_b(2)
    for copy in grow_copies:
        copy.wait_recv()
    for copy in grow_copies:
        copy.wait_send()
    build_halo(grow, gedge_in, gl, gc, gr)

    def back(b, carry):
        lhs = jnp.concatenate(
            [
                ref[b, r : r + H].reshape(PIX, CO)
                for r in range(3)
                for ref in (gl, gc, gr)
            ],
            axis=1,
        )
        value = jnp.dot(lhs, wgt_t[...], preferred_element_type=F32)
        gi_out[b] = value.reshape(H, W, CI)
        return carry

    lax.fori_loop(0, B, back, 0)

    own_cols = pl.ds(pl.multiple_of(z * 128, 128), 128)
    for r in range(3):
        total = part[r, :, mine, own_cols].reshape(384, 128)
        for k in range(1, 4):
            b_arrival(r, k).wait_recv()
            total = total + recv_b[r, lax.rem(z + k, 4)].astype(F32)
        sum_c[r * 384 : (r + 1) * 384] = total
        send_c[r * 384 : (r + 1) * 384] = total.astype(BF16)

    def c_copy(k):
        j = lax.rem(chip + k, 16)
        return remote(
            send_c.at[pl.ds(part_start(j), PART)],
            recv_c.at[chip],
            c_s.at[k],
            c_r.at[chip],
            dev16(j),
        )

    def c_arrival(k):
        j = lax.rem(chip + k, 16)
        return remote(
            send_c.at[pl.ds(part_start(j), PART)], recv_c.at[j], c_s.at[k], c_r.at[j], dev16(j)
        )

    def loop16(action):
        def body(k, carry):
            action(k)
            return carry

        lax.fori_loop(1, 16, body, 0)

    loop16(lambda k: c_copy(k).start())
    hd16_x[1]()
    head_all[...] = add_up(hd16, 16)
    gh_out[...] = head_all[:, own_cols]
    loop16(lambda k: c_arrival(k).wait_recv())

    def add_c(k, total):
        return total + recv_c[lax.rem(chip + k, 16)].astype(F32)

    total = lax.fori_loop(1, 16, add_c, sum_c[pl.ds(part_start(chip), PART)])
    gath[chip] = total.astype(BF16)
    gath_x = exchange(gath, chip, 16, dev16, g_s, g_r)
    gath_x[0]()
    gath_x[1]()
    o_copy = remote(gath, gath_other, o_s, o_r, other)
    o_copy.start()

    def unpack(src, half):
        for i in range(72):
            pair, rest = divmod(i, 9)
            owner, at = (2 * pair, rest) if rest < 5 else (2 * pair + 1, rest - 4)
            spot = pl.ds(pl.multiple_of(half * 128 + (i % 8) * 16, 16), 16)
            gw_out[i // 8, spot, :] = src[owner, at * 16 : (at + 1) * 16, :].astype(F32)

    unpack(gath, core)
    o_copy.wait_recv()
    unpack(gath_other, 1 - core)

    for copy in xrow_copies + xedge_copies + gedge_copies + a_copies + [o_copy]:
        copy.wait_send()
    for exchanged in (st8_x, st16_x, tot8_x, tot16_x, hd8_x, hd16_x, gath_x):
        exchanged[2]()
    for r in range(3):
        for k in range(1, 4):
            b_copy(r, k).wait_send()
    loop16(lambda k: c_copy(k).wait_send())


def per_device(features, conv_weight, bn_gain, bn_bias, head_weight, labels, raster):
    dma = pltpu.SemaphoreType.DMA
    vmem = pltpu.VMEM
    whole = pl.BlockSpec(memory_space=pltpu.VMEM)
    outs = pl.pallas_call(
        kernel,
        out_shape=(
            jax.ShapeDtypeStruct((TAPS, CI, 128), F32),
            jax.ShapeDtypeStruct((1, 128), F32),
            jax.ShapeDtypeStruct((1, 128), F32),
            jax.ShapeDtypeStruct((4, 128), F32),
            jax.ShapeDtypeStruct((B, H, W, CI), F32),
        ),
        in_specs=[whole, pl.BlockSpec(memory_space=pl.ANY)] + [whole] * 5,
        out_specs=(whole,) * 5,
        scratch_shapes=[
            vmem((TAPS * CI, CO), BF16),
            vmem((TAPS * CO, CI), BF16),
            vmem((B, H + 2, W, CI), BF16),
            vmem((B, H + 2, W, CI), BF16),
            vmem((B, H + 2, W, CI), BF16),
            vmem((B, H + 2, 3 * CI, W), BF16),
            vmem((B, PIX, CO), F32),
            vmem((B, PIX, CO), F32),
            vmem((B, PIX, CO), BF16),
            vmem((B, PIX, 128), BF16),
            vmem((B, PIX, 128), F32),
            vmem((B, PIX, 128), F32),
            vmem((CO, 128), F32),
            vmem((CO, 128), BF16),
            vmem((128, CO), BF16),
            vmem((B, H + 2, W, CO), BF16),
            vmem((B, H + 2, W, CO), BF16),
            vmem((B, H + 2, W, CO), BF16),
            vmem((2, B, W, CI), BF16),
            vmem((2, 16, CI), BF16),
            vmem((6, 16, CI), BF16),
            vmem((2, B, W, CO), BF16),
            vmem((2, 16, CO), F32),
            vmem((2, 16, CO), BF16),
            vmem((6, 16, CO), BF16),
            vmem((B, 2, CO), F32),
            vmem((8, 2, CO), F32),
            vmem((16, 2, CO), F32),
            vmem((8, 2, CO), F32),
            vmem((16, 2, CO), F32),
            vmem((8, 4, CO), F32),
            vmem((16, 4, CO), F32),
            vmem((4, CO), F32),
            vmem((3, 3, CI, CO), F32),
            vmem((3, 3, 128, CO), BF16),
            vmem((3, 3, 128, CO), BF16),
            vmem((3, 4, 384, 128), BF16),
            vmem((3, 4, 384, 128), BF16),
            vmem((OWN, 128), F32),
            vmem((OWN, 128), BF16),
            vmem((16, PART, 128), BF16),
            vmem((16, PART, 128), BF16),
            vmem((16, PART, 128), BF16),
            dma,
            dma((2,)),
            dma((2,)),
            dma((6,)),
            dma((6,)),
            dma((2,)),
            dma((2,)),
            dma((6,)),
            dma((6,)),
        ]
        + [dma((n,)) for n in (8, 8, 16, 16) * 3]
        + [
            dma((3,)),
            dma((3,)),
            dma((3, 4)),
            dma((3, 4)),
            dma((16,)),
            dma((16,)),
            dma((16,)),
            dma((16,)),
            dma,
            dma,
        ],
        compiler_params=pltpu.CompilerParams(
            collective_id=0, has_side_effects=True, vmem_limit_bytes=60 * 1024 * 1024
        ),
        cost_estimate=pl.CostEstimate(
            flops=15_000_000_000, bytes_accessed=8_000_000, transcendentals=300_000
        ),
    )(
        features,
        conv_weight.reshape(TAPS * CI, CO),
        bn_gain.reshape(1, CO),
        bn_bias.reshape(1, CO),
        head_weight,
        labels,
        raster,
    )
    grad_weight, grad_gain, grad_bias, grad_head, grad_input = outs
    return (
        grad_weight.reshape(3, 3, CI, 128),
        grad_gain.reshape(128),
        grad_bias.reshape(128),
        jnp.transpose(grad_head),
        grad_input,
    )


def solution(mesh):
    in_specs = (
        P(None, "rows", "cols", None),
        P(),
        P(),
        P(),
        P(),
        P(None, "rows", "cols"),
        P(None, "rows", "cols"),
    )
    out_specs = (
        P(None, None, None, "cols"),
        P("cols"),
        P("cols"),
        P("cols", None),
        P(None, "rows", "cols", None),
    )
    return jax.shard_map(
        per_device, mesh=mesh, in_specs=in_specs, out_specs=out_specs, check_vma=False
    )
```

time: 447 us -> 92 us (0.21)
  blocking collectives: 195 us -> 0 us
  waiting for transfers between devices: 137 us -> 0 us
  Pallas kernels: 0 us -> 84.2 us
  matrix products: 53.8 us -> 0 us
  starting transfers between devices: 22.6 us -> 0 us
  between operations: 14.5 us -> 0.68 us
  other arithmetic: 12.1 us -> 0 us
    psum x3 -> x0, blocking collectives: 195 us -> none  [reduce_all(): return lax.psum(values, ('rows', 'cols'))]
    psum x1 -> x0, waiting for transfers between devices: 137 us -> none  [per_device(): weight_total = lax.psum(weight_part, ('rows', 'cols'))]
    pallas_call x0 -> x1, Pallas kernels: none -> 84.2 us  [per_device(): pl.pallas_call(kernel, out_shape=(jax.ShapeDtypeStruct((TAPS, CI, 128), F...]
    dot_general x30 -> x0, matrix products: 53.8 us -> none  [the longest x9 26.1 us: shifted_conv(): jnp.einsum('bhwc,co->bhwo', window, kernel[offset_row, offset_col], prefe...]
    ppermute x8 -> x0, starting transfers between devices: 22.5 us -> none  [the longest x4 15.4 us: with_halo(): lax.ppermute(lax.slice_in_dim(block, block.shape[dim] - width, None, axis...]
    unnamed x29 -> x14, local copies, waits for them, and re-layouts: 1.26 us -> 6.94 us
    convert_element_type x2 -> x0, other arithmetic: 4.63 us -> none  [the longest x1 4.62 us: per_device(): conv_grad = (bn_gain * rstd * (pre_grad - bias_total / count - normed * g...]
  transfers between devices with their start and end apart: 9 -> 0, of which waited for: 2 -> 0; matrix products, arithmetic and copies ran while one was open for 7% -> 0% of each run, Pallas kernels for 0% -> 0%
where the time goes in v1:
time: 92 us; the launch traced here: 91.8 us
  Pallas kernels  84.2 us (92%)
  local copies, waits for them, and re-layouts  6.94 us (8%)
    pallas_call x1, Pallas kernels, per_device(): pl.pallas_call(kernel, out_shape=(jax.ShapeDtypeStruct((TAPS, CI, 128), F...  84.2 us
    unnamed x14, local copies, waits for them, and re-layouts  6.94 us

profile of v1, /device:TPU:1, one launch (start us, length us, event | category | flops | bytes accessed | tf_op | source)
XLA Modules:
  0.0 91.8 jit_solution(4529183982593650410)
XLA Ops:
  0.6 1.5 %copy.12.head_ref = bf16[512,4]{1,0:T(8,128)(2,1)} copy(bf16[512,4]{0,1:T(4,128)(2,1)} %param.11) | data formatting | bytes 8192 | tf_op args[4]
  2.1 84.2 %shard_map.110 = (f32[9,256,128]{2,1,0:T(8,128)}, f32[1,128]{1,0:T(1,128)}, f32[1,128]{1,0:T(1,128)}, f32[4,128]{1,0:T(4,128)}, f32[4,4,128,256]{3,2,1,0:T(8,128)}) custom-call(bf16[4,4,128,256]{3,2,1,0:T(8,128)(2,1)} %feat.1, bf16[2304,512]{1,0:T(8,128)(2,1)} %bitcast.9, f32[1,512]{1,0:T(1,128)} %bitcast.10, f32[1,512]{1,0:T(1,128)} %bitcast.11, ...), custom_call_target="tpu_custom_call" | custom-call | flops 15000000512 | bytes 8000000 | tf_op jit(solution)/shard_map/pallas_call | solution.py:608
  86.4 0.0 copy-start.3
  86.4 0.0 copy-start.2
  86.4 0.0 copy-start.1
  86.4 0.0 copy-start
  86.4 2.5 %copy.18 = f32[3,3,256,128]{3,2,1,0:T(8,128)} copy(f32[3,3,256,128]{3,2,1,0:T(8,128)} %bitcast.7) | data formatting | bytes 2359296
  88.9 0.0 copy-done.3
  88.9 0.5 copy.19
  89.4 0.0 copy-done.2
  89.4 0.5 copy.20
  89.9 0.0 copy-done.1
  89.9 0.6 copy.21
  90.5 0.0 copy-done
  90.5 1.3 %copy.22 = f32[4,4,128,256]{3,2,1,0:T(8,128)} copy(f32[4,4,128,256]{3,2,1,0:T(8,128)S(1)} %copy-done) | data formatting | bytes 4194304
Async XLA Ops:
  86.4 2.6 %copy-start.3 = (f32[1,128]{1,0:T(1,128)S(1)}, f32[1,128]{1,0:T(1,128)}, u32[]{:S(2)}) copy-start(f32[1,128]{1,0:T(1,128)} %get-tuple-element.11) | copy-start | bytes 1540
  86.4 3.1 %copy-start.2 = (f32[1,128]{1,0:T(1,128)S(1)}, f32[1,128]{1,0:T(1,128)}, u32[]{:S(2)}) copy-start(f32[1,128]{1,0:T(1,128)} %get-tuple-element.12) | copy-start | bytes 1540
  86.4 3.6 %copy-start.1 = (f32[4,128]{1,0:T(4,128)S(1)}, f32[4,128]{1,0:T(4,128)}, u32[]{:S(2)}) copy-start(f32[4,128]{1,0:T(4,128)} %get-tuple-element.13) | copy-start | bytes 6148
  86.4 4.1 %copy-start = (f32[4,4,128,256]{3,2,1,0:T(8,128)S(1)}, f32[4,4,128,256]{3,2,1,0:T(8,128)}, u32[]{:S(2)}) copy-start(f32[4,4,128,256]{3,2,1,0:T(8,128)} %get-tuple-element.24) | copy-start | bytes 6291460

commit v2 on v1

--- a/solution.py
+++ b/solution.py
@@ -18,12 +18,6 @@
 PIX = H * W
 COUNT = 4.0 * 128.0 * 512.0
 EPS = 1e-05
-OWN = 1152
-PART = 80
-
-
-def part_start(j):
-    return pl.multiple_of(((9 * j) // 2) * 16, 16)
 
 
 def kernel(
@@ -75,13 +69,28 @@
     part,
     send_a,
     recv_a,
-    send_b,
-    recv_b,
-    sum_c,
-    send_c,
-    recv_c,
-    gath,
-    gath_other,
+    acc,
+    ring1z_send,
+    ring1x_send,
+    ring1y_send,
+    ring1z_recv,
+    ring1x_recv,
+    ring1y_recv,
+    ring2z_send,
+    ring2x_send,
+    ring2y_send,
+    ring2z_recv,
+    ring2x_recv,
+    ring2y_recv,
+    two_own,
+    two_send,
+    two_recv,
+    three_send,
+    three_recv,
+    gat3,
+    gat2,
+    gat_other,
+    gi_buf,
     wsem,
     xrow_s,
     xrow_r,
@@ -105,14 +114,19 @@
     h16_r,
     a_s,
     a_r,
-    b_s,
-    b_r,
-    c_s,
-    c_r,
-    g_s,
-    g_r,
+    ring_s,
+    ring_r,
+    two_s,
+    two_r,
+    three_s,
+    three_r,
+    gat3_s,
+    gat3_r,
+    gat2_s,
+    gat2_r,
     o_s,
     o_r,
+    gi_sem,
 ):
     me = lax.axis_index("rows")
     z = lax.axis_index("cols")
@@ -149,8 +163,12 @@
 
     lax.fori_loop(1, 16, greet16, 0)
 
-    wcopy = pltpu.make_async_copy(wgt_hbm, wgt, wsem)
-    wcopy.start()
+    wcopies = []
+    for t in range(TAPS):
+        rows = pl.ds(t * CI, CI)
+        wcopies.append(pltpu.make_async_copy(wgt_hbm.at[rows], wgt.at[rows], wsem.at[t]))
+    for copy in wcopies:
+        copy.start()
 
     row_id = lax.broadcasted_iota(jnp.int32, (16, CI), 0)
     left_edge = jnp.zeros((16, CI), F32)
@@ -159,7 +177,7 @@
         for h in range(H):
             low = feat[b, h, 0:16, :].astype(F32)[0:1, :]
             top = feat[b, h, W - 16 : W, :].astype(F32)[15:16, :]
-            here = row_id == b * H + h
+            here = row_id == h * B + b
             left_edge = jnp.where(here, low, left_edge)
             right_edge = jnp.where(here, top, right_edge)
     xedge_out[0] = right_edge.astype(BF16)
@@ -202,13 +220,11 @@
     for copy in xedge_copies:
         copy.start()
 
-    head_pad[...] = jnp.zeros((CO, 128), F32)
-    head_pad[:, 0:4] = head_ref[...].astype(F32)
-    spread = head_pad[...]
-    head_t[...] = jnp.transpose(spread).astype(BF16)
-    for step in (4, 8, 16, 32, 64):
-        spread = spread + pltpu.roll(spread, step, 1)
-    head_tile[...] = spread.astype(BF16)
+    head_pad[...] = jnp.zeros((128, CO), F32)
+    head_pad[0:4] = head_ref[...].astype(F32)
+    head_t[...] = head_pad[...].astype(BF16)
+    head_pad[4:8] = head_ref[...].astype(F32)
+    head_tile[...] = jnp.transpose(jnp.concatenate([head_pad[0:8]] * 16, axis=0)).astype(BF16)
 
     west_ok = jnp.where(z > 0, 1.0, 0.0).astype(F32)
     east_ok = jnp.where(z < 3, 1.0, 0.0).astype(F32)
@@ -230,23 +246,20 @@
         copy.wait_recv()
 
     def build_x(i, carry):
-        b = i // H
-        h = lax.rem(i, H)
+        h = i // B
+        b = lax.rem(i, B)
         value = feat[b, h].astype(F32)
         left, right = shifted(
             value,
             pick_row(xedge_in, 1, i) * west_ok,
             pick_row(xedge_in, 4, i) * east_ok,
         )
-        xl[b, h + 1] = left
-        xc[b, h + 1] = feat[b, h]
-        xr[b, h + 1] = right
+        xl[h + 1, b] = left
+        xc[h + 1, b] = feat[b, h]
+        xr[h + 1, b] = right
         return carry
 
     lax.fori_loop(0, B * H, build_x, 0)
-
-    for copy in xrow_copies:
-        copy.wait_recv()
 
     def build_halo(land, edge_in, left_ref, mid_ref, right_ref):
         def body(b, carry):
@@ -255,36 +268,74 @@
                 slot = 2 * side
                 left, right = shifted(
                     value,
-                    pick_row(edge_in, slot, b * H + src) * (west_ok * ok),
-                    pick_row(edge_in, slot + 3, b * H + src) * (east_ok * ok),
+                    pick_row(edge_in, slot, src * B + b) * (west_ok * ok),
+                    pick_row(edge_in, slot + 3, src * B + b) * (east_ok * ok),
                 )
-                left_ref[b, line] = left
-                mid_ref[b, line] = value.astype(BF16)
-                right_ref[b, line] = right
+                left_ref[line, b] = left
+                mid_ref[line, b] = value.astype(BF16)
+                right_ref[line, b] = right
             return carry
 
         lax.fori_loop(0, B, body, 0)
 
-    build_halo(xrow, xedge_in, xl, xc, xr)
-    wcopy.wait()
-
-    def forward(b, carry):
+    for copy in wcopies:
+        copy.wait()
+
+    def conv_rows(h, first, count):
         lhs = jnp.concatenate(
             [
-                ref[b, r : r + H].reshape(PIX, CI)
-                for r in range(3)
+                ref[h + first + r].reshape(PIX, CI)
+                for r in range(count)
                 for ref in (xl, xc, xr)
             ],
             axis=1,
         )
-        value = jnp.dot(lhs, wgt[...], preferred_element_type=F32)
-        conv[b] = value
+        start = pl.multiple_of(first * 3 * CI, 3 * CI)
+        return jnp.dot(lhs, wgt[pl.ds(start, count * 3 * CI), :], preferred_element_type=F32)
+
+    def statistics(h, value):
         mid = jnp.sum(value, axis=0, keepdims=True) * (1.0 / PIX)
-        st_local[b, 0:1] = mid
-        st_local[b, 1:2] = jnp.sum((value - mid) ** 2, axis=0, keepdims=True)
+        st_local[h, 0:1] = mid
+        st_local[h, 1:2] = jnp.sum((value - mid) ** 2, axis=0, keepdims=True)
+
+    def transpose_x(line):
+        for c, ref in enumerate((xl, xc, xr)):
+            xt[line, c * CI : (c + 1) * CI, :] = jnp.transpose(ref[line].reshape(PIX, CI))
+
+    def transpose_w(t):
+        wgt_t[pl.ds(pl.multiple_of(t * CO, CO), CO), :] = jnp.transpose(
+            wgt[pl.ds(pl.multiple_of((TAPS - 1 - t) * CI, CI), CI), :]
+        )
+
+    def inner_rows(i, carry):
+        value = conv_rows(1 + i, 0, 3)
+        conv[1 + i] = value
+        transpose_x(1 + i)
+        transpose_x(3 + i)
+        statistics(1 + i, value)
         return carry
 
-    lax.fori_loop(0, B, forward, 0)
+    lax.fori_loop(0, 2, inner_rows, 0)
+
+    def outer_rows(i, carry):
+        conv[3 * i] = conv_rows(3 * i, 1 - i, 2)
+        for t in range(4):
+            transpose_w(4 * i + t)
+        return carry
+
+    lax.fori_loop(0, 2, outer_rows, 0)
+
+    for copy in xrow_copies:
+        copy.wait_recv()
+    build_halo(xrow, xedge_in, xl, xc, xr)
+
+    def halo_rows(i, carry):
+        value = conv[3 * i] + conv_rows(3 * i, 2 * i, 1)
+        conv[3 * i] = value
+        statistics(3 * i, value)
+        return carry
+
+    lax.fori_loop(0, 2, halo_rows, 0)
 
     def combine(parts, count):
         total = parts[0][0:1]
@@ -338,33 +389,20 @@
     hd8_x = exchange(hd8, rank8, 8, dev8, h8_s, h8_r)
     hd16_x = exchange(hd16, chip, 16, dev16, h16_s, h16_r)
 
-    mid, m2 = combine([st_local[b] for b in range(B)], float(PIX))
+    mid, m2 = combine([st_local[h] for h in range(H)], float(PIX))
     st8[rank8, 0:1] = mid
     st8[rank8, 1:2] = m2
     st8_x[0]()
 
-    def transpose_x(i, carry):
-        b = i // (H + 2)
-        h = lax.rem(i, H + 2)
-        for c, ref in enumerate((xl, xc, xr)):
-            xt[b, h, c * CI : (c + 1) * CI, :] = jnp.transpose(ref[b, h])
-        return carry
-
-    lax.fori_loop(0, B * (H + 2), transpose_x, 0)
+    transpose_x(0)
+    transpose_x(H + 1)
+    transpose_w(TAPS - 1)
 
     st8_x[1]()
     mid, m2 = combine([st8[j] for j in range(8)], float(B * PIX))
     st16[chip, 0:1] = mid
     st16[chip, 1:2] = m2
     st16_x[0]()
-
-    def transpose_w(t, carry):
-        wgt_t[pl.ds(pl.multiple_of(t * CO, CO), CO), :] = jnp.transpose(
-            wgt[pl.ds(pl.multiple_of((TAPS - 1 - t) * CI, CI), CI), :]
-        )
-        return carry
-
-    lax.fori_loop(0, TAPS, transpose_w, 0)
 
     lane_class = lax.rem(lax.broadcasted_iota(jnp.int32, (W, 128), 1), 4).astype(F32)
     for b in range(B):
@@ -373,8 +411,8 @@
             weight = raster_ref[b, h : h + 1, :].astype(F32)
             label_t = jnp.transpose(jnp.broadcast_to(label, (128, W)))
             weight_t = jnp.transpose(jnp.broadcast_to(weight, (128, W)))
-            onehot[b, h * W : (h + 1) * W] = jnp.where(label_t == lane_class, 1.0, 0.0)
-            pixw[b, h * W : (h + 1) * W] = (1.0 + weight_t) * 0.25
+            onehot[h, b * W : (b + 1) * W] = jnp.where(label_t == lane_class, 1.0, 0.0)
+            pixw[h, b * W : (b + 1) * W] = (1.0 + weight_t) * 0.25
 
     st16_x[1]()
     mean, m2 = combine([st16[j] for j in range(16)], float(8 * B * PIX))
@@ -438,16 +476,16 @@
     def conv_grad(i, carry):
         b = lax.rem(i, B)
         h = lax.rem(3 * (i // B), H)
-        spot = pl.ds(pl.multiple_of(h * W, W), W)
-        away = conv[b, spot] - mean
-        value = scale * (pgs[b, spot] - off - away * slope)
-        gc[b, h + 1] = value.astype(BF16)
-        gedge_f[0, pl.ds(b * H + h, 1)] = value[W - 1 : W, :]
-        gedge_f[1, pl.ds(b * H + h, 1)] = value[0:1, :]
+        spot = pl.ds(pl.multiple_of(b * W, W), W)
+        away = conv[h, spot] - mean
+        value = scale * (pgs[h, spot] - off - away * slope)
+        gc[h + 1, b] = value.astype(BF16)
+        gedge_f[0, pl.ds(h * B + b, 1)] = value[W - 1 : W, :]
+        gedge_f[1, pl.ds(h * B + b, 1)] = value[0:1, :]
         return carry
 
     lax.fori_loop(0, 2 * B, conv_grad, 0)
-    grow_copies = row_sends(gc.at[:, 1], gc.at[:, H], grow, grow_s, grow_r)
+    grow_copies = row_sends(gc.at[1], gc.at[H], grow, grow_s, grow_r)
     for copy in grow_copies:
         copy.start()
     lax.fori_loop(2 * B, 4 * B, conv_grad, 0)
@@ -456,149 +494,354 @@
     for copy in gedge_copies:
         copy.start()
 
+    x = chip // 4
+    y = lax.rem(chip, 4)
+    coords = {"x": x, "y": y, "z": z}
+
+    def on_axis(axis, j):
+        j = lax.rem(j, 4)
+        if axis == "z":
+            return (me, j)
+        if axis == "y":
+            return ((x * 4 + j) * 2 + core, z)
+        return ((j * 4 + y) * 2 + core, z)
+
+    ORDERS = (("z", "y", "x"), ("x", "z", "y"), ("y", "z", "x"))
     mine = pl.ds(pl.multiple_of(core * 128, 128), 128)
     theirs = pl.ds(pl.multiple_of((1 - core) * 128, 128), 128)
     a_copies = [remote(send_a.at[r], recv_a.at[r], a_s.at[r], a_r.at[r], other) for r in range(3)]
 
+    def build_g(i):
+        h, b = divmod(i, B)
+        value = gc[h + 1, b].astype(F32)
+        gl[h + 1, b], gr[h + 1, b] = shifted(value, 0.0, 0.0)
+
     def kernel_grad(r):
-        lhs = jnp.concatenate([xt[b, h + r] for b in range(B) for h in range(H)], axis=1)
-        grad = gc[:, 1 : H + 1].reshape(B * PIX, CO)
+        for i in ((0, 1, 2, 3, 4), (5, 6, 7, 8, 9), (10, 11, 12, 13, 14, 15))[r]:
+            build_g(i)
+        lhs = jnp.concatenate([xt[h + r] for h in range(H)], axis=1)
+        grad = gc[1 : H + 1].reshape(B * PIX, CO)
         part[r] = jnp.dot(lhs, grad, preferred_element_type=F32).reshape(3, CI, CO)
         send_a[r] = part[r, :, theirs, :].astype(BF16)
         a_copies[r].start()
 
-    def b_copy(r, k):
-        j = lax.rem(z + k, 4)
-        return remote(send_b.at[r, j], recv_b.at[r, z], b_s.at[r, k], b_r.at[r, z], (me, j))
-
-    def b_arrival(r, k):
-        j = lax.rem(z + k, 4)
-        return remote(send_b.at[r, j], recv_b.at[r, j], b_s.at[r, k], b_r.at[r, j], (me, j))
-
-    def stage_b(r):
+    ring1_send, ring1_recv = (ring1z_send, ring1x_send, ring1y_send), (
+        ring1z_recv,
+        ring1x_recv,
+        ring1y_recv,
+    )
+    ring2_send, ring2_recv = (ring2z_send, ring2x_send, ring2y_send), (
+        ring2z_recv,
+        ring2x_recv,
+        ring2y_recv,
+    )
+
+    def halves(r):
+        return 192 if r == 0 else 48
+
+    def block(r, q, low, high):
+        q = lax.rem(q, 4)
+        if r == 0:
+            return acc[r, low:high, pl.ds(pl.multiple_of(q * 128, 128), 128)]
+        return acc[r, pl.ds(pl.multiple_of(q * 96 + low, 16), high - low), :]
+
+    def ring1_copies(r):
+        axis = ORDERS[r][0]
+        here = coords[axis]
+        return [
+            remote(
+                ring1_send[r].at[way],
+                ring1_recv[r].at[way],
+                ring_s.at[r, way],
+                ring_r.at[r, way],
+                on_axis(axis, here + (1, 3)[way]),
+            )
+            for way in range(2)
+        ]
+
+    def ring2_copies(r):
+        axis = ORDERS[r][0]
+        here = coords[axis]
+        return [
+            remote(
+                ring2_send[r].at[way],
+                ring2_recv[r].at[way],
+                ring_s.at[r, 2 + way],
+                ring_r.at[r, 2 + way],
+                on_axis(axis, here + (1, 3)[way]),
+            )
+            for way in range(2)
+        ]
+
+    def ring1(r):
         a_copies[r].wait_recv()
-        value = part[r, :, mine, :] + recv_a[r].astype(F32)
-        part[r, :, mine, :] = value
-        for j in range(4):
-            send_b[r, j] = value[:, :, j * 128 : (j + 1) * 128].reshape(384, 128).astype(BF16)
+        acc[r] = part[r, :, mine, :].reshape(384, CO) + recv_a[r].reshape(384, CO).astype(F32)
+        here, half = coords[ORDERS[r][0]], halves(r)
+        ring1_send[r][0] = block(r, here + 2, 0, half).astype(BF16)
+        ring1_send[r][1] = block(r, here + 2, half, 2 * half).astype(BF16)
+        for copy in ring1_copies(r):
+            copy.start()
+
+    def ring2(r):
+        for copy in ring1_copies(r):
+            copy.wait_recv()
+        here, half = coords[ORDERS[r][0]], halves(r)
+        low = ring1_recv[r][0].astype(F32)
+        high = ring1_recv[r][1].astype(F32)
+        ring2_send[r][0, 0:half] = (block(r, here + 1, 0, half) + low).astype(BF16)
+        ring2_send[r][0, half : 2 * half] = block(r, here + 1, half, 2 * half).astype(BF16)
+        ring2_send[r][1, 0:half] = block(r, here + 3, 0, half).astype(BF16)
+        ring2_send[r][1, half : 2 * half] = (
+            block(r, here + 3, half, 2 * half) + high
+        ).astype(BF16)
+        for copy in ring2_copies(r):
+            copy.start()
+
+    def along(r, axis, send, recv, ssem, rsem, piece):
+        here = coords[axis]
+
+        def towards(k):
+            j = lax.rem(here + k, 4)
+            return remote(piece(send, j), recv.at[r, here], ssem.at[r, k], rsem.at[r, here], on_axis(axis, j))
+
+        def arriving(k):
+            j = lax.rem(here + k, 4)
+            return remote(piece(send, j), recv.at[r, j], ssem.at[r, k], rsem.at[r, j], on_axis(axis, j))
+
+        def start():
+            for k in range(1, 4):
+                towards(k).start()
+
+        def wait():
+            for k in range(1, 4):
+                arriving(k).wait_recv()
+
+        def finish():
+            for k in range(1, 4):
+                towards(k).wait_send()
+
+        return start, wait, finish
+
+    second = [
+        along(r, ORDERS[r][1], two_send, two_recv, two_s, two_r, lambda ref, j, r=r: ref.at[r, j])
+        for r in range(3)
+    ]
+    third = [
+        along(
+            r,
+            ORDERS[r][2],
+            three_send,
+            three_recv,
+            three_s,
+            three_r,
+            lambda ref, j, r=r: ref.at[r, j],
+        )
+        for r in range(3)
+    ]
+    row_axis = ("y", "x", "y")
+    gather3 = [
+        along(
+            r,
+            ORDERS[r][2],
+            gat3,
+            gat3,
+            gat3_s,
+            gat3_r,
+            lambda ref, j, r=r: ref.at[r, coords[ORDERS[r][2]]],
+        )
+        for r in range(3)
+    ]
+    gather2 = [
+        along(
+            r,
+            row_axis[r],
+            gat2,
+            gat2,
+            gat2_s,
+            gat2_r,
+            lambda ref, j, r=r: ref.at[r, coords[row_axis[r]]],
+        )
+        for r in range(3)
+    ]
+
+    def stage2(r):
+        for copy in ring2_copies(r):
+            copy.wait_recv()
+        here, half = coords[ORDERS[r][0]], halves(r)
+        total = (
+            block(r, here, 0, 2 * half)
+            + ring2_recv[r][0].astype(F32)
+            + ring2_recv[r][1].astype(F32)
+        )
+        for q in range(4):
+            piece = (
+                total[q * 96 : (q + 1) * 96] if r == 0 else total[:, q * 128 : (q + 1) * 128]
+            )
+            two_own[r, q] = piece
+            two_send[r, q] = piece.astype(BF16)
+        second[r][0]()
+
+    def stage3(r):
+        second[r][1]()
+        here = coords[ORDERS[r][1]]
+        total = two_own[r, here]
         for k in range(1, 4):
-            b_copy(r, k).start()
-
-    kernel_grad(0)
-    hd8_x[1]()
-    hd16[chip] = add_up(hd8, 8)
-    hd16_x[0]()
-    kernel_grad(1)
-    stage_b(0)
-    kernel_grad(2)
-    stage_b(1)
-
-    for copy in gedge_copies:
-        copy.wait_recv()
-
-    def build_g(i, carry):
-        b = i // H
-        h = lax.rem(i, H)
-        left, right = shifted(
-            gc[b, h + 1].astype(F32),
-            pick_row(gedge_in, 1, i) * west_ok,
-            pick_row(gedge_in, 4, i) * east_ok,
-        )
-        gl[b, h + 1] = left
-        gr[b, h + 1] = right
-        return carry
-
-    lax.fori_loop(0, B * H, build_g, 0)
-    stage_b(2)
-    for copy in grow_copies:
-        copy.wait_recv()
-    for copy in grow_copies:
-        copy.wait_send()
-    build_halo(grow, gedge_in, gl, gc, gr)
-
-    def back(b, carry):
+            total = total + two_recv[r, lax.rem(here + k, 4)].astype(F32)
+        for q in range(4):
+            three_send[r, q] = total[q * 24 : (q + 1) * 24]
+        third[r][0]()
+
+    def collect3(r):
+        third[r][1]()
+        here = coords[ORDERS[r][2]]
+        total = three_send[r, here]
+        for k in range(1, 4):
+            total = total + three_recv[r, lax.rem(here + k, 4)]
+        gat3[r, here] = total
+        gather3[r][0]()
+
+    def collect2(r):
+        gather3[r][1]()
+        here = coords[row_axis[r]]
+        gat2[r, here] = jnp.concatenate([gat3[r, q] for q in range(4)], axis=0).astype(BF16)
+        gather2[r][0]()
+
+    o_copies = [remote(gat2.at[r], gat_other.at[r], o_s.at[r], o_r.at[r], other) for r in range(3)]
+
+    def swap(r):
+        gather2[r][1]()
+        o_copies[r].start()
+        unpack(r, gat2, core)
+
+    def unpack(r, src, half):
+        rows = src[r].reshape(384, 128)
+        spot = pl.ds(pl.multiple_of(half * 128, 128), 128)
+        for c in range(3):
+            gw_out[3 * r + c, spot, :] = rows[c * 128 : (c + 1) * 128].astype(F32)
+
+    def unpack_other(r):
+        o_copies[r].wait_recv()
+        unpack(r, gat_other, 1 - core)
+
+    gi_copies = [
+        pltpu.make_async_copy(gi_buf.at[h], gi_out.at[:, h], gi_sem.at[h]) for h in range(H)
+    ]
+
+    def back(h):
         lhs = jnp.concatenate(
             [
-                ref[b, r : r + H].reshape(PIX, CO)
+                ref[h + r].reshape(PIX, CO)
                 for r in range(3)
                 for ref in (gl, gc, gr)
             ],
             axis=1,
         )
         value = jnp.dot(lhs, wgt_t[...], preferred_element_type=F32)
-        gi_out[b] = value.reshape(H, W, CI)
+        gi_buf[h] = value.reshape(B, W, CI)
+        gi_copies[h].start()
+
+    def set_edges(i, carry):
+        h = i // B
+        b = lax.rem(i, B)
+        ids = lax.broadcasted_iota(jnp.int32, (16, CO), 0)
+        low = pick_row(gedge_in, 1, i) * west_ok
+        top = pick_row(gedge_in, 4, i) * east_ok
+        block16 = gl[h + 1, b, 0:16].astype(F32)
+        gl[h + 1, b, 0:16] = jnp.where(ids == 0, low, block16).astype(BF16)
+        block16 = gr[h + 1, b, W - 16 : W].astype(F32)
+        gr[h + 1, b, W - 16 : W] = jnp.where(ids == 15, top, block16).astype(BF16)
         return carry
 
-    lax.fori_loop(0, B, back, 0)
-
-    own_cols = pl.ds(pl.multiple_of(z * 128, 128), 128)
-    for r in range(3):
-        total = part[r, :, mine, own_cols].reshape(384, 128)
-        for k in range(1, 4):
-            b_arrival(r, k).wait_recv()
-            total = total + recv_b[r, lax.rem(z + k, 4)].astype(F32)
-        sum_c[r * 384 : (r + 1) * 384] = total
-        send_c[r * 384 : (r + 1) * 384] = total.astype(BF16)
-
-    def c_copy(k):
-        j = lax.rem(chip + k, 16)
-        return remote(
-            send_c.at[pl.ds(part_start(j), PART)],
-            recv_c.at[chip],
-            c_s.at[k],
-            c_r.at[chip],
-            dev16(j),
-        )
-
-    def c_arrival(k):
-        j = lax.rem(chip + k, 16)
-        return remote(
-            send_c.at[pl.ds(part_start(j), PART)], recv_c.at[j], c_s.at[k], c_r.at[j], dev16(j)
-        )
-
-    def loop16(action):
-        def body(k, carry):
-            action(k)
-            return carry
-
-        lax.fori_loop(1, 16, body, 0)
-
-    loop16(lambda k: c_copy(k).start())
+    kernel_grad(0)
+    hd8_x[1]()
+    hd16[chip] = add_up(hd8, 8)
+    hd16_x[0]()
+    kernel_grad(1)
+    ring1(0)
+    kernel_grad(2)
+    ring1(1)
+    ring2(0)
+    for copy in gedge_copies:
+        copy.wait_recv()
+    lax.fori_loop(0, B * H, set_edges, 0)
+    ring1(2)
+    ring2(1)
+    stage2(0)
+    back(1)
+    ring2(2)
+    stage2(1)
+    stage3(0)
+    back(2)
+    stage2(2)
+    stage3(1)
+    collect3(0)
+    for copy in grow_copies:
+        copy.wait_recv()
+    build_halo(grow, gedge_in, gl, gc, gr)
+    back(0)
+    stage3(2)
+    collect3(1)
+    collect2(0)
+    back(3)
+    collect3(2)
+    collect2(1)
+    swap(0)
     hd16_x[1]()
     head_all[...] = add_up(hd16, 16)
-    gh_out[...] = head_all[:, own_cols]
-    loop16(lambda k: c_arrival(k).wait_recv())
-
-    def add_c(k, total):
-        return total + recv_c[lax.rem(chip + k, 16)].astype(F32)
-
-    total = lax.fori_loop(1, 16, add_c, sum_c[pl.ds(part_start(chip), PART)])
-    gath[chip] = total.astype(BF16)
-    gath_x = exchange(gath, chip, 16, dev16, g_s, g_r)
-    gath_x[0]()
-    gath_x[1]()
-    o_copy = remote(gath, gath_other, o_s, o_r, other)
-    o_copy.start()
-
-    def unpack(src, half):
-        for i in range(72):
-            pair, rest = divmod(i, 9)
-            owner, at = (2 * pair, rest) if rest < 5 else (2 * pair + 1, rest - 4)
-            spot = pl.ds(pl.multiple_of(half * 128 + (i % 8) * 16, 16), 16)
-            gw_out[i // 8, spot, :] = src[owner, at * 16 : (at + 1) * 16, :].astype(F32)
-
-    unpack(gath, core)
-    o_copy.wait_recv()
-    unpack(gath_other, 1 - core)
-
-    for copy in xrow_copies + xedge_copies + gedge_copies + a_copies + [o_copy]:
+    gh_out[...] = head_all[:, pl.ds(pl.multiple_of(z * 128, 128), 128)]
+    collect2(2)
+    swap(1)
+    unpack_other(0)
+    swap(2)
+    unpack_other(1)
+
+    for copy in xrow_copies + xedge_copies + grow_copies + gedge_copies + a_copies:
         copy.wait_send()
-    for exchanged in (st8_x, st16_x, tot8_x, tot16_x, hd8_x, hd16_x, gath_x):
+    for exchanged in (st8_x, st16_x, tot8_x, tot16_x, hd8_x, hd16_x):
         exchanged[2]()
     for r in range(3):
-        for k in range(1, 4):
-            b_copy(r, k).wait_send()
-    loop16(lambda k: c_copy(k).wait_send())
+        for copy in ring1_copies(r) + ring2_copies(r):
+            copy.wait_send()
+        for exchanged in (second[r], third[r], gather3[r], gather2[r]):
+            exchanged[2]()
+    for copy in gi_copies:
+        copy.wait()
+    unpack_other(2)
+    for copy in o_copies:
+        copy.wait_send()
+
+
+def move_kernel(*refs):
+    count = (len(refs) - 2) // 3
+    in_sem, out_sem = refs[-2:]
+    arrivals, leaves = [], []
+    for src, dst, held in zip(refs[:count], refs[count : 2 * count], refs[2 * count : 3 * count]):
+        size = src.shape[0] if len(src.shape) > 2 else 1
+        for i in range(size):
+            here, there, hold = (src.at[i], dst.at[i], held.at[i]) if size > 1 else (src, dst, held)
+            slot = len(arrivals)
+            arrivals.append(pltpu.make_async_copy(here, hold, in_sem.at[slot]))
+            leaves.append(pltpu.make_async_copy(hold, there, out_sem.at[slot]))
+    for copy in arrivals:
+        copy.start()
+    for arrival, leave in zip(arrivals, leaves):
+        arrival.wait()
+        leave.start()
+    for leave in leaves:
+        leave.wait()
+
+
+def move_out(arrays):
+    anywhere = pl.BlockSpec(memory_space=pl.ANY)
+    return pl.pallas_call(
+        move_kernel,
+        out_shape=tuple(jax.ShapeDtypeStruct(a.shape, a.dtype) for a in arrays),
+        in_specs=[anywhere] * len(arrays),
+        out_specs=(anywhere,) * len(arrays),
+        scratch_shapes=[pltpu.VMEM(a.shape, a.dtype) for a in arrays]
+        + [pltpu.SemaphoreType.DMA((16,)), pltpu.SemaphoreType.DMA((16,))],
+        compiler_params=pltpu.CompilerParams(vmem_limit_bytes=60 * 1024 * 1024),
+    )(*arrays)
 
 
 def per_device(features, conv_weight, bn_gain, bn_bias, head_weight, labels, raster):
@@ -615,26 +858,26 @@
             jax.ShapeDtypeStruct((B, H, W, CI), F32),
         ),
         in_specs=[whole, pl.BlockSpec(memory_space=pl.ANY)] + [whole] * 5,
-        out_specs=(whole,) * 5,
+        out_specs=(whole,) * 4 + (pl.BlockSpec(memory_space=pl.ANY),),
         scratch_shapes=[
             vmem((TAPS * CI, CO), BF16),
             vmem((TAPS * CO, CI), BF16),
-            vmem((B, H + 2, W, CI), BF16),
-            vmem((B, H + 2, W, CI), BF16),
-            vmem((B, H + 2, W, CI), BF16),
-            vmem((B, H + 2, 3 * CI, W), BF16),
-            vmem((B, PIX, CO), F32),
-            vmem((B, PIX, CO), F32),
-            vmem((B, PIX, CO), BF16),
-            vmem((B, PIX, 128), BF16),
-            vmem((B, PIX, 128), F32),
-            vmem((B, PIX, 128), F32),
-            vmem((CO, 128), F32),
+            vmem((H + 2, B, W, CI), BF16),
+            vmem((H + 2, B, W, CI), BF16),
+            vmem((H + 2, B, W, CI), BF16),
+            vmem((H + 2, 3 * CI, PIX), BF16),
+            vmem((H, PIX, CO), F32),
+            vmem((H, PIX, CO), F32),
+            vmem((H, PIX, CO), BF16),
+            vmem((H, PIX, 128), BF16),
+            vmem((H, PIX, 128), F32),
+            vmem((H, PIX, 128), F32),
+            vmem((128, CO), F32),
             vmem((CO, 128), BF16),
             vmem((128, CO), BF16),
-            vmem((B, H + 2, W, CO), BF16),
-            vmem((B, H + 2, W, CO), BF16),
-            vmem((B, H + 2, W, CO), BF16),
+            vmem((H + 2, B, W, CO), BF16),
+            vmem((H + 2, B, W, CO), BF16),
+            vmem((H + 2, B, W, CO), BF16),
             vmem((2, B, W, CI), BF16),
             vmem((2, 16, CI), BF16),
             vmem((6, 16, CI), BF16),
@@ -653,14 +896,29 @@
             vmem((3, 3, CI, CO), F32),
             vmem((3, 3, 128, CO), BF16),
             vmem((3, 3, 128, CO), BF16),
-            vmem((3, 4, 384, 128), BF16),
-            vmem((3, 4, 384, 128), BF16),
-            vmem((OWN, 128), F32),
-            vmem((OWN, 128), BF16),
-            vmem((16, PART, 128), BF16),
-            vmem((16, PART, 128), BF16),
-            vmem((16, PART, 128), BF16),
-            dma,
+            vmem((3, 384, CO), F32),
+            vmem((2, 192, 128), BF16),
+            vmem((2, 48, CO), BF16),
+            vmem((2, 48, CO), BF16),
+            vmem((2, 192, 128), BF16),
+            vmem((2, 48, CO), BF16),
+            vmem((2, 48, CO), BF16),
+            vmem((2, 384, 128), BF16),
+            vmem((2, 96, CO), BF16),
+            vmem((2, 96, CO), BF16),
+            vmem((2, 384, 128), BF16),
+            vmem((2, 96, CO), BF16),
+            vmem((2, 96, CO), BF16),
+            vmem((3, 4, 96, 128), F32),
+            vmem((3, 4, 96, 128), BF16),
+            vmem((3, 4, 96, 128), BF16),
+            vmem((3, 4, 24, 128), F32),
+            vmem((3, 4, 24, 128), F32),
+            vmem((3, 4, 24, 128), F32),
+            vmem((3, 4, 96, 128), BF16),
+            vmem((3, 4, 96, 128), BF16),
+            vmem((H, B, W, CI), F32),
+            dma((TAPS,)),
             dma((2,)),
             dma((2,)),
             dma((6,)),
@@ -676,12 +934,17 @@
             dma((3,)),
             dma((3, 4)),
             dma((3, 4)),
-            dma((16,)),
-            dma((16,)),
-            dma((16,)),
-            dma((16,)),
-            dma,
-            dma,
+            dma((3, 4)),
+            dma((3, 4)),
+            dma((3, 4)),
+            dma((3, 4)),
+            dma((3, 4)),
+            dma((3, 4)),
+            dma((3, 4)),
+            dma((3, 4)),
+            dma((3,)),
+            dma((3,)),
+            dma((H,)),
         ],
         compiler_params=pltpu.CompilerParams(
             collective_id=0, has_side_effects=True, vmem_limit_bytes=60 * 1024 * 1024
@@ -694,11 +957,11 @@
         conv_weight.reshape(TAPS * CI, CO),
         bn_gain.reshape(1, CO),
         bn_bias.reshape(1, CO),
-        head_weight,
+        jnp.transpose(head_weight),
         labels,
         raster,
     )
-    grad_weight, grad_gain, grad_bias, grad_head, grad_input = outs
+    grad_weight, grad_gain, grad_bias, grad_head, grad_input = move_out(outs)
     return (
         grad_weight.reshape(3, 3, CI, 128),
         grad_gain.reshape(128),

time: 92 us -> 90.8 us (0.987)
  local copies, waits for them, and re-layouts: 6.94 us -> 0 us
  Pallas kernels: 84.2 us -> 89.8 us
    unnamed x14 -> x0, local copies, waits for them, and re-layouts: 6.94 us -> none
    pallas_call x0 -> x1, Pallas kernels: none -> 3.49 us  [move_out(): pl.pallas_call(move_kernel, out_shape=tuple((jax.ShapeDtypeStruct(a.shape...]
    pallas_call x1, Pallas kernels: 84.2 us -> 86.3 us  [per_device(): pl.pallas_call(kernel, out_shape=(jax.ShapeDtypeStruct((TAPS, CI, 128), F...]
where the time goes in v2:
time: 90.8 us; the launch traced here: 90.6 us
  Pallas kernels  89.8 us (99%)
    pallas_call x1, Pallas kernels, per_device(): pl.pallas_call(kernel, out_shape=(jax.ShapeDtypeStruct((TAPS, CI, 128), F...  86.3 us
    pallas_call x1, Pallas kernels, move_out(): pl.pallas_call(move_kernel, out_shape=tuple((jax.ShapeDtypeStruct(a.shape...  3.49 us

profile of v2, /device:TPU:1, one launch (start us, length us, event | category | flops | bytes accessed | tf_op | source)
XLA Modules:
  0.0 90.6 jit_solution(13536523371121223680)
XLA Ops:
  0.6 86.3 %shard_map.110 = (f32[9,256,128]{2,1,0:T(8,128)}, f32[1,128]{1,0:T(1,128)}, f32[1,128]{1,0:T(1,128)}, f32[4,128]{1,0:T(4,128)}, f32[4,4,128,256]{3,2,1,0:T(8,128)}) custom-call(bf16[4,4,128,256]{3,2,1,0:T(8,128)(2,1)} %feat.1, bf16[2304,512]{1,0:T(8,128)(2,1)} %bitcast.8, f32[1,512]{1,0:T(1,128)} %bitcast.11, f32[1,512]{1,0:T(1,128)} %bitcast.12, ...), custom_call_target="tpu_custom_call" | custom-call | flops 15000000512 | bytes 8000000 | tf_op jit(solution)/shard_map/pallas_call | solution.py:851
  87.0 3.5 %shard_map.111 = (f32[9,256,128]{2,1,0:T(8,128)}, f32[1,128]{1,0:T(1,128)}, f32[1,128]{1,0:T(1,128)}, f32[4,128]{1,0:T(4,128)}, f32[4,4,128,256]{3,2,1,0:T(8,128)}) custom-call(f32[9,256,128]{2,1,0:T(8,128)} %get-tuple-element.15.refs_0_, f32[1,128]{1,0:T(1,128)} %get-tuple-element.16.refs_1_, f32[1,128]{1,0:T(1,128)} %get-tuple-element.17.refs_2_, ...), custom_call_target="tpu_custom_call" | custom-call | tf_op jit(solution)/shard_map/pallas_call | solution.py:836

commit v3 on v2

--- a/solution.py
+++ b/solution.py
@@ -63,9 +63,11 @@
     st16,
     tot8,
     tot16,
-    hd8,
-    hd16,
-    head_all,
+    hd2,
+    hdz_send,
+    hdz,
+    hdy,
+    hdx,
     part,
     send_a,
     recv_a,
@@ -100,30 +102,16 @@
     grow_r,
     gedge_s,
     gedge_r,
-    s8_s,
-    s8_r,
-    s16_s,
-    s16_r,
-    t8_s,
-    t8_r,
-    t16_s,
-    t16_r,
-    h8_s,
-    h8_r,
-    h16_s,
-    h16_r,
+    st_s,
+    st_r,
+    hd_s,
+    hd_r,
     a_s,
     a_r,
     ring_s,
     ring_r,
-    two_s,
-    two_r,
-    three_s,
-    three_r,
-    gat3_s,
-    gat3_r,
-    gat2_s,
-    gat2_r,
+    dir_s,
+    dir_r,
     o_s,
     o_r,
     gi_sem,
@@ -132,15 +120,24 @@
     z = lax.axis_index("cols")
     core = lax.rem(me, 2)
     chip = me // 2
+    x = chip // 4
+    y = lax.rem(chip, 4)
     rank8 = z * 2 + core
-
-    def dev8(j):
-        return (chip * 2 + lax.rem(j, 2), j // 2)
-
-    def dev16(j):
-        return (j * 2 + core, z)
-
-    other = (chip * 2 + 1 - core, z)
+    coords = {"x": x, "y": y, "z": z}
+
+    def flip(value, bits):
+        return lax.bitwise_xor(value, jnp.int32(bits)) if bits else value
+
+    def dev8(k):
+        return (flip(me, k % 2), flip(z, k // 2))
+
+    def dev16(k):
+        return (flip(me, 2 * k), z)
+
+    def on_axis(axis, k):
+        return (me, flip(z, k)) if axis == "z" else (flip(me, (2 if axis == "y" else 8) * k), z)
+
+    other = (flip(me, 1), z)
     up = lax.rem(me + 31, 32)
     down = lax.rem(me + 1, 32)
     west = lax.rem(z + 3, 4)
@@ -153,15 +150,11 @@
         pl.semaphore_signal(barrier, inc=1, device_id=device, device_id_type=MESH)
 
     for k in range(1, 8):
-        greet(dev8(lax.rem(rank8 + k, 8)))
+        greet(dev8(k))
     for col in (west, z, east):
         greet((beyond, col))
-
-    def greet16(k, carry):
-        greet(dev16(lax.rem(chip + k, 16)))
-        return carry
-
-    lax.fori_loop(1, 16, greet16, 0)
+    for k in range(1, 16):
+        greet(dev16(k))
 
     wcopies = []
     for t in range(TAPS):
@@ -348,46 +341,36 @@
             spread_sum = term if spread_sum is None else spread_sum + term
         return mid, spread_sum
 
-    def exchange(buf, rank, size, dev, ssem, rsem):
-        def copy_to(k):
-            return remote(
-                buf.at[rank],
-                buf.at[rank],
-                ssem.at[k],
-                rsem.at[rank],
-                dev(lax.rem(rank + k, size)),
-            )
+    def exchange(size, devices, src_of, land, rank, ssem, rsem):
+        def all_of(sem):
+            few = land.at[0 : size - 1]
+            return pltpu.make_async_copy(few, few, sem)
 
         def start():
-            def body(k, carry):
-                copy_to(k).start()
-                return carry
-
-            lax.fori_loop(1, size, body, 0)
-
-        def wait():
-            def body(k, carry):
-                j = lax.rem(rank + k, size)
-                remote(buf.at[j], buf.at[j], ssem.at[k], rsem.at[j], dev(j)).wait_recv()
-                return carry
-
-            lax.fori_loop(1, size, body, 0)
-
-        def finish():
-            def body(k, carry):
-                copy_to(k).wait_send()
-                return carry
-
-            lax.fori_loop(1, size, body, 0)
-
-        return start, wait, finish
-
-    st8_x = exchange(st8, rank8, 8, dev8, s8_s, s8_r)
-    st16_x = exchange(st16, chip, 16, dev16, s16_s, s16_r)
-    tot8_x = exchange(tot8, rank8, 8, dev8, t8_s, t8_r)
-    tot16_x = exchange(tot16, chip, 16, dev16, t16_s, t16_r)
-    hd8_x = exchange(hd8, rank8, 8, dev8, h8_s, h8_r)
-    hd16_x = exchange(hd16, chip, 16, dev16, h16_s, h16_r)
+            for k in range(1, size):
+                remote(src_of(flip(rank, k)), land.at[rank], ssem, rsem, devices(k)).start()
+
+        return start, lambda: all_of(rsem).wait(), lambda: all_of(ssem).wait()
+
+    def share(size, devices, land, rank, ssem, rsem):
+        return exchange(size, devices, lambda j: land.at[rank], land, rank, ssem, rsem)
+
+    def along(axis, src_of, land, ssem, rsem):
+        return exchange(
+            4, lambda k: on_axis(axis, k), src_of, land, coords[axis], ssem, rsem
+        )
+
+    def share_along(axis, land, ssem, rsem):
+        return along(axis, lambda j: land.at[coords[axis]], land, ssem, rsem)
+
+    st8_x = share(8, dev8, st8, rank8, st_s.at[0], st_r.at[0])
+    st16_x = share(16, dev16, st16, chip, st_s.at[1], st_r.at[1])
+    tot8_x = share(8, dev8, tot8, rank8, st_s.at[2], st_r.at[2])
+    tot16_x = share(16, dev16, tot16, chip, st_s.at[3], st_r.at[3])
+    hd2_copy = remote(hd2.at[core], hd2.at[core], hd_s.at[0], hd_r.at[0], other)
+    hdz_x = along("z", lambda j: hdz_send.at[j], hdz, hd_s.at[1], hd_r.at[1])
+    hdy_x = share_along("y", hdy, hd_s.at[2], hd_r.at[2])
+    hdx_x = share_along("x", hdx, hd_s.at[3], hd_r.at[3])
 
     mid, m2 = combine([st_local[h] for h in range(H)], float(PIX))
     st8[rank8, 0:1] = mid
@@ -463,8 +446,12 @@
     tot8_x[1]()
     tot16[chip] = add_up(tot8, 8)
     tot16_x[0]()
-    hd8[rank8] = head_sum[0:4, :]
-    hd8_x[0]()
+    hd2[core] = head_sum[0:4, :]
+    hd2_copy.start()
+    st8_x[2]()
+    st16_x[2]()
+    for copy in xrow_copies + xedge_copies:
+        copy.wait_send()
     tot16_x[1]()
     totals = add_up(tot16, 16)
     off = totals[0:1] * (1.0 / COUNT)
@@ -494,18 +481,6 @@
     for copy in gedge_copies:
         copy.start()
 
-    x = chip // 4
-    y = lax.rem(chip, 4)
-    coords = {"x": x, "y": y, "z": z}
-
-    def on_axis(axis, j):
-        j = lax.rem(j, 4)
-        if axis == "z":
-            return (me, j)
-        if axis == "y":
-            return ((x * 4 + j) * 2 + core, z)
-        return ((j * 4 + y) * 2 + core, z)
-
     ORDERS = (("z", "y", "x"), ("x", "z", "y"), ("y", "z", "x"))
     mine = pl.ds(pl.multiple_of(core * 128, 128), 128)
     theirs = pl.ds(pl.multiple_of((1 - core) * 128, 128), 128)
@@ -545,30 +520,36 @@
             return acc[r, low:high, pl.ds(pl.multiple_of(q * 128, 128), 128)]
         return acc[r, pl.ds(pl.multiple_of(q * 96 + low, 16), high - low), :]
 
+    def around(axis, way):
+        step = 1 if way == 0 else 3
+        if axis == "z":
+            return (me, lax.rem(z + step, 4))
+        stride = 2 if axis == "y" else 8
+        here = coords[axis]
+        return (me + stride * (lax.rem(here + step, 4) - here), z)
+
     def ring1_copies(r):
         axis = ORDERS[r][0]
-        here = coords[axis]
         return [
             remote(
                 ring1_send[r].at[way],
                 ring1_recv[r].at[way],
                 ring_s.at[r, way],
                 ring_r.at[r, way],
-                on_axis(axis, here + (1, 3)[way]),
+                around(axis, way),
             )
             for way in range(2)
         ]
 
     def ring2_copies(r):
         axis = ORDERS[r][0]
-        here = coords[axis]
         return [
             remote(
                 ring2_send[r].at[way],
                 ring2_recv[r].at[way],
                 ring_s.at[r, 2 + way],
                 ring_r.at[r, 2 + way],
-                on_axis(axis, here + (1, 3)[way]),
+                around(axis, way),
             )
             for way in range(2)
         ]
@@ -597,72 +578,29 @@
         for copy in ring2_copies(r):
             copy.start()
 
-    def along(r, axis, send, recv, ssem, rsem, piece):
-        here = coords[axis]
-
-        def towards(k):
-            j = lax.rem(here + k, 4)
-            return remote(piece(send, j), recv.at[r, here], ssem.at[r, k], rsem.at[r, here], on_axis(axis, j))
-
-        def arriving(k):
-            j = lax.rem(here + k, 4)
-            return remote(piece(send, j), recv.at[r, j], ssem.at[r, k], rsem.at[r, j], on_axis(axis, j))
-
-        def start():
-            for k in range(1, 4):
-                towards(k).start()
-
-        def wait():
-            for k in range(1, 4):
-                arriving(k).wait_recv()
-
-        def finish():
-            for k in range(1, 4):
-                towards(k).wait_send()
-
-        return start, wait, finish
-
-    second = [
-        along(r, ORDERS[r][1], two_send, two_recv, two_s, two_r, lambda ref, j, r=r: ref.at[r, j])
-        for r in range(3)
-    ]
-    third = [
-        along(
-            r,
-            ORDERS[r][2],
-            three_send,
-            three_recv,
-            three_s,
-            three_r,
-            lambda ref, j, r=r: ref.at[r, j],
+    row_axis = ("y", "x", "y")
+    second, third, gather3, gather2 = [], [], [], []
+    for r in range(3):
+        second.append(
+            along(
+                ORDERS[r][1],
+                lambda j, r=r: two_send.at[r, j],
+                two_recv.at[r],
+                dir_s.at[0, r],
+                dir_r.at[0, r],
+            )
         )
-        for r in range(3)
-    ]
-    row_axis = ("y", "x", "y")
-    gather3 = [
-        along(
-            r,
-            ORDERS[r][2],
-            gat3,
-            gat3,
-            gat3_s,
-            gat3_r,
-            lambda ref, j, r=r: ref.at[r, coords[ORDERS[r][2]]],
+        third.append(
+            along(
+                ORDERS[r][2],
+                lambda j, r=r: three_send.at[r, j],
+                three_recv.at[r],
+                dir_s.at[1, r],
+                dir_r.at[1, r],
+            )
         )
-        for r in range(3)
-    ]
-    gather2 = [
-        along(
-            r,
-            row_axis[r],
-            gat2,
-            gat2,
-            gat2_s,
-            gat2_r,
-            lambda ref, j, r=r: ref.at[r, coords[row_axis[r]]],
-        )
-        for r in range(3)
-    ]
+        gather3.append(share_along(ORDERS[r][2], gat3.at[r], dir_s.at[2, r], dir_r.at[2, r]))
+        gather2.append(share_along(row_axis[r], gat2.at[r], dir_s.at[3, r], dir_r.at[3, r]))
 
     def stage2(r):
         for copy in ring2_copies(r):
@@ -686,7 +624,7 @@
         here = coords[ORDERS[r][1]]
         total = two_own[r, here]
         for k in range(1, 4):
-            total = total + two_recv[r, lax.rem(here + k, 4)].astype(F32)
+            total = total + two_recv[r, flip(here, k)].astype(F32)
         for q in range(4):
             three_send[r, q] = total[q * 24 : (q + 1) * 24]
         third[r][0]()
@@ -696,7 +634,7 @@
         here = coords[ORDERS[r][2]]
         total = three_send[r, here]
         for k in range(1, 4):
-            total = total + three_recv[r, lax.rem(here + k, 4)]
+            total = total + three_recv[r, flip(here, k)]
         gat3[r, here] = total
         gather3[r][0]()
 
@@ -753,12 +691,23 @@
         return carry
 
     kernel_grad(0)
-    hd8_x[1]()
-    hd16[chip] = add_up(hd8, 8)
-    hd16_x[0]()
+    hd2_copy.wait_recv()
+    head_pair = hd2[0] + hd2[1]
+    for q in range(4):
+        hdz_send[q] = head_pair[:, q * 128 : (q + 1) * 128]
+    hdz_x[0]()
     kernel_grad(1)
     ring1(0)
+    hdz_x[1]()
+    head_line = hdz_send[z]
+    for k in range(1, 4):
+        head_line = head_line + hdz[flip(z, k)]
+    hdy[y] = head_line
+    hdy_x[0]()
     kernel_grad(2)
+    hdy_x[1]()
+    hdx[x] = add_up(hdy, 4)
+    hdx_x[0]()
     ring1(1)
     ring2(0)
     for copy in gedge_copies:
@@ -768,6 +717,8 @@
     ring2(1)
     stage2(0)
     back(1)
+    hdx_x[1]()
+    gh_out[...] = add_up(hdx, 4)
     ring2(2)
     stage2(1)
     stage3(0)
@@ -786,24 +737,19 @@
     collect3(2)
     collect2(1)
     swap(0)
-    hd16_x[1]()
-    head_all[...] = add_up(hd16, 16)
-    gh_out[...] = head_all[:, pl.ds(pl.multiple_of(z * 128, 128), 128)]
     collect2(2)
     swap(1)
     unpack_other(0)
     swap(2)
     unpack_other(1)
 
-    for copy in xrow_copies + xedge_copies + grow_copies + gedge_copies + a_copies:
+    for copy in [hd2_copy] + grow_copies + gedge_copies + a_copies:
         copy.wait_send()
-    for exchanged in (st8_x, st16_x, tot8_x, tot16_x, hd8_x, hd16_x):
+    for exchanged in [tot8_x, tot16_x, hdz_x, hdy_x, hdx_x] + second + third + gather3 + gather2:
         exchanged[2]()
     for r in range(3):
         for copy in ring1_copies(r) + ring2_copies(r):
             copy.wait_send()
-        for exchanged in (second[r], third[r], gather3[r], gather2[r]):
-            exchanged[2]()
     for copy in gi_copies:
         copy.wait()
     unpack_other(2)
@@ -890,9 +836,11 @@
             vmem((16, 2, CO), F32),
             vmem((8, 2, CO), F32),
             vmem((16, 2, CO), F32),
-            vmem((8, 4, CO), F32),
-            vmem((16, 4, CO), F32),
-            vmem((4, CO), F32),
+            vmem((2, 4, CO), F32),
+            vmem((4, 4, 128), F32),
+            vmem((4, 4, 128), F32),
+            vmem((4, 4, 128), F32),
+            vmem((4, 4, 128), F32),
             vmem((3, 3, CI, CO), F32),
             vmem((3, 3, 128, CO), BF16),
             vmem((3, 3, 128, CO), BF16),
@@ -928,20 +876,14 @@
             dma((6,)),
             dma((6,)),
         ]
-        + [dma((n,)) for n in (8, 8, 16, 16) * 3]
+        + [dma((4,))] * 4
         + [
             dma((3,)),
             dma((3,)),
             dma((3, 4)),
             dma((3, 4)),
-            dma((3, 4)),
-            dma((3, 4)),
-            dma((3, 4)),
-            dma((3, 4)),
-            dma((3, 4)),
-            dma((3, 4)),
-            dma((3, 4)),
-            dma((3, 4)),
+            dma((4, 3)),
+            dma((4, 3)),
             dma((3,)),
             dma((3,)),
             dma((H,)),

time: 90.8 us -> 89.8 us (0.989)
    pallas_call x1, Pallas kernels: 86.3 us -> 85.4 us  [per_device(): pl.pallas_call(kernel, out_shape=(jax.ShapeDtypeStruct((TAPS, CI, 128), F...]
where the time goes in v3:
time: 89.8 us; the launch traced here: 89.7 us
  Pallas kernels  88.9 us (99%)
    pallas_call x1, Pallas kernels, per_device(): pl.pallas_call(kernel, out_shape=(jax.ShapeDtypeStruct((TAPS, CI, 128), F...  85.4 us
    pallas_call x1, Pallas kernels, move_out(): pl.pallas_call(move_kernel, out_shape=tuple((jax.ShapeDtypeStruct(a.shape...  3.49 us

profile of v3, /device:TPU:1, one launch (start us, length us, event | category | flops | bytes accessed | tf_op | source)
XLA Modules:
  0.0 89.7 jit_solution(10621876082731800455)
XLA Ops:
  0.6 85.4 %shard_map.110 = (f32[9,256,128]{2,1,0:T(8,128)}, f32[1,128]{1,0:T(1,128)}, f32[1,128]{1,0:T(1,128)}, f32[4,128]{1,0:T(4,128)}, f32[4,4,128,256]{3,2,1,0:T(8,128)}) custom-call(bf16[4,4,128,256]{3,2,1,0:T(8,128)(2,1)} %feat.1, bf16[2304,512]{1,0:T(8,128)(2,1)} %bitcast.8, f32[1,512]{1,0:T(1,128)} %bitcast.11, f32[1,512]{1,0:T(1,128)} %bitcast.12, ...), custom_call_target="tpu_custom_call" | custom-call | flops 15000000512 | bytes 8000000 | tf_op jit(solution)/shard_map/pallas_call | solution.py:797
  86.0 3.5 %shard_map.111 = (f32[9,256,128]{2,1,0:T(8,128)}, f32[1,128]{1,0:T(1,128)}, f32[1,128]{1,0:T(1,128)}, f32[4,128]{1,0:T(4,128)}, f32[4,4,128,256]{3,2,1,0:T(8,128)}) custom-call(f32[9,256,128]{2,1,0:T(8,128)} %get-tuple-element.15.refs_0_, f32[1,128]{1,0:T(1,128)} %get-tuple-element.16.refs_1_, f32[1,128]{1,0:T(1,128)} %get-tuple-element.17.refs_2_, ...), custom_call_target="tpu_custom_call" | custom-call | tf_op jit(solution)/shard_map/pallas_call | solution.py:782

commit v4 on v3

--- a/solution.py
+++ b/solution.py
@@ -69,9 +69,10 @@
     hdy,
     hdx,
     part,
+    with_conv,
+    with_one,
     send_a,
     recv_a,
-    acc,
     ring1z_send,
     ring1x_send,
     ring1y_send,
@@ -92,7 +93,6 @@
     gat3,
     gat2,
     gat_other,
-    gi_buf,
     wsem,
     xrow_s,
     xrow_r,
@@ -219,6 +219,17 @@
     head_pad[4:8] = head_ref[...].astype(F32)
     head_tile[...] = jnp.transpose(jnp.concatenate([head_pad[0:8]] * 16, axis=0)).astype(BF16)
 
+    lane_class = lax.rem(lax.broadcasted_iota(jnp.int32, (W, 128), 1), 4).astype(F32)
+    for b in range(B):
+        for h in range(H):
+            label = labels_ref[b, h : h + 1, :].astype(F32)
+            weight = raster_ref[b, h : h + 1, :].astype(F32)
+            label_t = jnp.transpose(jnp.broadcast_to(label, (128, W)))
+            weight_t = jnp.transpose(jnp.broadcast_to(weight, (128, W)))
+            marks = jnp.where(label_t == lane_class, 1.0, 0.0)
+            onehot[h, b * W : (b + 1) * W] = marks.astype(BF16)
+            pixw[h, b * W : (b + 1) * W] = ((1.0 + weight_t) * 0.25).astype(BF16)
+
     west_ok = jnp.where(z > 0, 1.0, 0.0).astype(F32)
     east_ok = jnp.where(z < 3, 1.0, 0.0).astype(F32)
     up_ok = jnp.where(me > 0, 1.0, 0.0).astype(F32)
@@ -377,26 +388,33 @@
     st8[rank8, 1:2] = m2
     st8_x[0]()
 
+    local_mean = mid
     transpose_x(0)
     transpose_x(H + 1)
-    transpose_w(TAPS - 1)
-
+
+    def center(h, carry):
+        act[h] = (conv[h] - local_mean).astype(BF16)
+        return carry
+
+    lax.fori_loop(0, H, center, 0)
+
+    def features_of(r):
+        return jnp.concatenate([xt[h + r] for h in range(H)], axis=1)
+
+    def cross_conv(r, carry):
+        lhs = features_of(r)
+        with_conv[r] = jnp.dot(lhs, act[...].reshape(B * PIX, CO), preferred_element_type=F32)
+        with_one[r] = jnp.dot(lhs, jnp.ones((B * PIX, 128), BF16), preferred_element_type=F32)
+        return carry
+
+    lax.fori_loop(0, 1, cross_conv, 0)
     st8_x[1]()
     mid, m2 = combine([st8[j] for j in range(8)], float(B * PIX))
     st16[chip, 0:1] = mid
     st16[chip, 1:2] = m2
     st16_x[0]()
-
-    lane_class = lax.rem(lax.broadcasted_iota(jnp.int32, (W, 128), 1), 4).astype(F32)
-    for b in range(B):
-        for h in range(H):
-            label = labels_ref[b, h : h + 1, :].astype(F32)
-            weight = raster_ref[b, h : h + 1, :].astype(F32)
-            label_t = jnp.transpose(jnp.broadcast_to(label, (128, W)))
-            weight_t = jnp.transpose(jnp.broadcast_to(weight, (128, W)))
-            onehot[h, b * W : (b + 1) * W] = jnp.where(label_t == lane_class, 1.0, 0.0)
-            pixw[h, b * W : (b + 1) * W] = (1.0 + weight_t) * 0.25
-
+    lax.fori_loop(1, 3, cross_conv, 0)
+    transpose_w(TAPS - 1)
     st16_x[1]()
     mean, m2 = combine([st16[j] for j in range(16)], float(8 * B * PIX))
     rstd = lax.rsqrt(m2 * (1.0 / COUNT) + EPS)
@@ -414,11 +432,12 @@
         expo = jnp.exp(logits)
         total = expo + pltpu.roll(expo, 1, 1)
         total = total + pltpu.roll(total, 2, 1)
-        score = (pixw[b] * (expo / total - onehot[b])).astype(BF16)
+        score = (pixw[b].astype(F32) * (expo / total - onehot[b].astype(F32))).astype(BF16)
         sgs[b] = score
         act_grad = jnp.dot(score, head_t[...], preferred_element_type=F32)
         pre_grad = jnp.where(pre > 0.0, act_grad, 0.0)
         pgs[b] = pre_grad
+        gc[b + 1] = pre_grad.astype(BF16).reshape(B, W, CO)
         sum_g = sum_g + jnp.sum(pre_grad, axis=0, keepdims=True)
         sum_gn = sum_gn + jnp.sum(pre_grad * away, axis=0, keepdims=True)
         return sum_g, sum_gn
@@ -436,16 +455,25 @@
     tot8[rank8, 1:2] = sum_gn * rstd
     tot8_x[0]()
 
+    def cross_grad(r, carry):
+        part[r] = jnp.dot(
+            features_of(r),
+            gc[1 : H + 1].reshape(B * PIX, CO),
+            preferred_element_type=F32,
+        ).reshape(3, CI, CO)
+        return carry
+
     def head_part(b, total):
         return total + lax.dot_general(
             sgs[b], act[b], (((0,), (0,)), ((), ())), preferred_element_type=F32
         )
 
-    head_sum = lax.fori_loop(0, B, head_part, jnp.zeros((128, CO), F32))
-
+    lax.fori_loop(0, 1, cross_grad, 0)
     tot8_x[1]()
     tot16[chip] = add_up(tot8, 8)
     tot16_x[0]()
+    lax.fori_loop(1, 3, cross_grad, 0)
+    head_sum = lax.fori_loop(0, B, head_part, jnp.zeros((128, CO), F32))
     hd2[core] = head_sum[0:4, :]
     hd2_copy.start()
     st8_x[2]()
@@ -460,6 +488,29 @@
     gb_out[...] = st_local[0, 0:1, pl.ds(pl.multiple_of(z * 128, 128), 128)]
     gg_out[...] = st_local[0, 1:2, pl.ds(pl.multiple_of(z * 128, 128), 128)]
 
+    ORDERS = (("z", "y", "x"), ("x", "z", "y"), ("y", "z", "x"))
+    a_copies = [remote(send_a.at[r], recv_a.at[r], a_s.at[r], a_r.at[r], other) for r in range(3)]
+
+    shift = scale * (off + slope * (local_mean - mean))
+    turn = scale * slope
+
+    def kernel_grad(r, half):
+        pieces = []
+        for c in range(3):
+            rows = pl.ds(pl.multiple_of(c * CI + half * 128, 128), 128)
+            ones = jnp.concatenate([with_one[r, rows, :]] * 4, axis=1)
+            pieces.append(
+                part[r, c, pl.ds(pl.multiple_of(half * 128, 128), 128), :] * scale
+                - with_conv[r, rows, :] * turn
+                - ones * shift
+            )
+        return pieces
+
+    for r in range(3):
+        for c, piece in enumerate(kernel_grad(r, 1 - core)):
+            send_a[r, c] = piece.astype(BF16)
+        a_copies[r].start()
+
     def conv_grad(i, carry):
         b = lax.rem(i, B)
         h = lax.rem(3 * (i // B), H)
@@ -467,38 +518,10 @@
         away = conv[h, spot] - mean
         value = scale * (pgs[h, spot] - off - away * slope)
         gc[h + 1, b] = value.astype(BF16)
+        gl[h + 1, b], gr[h + 1, b] = shifted(value, 0.0, 0.0)
         gedge_f[0, pl.ds(h * B + b, 1)] = value[W - 1 : W, :]
         gedge_f[1, pl.ds(h * B + b, 1)] = value[0:1, :]
         return carry
-
-    lax.fori_loop(0, 2 * B, conv_grad, 0)
-    grow_copies = row_sends(gc.at[1], gc.at[H], grow, grow_s, grow_r)
-    for copy in grow_copies:
-        copy.start()
-    lax.fori_loop(2 * B, 4 * B, conv_grad, 0)
-    gedge_out[...] = gedge_f[...].astype(BF16)
-    gedge_copies = edge_sends(gedge_out, gedge_in, gedge_s, gedge_r)
-    for copy in gedge_copies:
-        copy.start()
-
-    ORDERS = (("z", "y", "x"), ("x", "z", "y"), ("y", "z", "x"))
-    mine = pl.ds(pl.multiple_of(core * 128, 128), 128)
-    theirs = pl.ds(pl.multiple_of((1 - core) * 128, 128), 128)
-    a_copies = [remote(send_a.at[r], recv_a.at[r], a_s.at[r], a_r.at[r], other) for r in range(3)]
-
-    def build_g(i):
-        h, b = divmod(i, B)
-        value = gc[h + 1, b].astype(F32)
-        gl[h + 1, b], gr[h + 1, b] = shifted(value, 0.0, 0.0)
-
-    def kernel_grad(r):
-        for i in ((0, 1, 2, 3, 4), (5, 6, 7, 8, 9), (10, 11, 12, 13, 14, 15))[r]:
-            build_g(i)
-        lhs = jnp.concatenate([xt[h + r] for h in range(H)], axis=1)
-        grad = gc[1 : H + 1].reshape(B * PIX, CO)
-        part[r] = jnp.dot(lhs, grad, preferred_element_type=F32).reshape(3, CI, CO)
-        send_a[r] = part[r, :, theirs, :].astype(BF16)
-        a_copies[r].start()
 
     ring1_send, ring1_recv = (ring1z_send, ring1x_send, ring1y_send), (
         ring1z_recv,
@@ -517,8 +540,8 @@
     def block(r, q, low, high):
         q = lax.rem(q, 4)
         if r == 0:
-            return acc[r, low:high, pl.ds(pl.multiple_of(q * 128, 128), 128)]
-        return acc[r, pl.ds(pl.multiple_of(q * 96 + low, 16), high - low), :]
+            return with_conv[r, low:high, pl.ds(pl.multiple_of(q * 128, 128), 128)]
+        return with_conv[r, pl.ds(pl.multiple_of(q * 96 + low, 16), high - low), :]
 
     def around(axis, way):
         step = 1 if way == 0 else 3
@@ -556,7 +579,8 @@
 
     def ring1(r):
         a_copies[r].wait_recv()
-        acc[r] = part[r, :, mine, :].reshape(384, CO) + recv_a[r].reshape(384, CO).astype(F32)
+        for c, piece in enumerate(kernel_grad(r, core)):
+            with_conv[r, c * 128 : (c + 1) * 128] = piece + recv_a[r, c].astype(F32)
         here, half = coords[ORDERS[r][0]], halves(r)
         ring1_send[r][0] = block(r, here + 2, 0, half).astype(BF16)
         ring1_send[r][1] = block(r, here + 2, half, 2 * half).astype(BF16)
@@ -662,7 +686,13 @@
         unpack(r, gat_other, 1 - core)
 
     gi_copies = [
-        pltpu.make_async_copy(gi_buf.at[h], gi_out.at[:, h], gi_sem.at[h]) for h in range(H)
+        [
+            pltpu.make_async_copy(
+                pgs.at[h, pl.ds(b * W, W), pl.ds(0, CI)], gi_out.at[b, h], gi_sem.at[h, b]
+            )
+            for b in range(B)
+        ]
+        for h in range(H)
     ]
 
     def back(h):
@@ -675,8 +705,9 @@
             axis=1,
         )
         value = jnp.dot(lhs, wgt_t[...], preferred_element_type=F32)
-        gi_buf[h] = value.reshape(B, W, CI)
-        gi_copies[h].start()
+        pgs[h, :, 0:CI] = value
+        for copy in gi_copies[h]:
+            copy.start()
 
     def set_edges(i, carry):
         h = i // B
@@ -690,57 +721,63 @@
         gr[h + 1, b, W - 16 : W] = jnp.where(ids == 15, top, block16).astype(BF16)
         return carry
 
-    kernel_grad(0)
+    lax.fori_loop(0, 2 * B, conv_grad, 0)
+    grow_copies = row_sends(gc.at[1], gc.at[H], grow, grow_s, grow_r)
+    for copy in grow_copies:
+        copy.start()
+    ring1(0)
+    lax.fori_loop(2 * B, 4 * B, conv_grad, 0)
+    gedge_out[...] = gedge_f[...].astype(BF16)
+    gedge_copies = edge_sends(gedge_out, gedge_in, gedge_s, gedge_r)
+    for copy in gedge_copies:
+        copy.start()
+    ring1(1)
+    ring1(2)
     hd2_copy.wait_recv()
     head_pair = hd2[0] + hd2[1]
     for q in range(4):
         hdz_send[q] = head_pair[:, q * 128 : (q + 1) * 128]
     hdz_x[0]()
-    kernel_grad(1)
-    ring1(0)
+    ring2(0)
+    ring2(1)
+    ring2(2)
+    for copy in gedge_copies:
+        copy.wait_recv()
+    lax.fori_loop(0, B * H, set_edges, 0)
     hdz_x[1]()
     head_line = hdz_send[z]
     for k in range(1, 4):
         head_line = head_line + hdz[flip(z, k)]
     hdy[y] = head_line
     hdy_x[0]()
-    kernel_grad(2)
+    back(1)
+    stage2(0)
+    stage2(1)
+    stage2(2)
     hdy_x[1]()
     hdx[x] = add_up(hdy, 4)
     hdx_x[0]()
-    ring1(1)
-    ring2(0)
-    for copy in gedge_copies:
-        copy.wait_recv()
-    lax.fori_loop(0, B * H, set_edges, 0)
-    ring1(2)
-    ring2(1)
-    stage2(0)
-    back(1)
-    hdx_x[1]()
-    gh_out[...] = add_up(hdx, 4)
-    ring2(2)
-    stage2(1)
+    back(2)
     stage3(0)
-    back(2)
-    stage2(2)
     stage3(1)
-    collect3(0)
+    stage3(2)
     for copy in grow_copies:
         copy.wait_recv()
     build_halo(grow, gedge_in, gl, gc, gr)
+    hdx_x[1]()
+    gh_out[...] = add_up(hdx, 4)
+    collect3(0)
+    collect3(1)
+    collect3(2)
     back(0)
-    stage3(2)
-    collect3(1)
     collect2(0)
+    collect2(1)
+    collect2(2)
     back(3)
-    collect3(2)
-    collect2(1)
     swap(0)
-    collect2(2)
     swap(1)
+    swap(2)
     unpack_other(0)
-    swap(2)
     unpack_other(1)
 
     for copy in [hd2_copy] + grow_copies + gedge_copies + a_copies:
@@ -750,8 +787,9 @@
     for r in range(3):
         for copy in ring1_copies(r) + ring2_copies(r):
             copy.wait_send()
-    for copy in gi_copies:
-        copy.wait()
+    for line in gi_copies:
+        for copy in line:
+            copy.wait()
     unpack_other(2)
     for copy in o_copies:
         copy.wait_send()
@@ -816,8 +854,8 @@
             vmem((H, PIX, CO), F32),
             vmem((H, PIX, CO), BF16),
             vmem((H, PIX, 128), BF16),
-            vmem((H, PIX, 128), F32),
-            vmem((H, PIX, 128), F32),
+            vmem((H, PIX, 128), BF16),
+            vmem((H, PIX, 128), BF16),
             vmem((128, CO), F32),
             vmem((CO, 128), BF16),
             vmem((128, CO), BF16),
@@ -842,9 +880,10 @@
             vmem((4, 4, 128), F32),
             vmem((4, 4, 128), F32),
             vmem((3, 3, CI, CO), F32),
+            vmem((3, 3 * CI, CO), F32),
+            vmem((3, 3 * CI, 128), F32),
             vmem((3, 3, 128, CO), BF16),
             vmem((3, 3, 128, CO), BF16),
-            vmem((3, 384, CO), F32),
             vmem((2, 192, 128), BF16),
             vmem((2, 48, CO), BF16),
             vmem((2, 48, CO), BF16),
@@ -865,7 +904,6 @@
             vmem((3, 4, 24, 128), F32),
             vmem((3, 4, 96, 128), BF16),
             vmem((3, 4, 96, 128), BF16),
-            vmem((H, B, W, CI), F32),
             dma((TAPS,)),
             dma((2,)),
             dma((2,)),
@@ -886,7 +924,7 @@
             dma((4, 3)),
             dma((3,)),
             dma((3,)),
-            dma((H,)),
+            dma((H, B)),
         ],
         compiler_params=pltpu.CompilerParams(
             collective_id=0, has_side_effects=True, vmem_limit_bytes=60 * 1024 * 1024

time: 89.8 us -> 87 us (0.969)
  Pallas kernels: 88.9 us -> 86.1 us
    pallas_call x1, Pallas kernels: 85.4 us -> 82.6 us  [per_device(): pl.pallas_call(kernel, out_shape=(jax.ShapeDtypeStruct((TAPS, CI, 128), F...]
where the time goes in v4:
time: 87 us; the launch traced here: 86.9 us
  Pallas kernels  86.1 us (99%)
    pallas_call x1, Pallas kernels, per_device(): pl.pallas_call(kernel, out_shape=(jax.ShapeDtypeStruct((TAPS, CI, 128), F...  82.6 us
    pallas_call x1, Pallas kernels, move_out(): pl.pallas_call(move_kernel, out_shape=tuple((jax.ShapeDtypeStruct(a.shape...  3.49 us

profile of v4, /device:TPU:1, one launch (start us, length us, event | category | flops | bytes accessed | tf_op | source)
XLA Modules:
  0.0 86.9 jit_solution(129732566813559919)
XLA Ops:
  0.6 82.6 %shard_map.110 = (f32[9,256,128]{2,1,0:T(8,128)}, f32[1,128]{1,0:T(1,128)}, f32[1,128]{1,0:T(1,128)}, f32[4,128]{1,0:T(4,128)}, f32[4,4,128,256]{3,2,1,0:T(8,128)}) custom-call(bf16[4,4,128,256]{3,2,1,0:T(8,128)(2,1)} %feat.1, bf16[2304,512]{1,0:T(8,128)(2,1)} %bitcast.8, f32[1,512]{1,0:T(1,128)} %bitcast.11, f32[1,512]{1,0:T(1,128)} %bitcast.12, ...), custom_call_target="tpu_custom_call" | custom-call | flops 15000000512 | bytes 8000000 | tf_op jit(solution)/shard_map/pallas_call | solution.py:835
  83.2 3.5 %shard_map.111 = (f32[9,256,128]{2,1,0:T(8,128)}, f32[1,128]{1,0:T(1,128)}, f32[1,128]{1,0:T(1,128)}, f32[4,128]{1,0:T(4,128)}, f32[4,4,128,256]{3,2,1,0:T(8,128)}) custom-call(f32[9,256,128]{2,1,0:T(8,128)} %get-tuple-element.15.refs_0_, f32[1,128]{1,0:T(1,128)} %get-tuple-element.16.refs_1_, f32[1,128]{1,0:T(1,128)} %get-tuple-element.17.refs_2_, ...), custom_call_target="tpu_custom_call" | custom-call | tf_op jit(solution)/shard_map/pallas_call | solution.py:820

commit v5 on v4

--- a/solution.py
+++ b/solution.py
@@ -35,9 +35,7 @@
     gi_out,
     wgt,
     wgt_t,
-    xl,
-    xc,
-    xr,
+    x3,
     xt,
     conv,
     pgs,
@@ -220,15 +218,20 @@
     head_tile[...] = jnp.transpose(jnp.concatenate([head_pad[0:8]] * 16, axis=0)).astype(BF16)
 
     lane_class = lax.rem(lax.broadcasted_iota(jnp.int32, (W, 128), 1), 4).astype(F32)
-    for b in range(B):
-        for h in range(H):
-            label = labels_ref[b, h : h + 1, :].astype(F32)
-            weight = raster_ref[b, h : h + 1, :].astype(F32)
-            label_t = jnp.transpose(jnp.broadcast_to(label, (128, W)))
-            weight_t = jnp.transpose(jnp.broadcast_to(weight, (128, W)))
-            marks = jnp.where(label_t == lane_class, 1.0, 0.0)
-            onehot[h, b * W : (b + 1) * W] = marks.astype(BF16)
-            pixw[h, b * W : (b + 1) * W] = ((1.0 + weight_t) * 0.25).astype(BF16)
+
+    def class_marks(i, carry):
+        b = i // H
+        h = lax.rem(i, H)
+        spot = pl.ds(pl.multiple_of(b * W, W), W)
+        label = labels_ref[b, pl.ds(h, 1), :].astype(F32)
+        weight = raster_ref[b, pl.ds(h, 1), :].astype(F32)
+        label_t = jnp.transpose(jnp.broadcast_to(label, (128, W)))
+        weight_t = jnp.transpose(jnp.broadcast_to(weight, (128, W)))
+        onehot[h, spot] = jnp.where(label_t == lane_class, 1.0, 0.0).astype(BF16)
+        pixw[h, spot] = ((1.0 + weight_t) * 0.25).astype(BF16)
+        return carry
+
+    lax.fori_loop(0, B * H, class_marks, 0)
 
     west_ok = jnp.where(z > 0, 1.0, 0.0).astype(F32)
     east_ok = jnp.where(z < 3, 1.0, 0.0).astype(F32)
@@ -246,6 +249,11 @@
         right = jnp.where(ids == W - 1, after, pltpu.roll(value, W - 1, 0))
         return left.astype(BF16), right.astype(BF16)
 
+    def clear(h, carry):
+        conv[h] = jnp.zeros((PIX, CO), F32)
+        return carry
+
+    lax.fori_loop(0, H, clear, 0)
     for copy in xedge_copies:
         copy.wait_recv()
 
@@ -258,14 +266,14 @@
             pick_row(xedge_in, 1, i) * west_ok,
             pick_row(xedge_in, 4, i) * east_ok,
         )
-        xl[h + 1, b] = left
-        xc[h + 1, b] = feat[b, h]
-        xr[h + 1, b] = right
+        x3[0, h + 1, b] = left
+        x3[1, h + 1, b] = feat[b, h]
+        x3[2, h + 1, b] = right
         return carry
 
     lax.fori_loop(0, B * H, build_x, 0)
 
-    def build_halo(land, edge_in, left_ref, mid_ref, right_ref):
+    def build_halo(land, edge_in, store):
         def body(b, carry):
             for side, line, ok, src in ((0, 0, up_ok, H - 1), (1, H + 1, down_ok, 0)):
                 value = land[side, b].astype(F32) * ok
@@ -275,9 +283,7 @@
                     pick_row(edge_in, slot, src * B + b) * (west_ok * ok),
                     pick_row(edge_in, slot + 3, src * B + b) * (east_ok * ok),
                 )
-                left_ref[line, b] = left
-                mid_ref[line, b] = value.astype(BF16)
-                right_ref[line, b] = right
+                store(line, b, left, value.astype(BF16), right)
             return carry
 
         lax.fori_loop(0, B, body, 0)
@@ -285,61 +291,49 @@
     for copy in wcopies:
         copy.wait()
 
-    def conv_rows(h, first, count):
-        lhs = jnp.concatenate(
-            [
-                ref[h + first + r].reshape(PIX, CI)
-                for r in range(count)
-                for ref in (xl, xc, xr)
-            ],
-            axis=1,
-        )
-        start = pl.multiple_of(first * 3 * CI, 3 * CI)
-        return jnp.dot(lhs, wgt[pl.ds(start, count * 3 * CI), :], preferred_element_type=F32)
-
-    def statistics(h, value):
-        mid = jnp.sum(value, axis=0, keepdims=True) * (1.0 / PIX)
-        st_local[h, 0:1] = mid
-        st_local[h, 1:2] = jnp.sum((value - mid) ** 2, axis=0, keepdims=True)
-
-    def transpose_x(line):
-        for c, ref in enumerate((xl, xc, xr)):
-            xt[line, c * CI : (c + 1) * CI, :] = jnp.transpose(ref[line].reshape(PIX, CI))
+    def store_x(line, b, left, value, right):
+        x3[0, line, b] = left
+        x3[1, line, b] = value
+        x3[2, line, b] = right
+
+    def transpose_x(c, line):
+        rows = pl.ds(pl.multiple_of(c * CI, CI), CI)
+        xt[line, rows, :] = jnp.transpose(x3[c, line].reshape(PIX, CI))
 
     def transpose_w(t):
         wgt_t[pl.ds(pl.multiple_of(t * CO, CO), CO), :] = jnp.transpose(
             wgt[pl.ds(pl.multiple_of((TAPS - 1 - t) * CI, CI), CI), :]
         )
 
-    def inner_rows(i, carry):
-        value = conv_rows(1 + i, 0, 3)
-        conv[1 + i] = value
-        transpose_x(1 + i)
-        transpose_x(3 + i)
-        statistics(1 + i, value)
-        return carry
-
-    lax.fori_loop(0, 2, inner_rows, 0)
-
-    def outer_rows(i, carry):
-        conv[3 * i] = conv_rows(3 * i, 1 - i, 2)
-        for t in range(4):
-            transpose_w(4 * i + t)
-        return carry
-
-    lax.fori_loop(0, 2, outer_rows, 0)
-
-    for copy in xrow_copies:
-        copy.wait_recv()
-    build_halo(xrow, xedge_in, xl, xc, xr)
-
-    def halo_rows(i, carry):
-        value = conv[3 * i] + conv_rows(3 * i, 2 * i, 1)
-        conv[3 * i] = value
-        statistics(3 * i, value)
-        return carry
-
-    lax.fori_loop(0, 2, halo_rows, 0)
+    def forward(k, carry):
+        q = k // 4
+        flipped = lax.rem(q, 2)
+        h = 3 * flipped + (1 - 2 * flipped) * lax.rem(k, 4)
+        r = lax.rem(2 * q + 1, 3)
+
+        @pl.when(k == 7)
+        def _():
+            for copy in xrow_copies:
+                copy.wait_recv()
+            build_halo(xrow, xedge_in, store_x)
+
+        lhs = jnp.concatenate([x3[c, h + r].reshape(PIX, CI) for c in range(3)], axis=1)
+        rows = pl.ds(pl.multiple_of(r * 3 * CI, 3 * CI), 3 * CI)
+        conv[h] += jnp.dot(lhs, wgt[rows, :], preferred_element_type=F32)
+        transpose_x(lax.rem(k, 3), 1 + k // 3)
+        transpose_w(lax.rem(k, TAPS))
+        return carry
+
+    lax.fori_loop(0, 12, forward, 0)
+
+    def statistics(h, carry):
+        value = conv[h]
+        mid = jnp.sum(value, axis=0, keepdims=True) * (1.0 / PIX)
+        st_local[h, 0:1] = mid
+        st_local[h, 1:2] = jnp.sum((value - mid) ** 2, axis=0, keepdims=True)
+        return carry
+
+    lax.fori_loop(0, H, statistics, 0)
 
     def combine(parts, count):
         total = parts[0][0:1]
@@ -389,8 +383,12 @@
     st8_x[0]()
 
     local_mean = mid
-    transpose_x(0)
-    transpose_x(H + 1)
+
+    def transpose_outer(i, carry):
+        transpose_x(lax.rem(i, 3), (H + 1) * (i // 3))
+        return carry
+
+    lax.fori_loop(0, 6, transpose_outer, 0)
 
     def center(h, carry):
         act[h] = (conv[h] - local_mean).astype(BF16)
@@ -401,20 +399,34 @@
     def features_of(r):
         return jnp.concatenate([xt[h + r] for h in range(H)], axis=1)
 
-    def cross_conv(r, carry):
-        lhs = features_of(r)
-        with_conv[r] = jnp.dot(lhs, act[...].reshape(B * PIX, CO), preferred_element_type=F32)
-        with_one[r] = jnp.dot(lhs, jnp.ones((B * PIX, 128), BF16), preferred_element_type=F32)
-        return carry
-
-    lax.fori_loop(0, 1, cross_conv, 0)
-    st8_x[1]()
-    mid, m2 = combine([st8[j] for j in range(8)], float(B * PIX))
-    st16[chip, 0:1] = mid
-    st16[chip, 1:2] = m2
-    st16_x[0]()
-    lax.fori_loop(1, 3, cross_conv, 0)
-    transpose_w(TAPS - 1)
+    def half_cols(i):
+        return pl.ds(pl.multiple_of(lax.rem(i, 2) * 256, 256), 256)
+
+    def with_ones(r, carry):
+        with_one[r] = jnp.dot(
+            features_of(r), jnp.ones((B * PIX, 128), BF16), preferred_element_type=F32
+        )
+        return carry
+
+    def cross_conv(i, carry):
+        @pl.when(i == 2)
+        def _():
+            st8_x[1]()
+            first, second_moment = combine([st8[j] for j in range(8)], float(B * PIX))
+            st16[chip, 0:1] = first
+            st16[chip, 1:2] = second_moment
+            st16_x[0]()
+
+        with_conv[i // 2, :, half_cols(i)] = jnp.dot(
+            features_of(i // 2),
+            act[:, :, half_cols(i)].reshape(B * PIX, 256),
+            preferred_element_type=F32,
+        )
+        return carry
+
+    lax.fori_loop(0, 6, cross_conv, 0)
+    lax.fori_loop(0, 3, with_ones, 0)
+
     st16_x[1]()
     mean, m2 = combine([st16[j] for j in range(16)], float(8 * B * PIX))
     rstd = lax.rsqrt(m2 * (1.0 / COUNT) + EPS)
@@ -455,12 +467,18 @@
     tot8[rank8, 1:2] = sum_gn * rstd
     tot8_x[0]()
 
-    def cross_grad(r, carry):
-        part[r] = jnp.dot(
-            features_of(r),
-            gc[1 : H + 1].reshape(B * PIX, CO),
+    def cross_grad(i, carry):
+        @pl.when(i == 2)
+        def _():
+            tot8_x[1]()
+            tot16[chip] = add_up(tot8, 8)
+            tot16_x[0]()
+
+        part[i // 2, :, :, half_cols(i)] = jnp.dot(
+            features_of(i // 2),
+            gc[1 : H + 1, :, :, half_cols(i)].reshape(B * PIX, 256),
             preferred_element_type=F32,
-        ).reshape(3, CI, CO)
+        ).reshape(3, CI, 256)
         return carry
 
     def head_part(b, total):
@@ -468,11 +486,7 @@
             sgs[b], act[b], (((0,), (0,)), ((), ())), preferred_element_type=F32
         )
 
-    lax.fori_loop(0, 1, cross_grad, 0)
-    tot8_x[1]()
-    tot16[chip] = add_up(tot8, 8)
-    tot16_x[0]()
-    lax.fori_loop(1, 3, cross_grad, 0)
+    lax.fori_loop(0, 6, cross_grad, 0)
     head_sum = lax.fori_loop(0, B, head_part, jnp.zeros((128, CO), F32))
     hd2[core] = head_sum[0:4, :]
     hd2_copy.start()
@@ -489,7 +503,10 @@
     gg_out[...] = st_local[0, 1:2, pl.ds(pl.multiple_of(z * 128, 128), 128)]
 
     ORDERS = (("z", "y", "x"), ("x", "z", "y"), ("y", "z", "x"))
-    a_copies = [remote(send_a.at[r], recv_a.at[r], a_s.at[r], a_r.at[r], other) for r in range(3)]
+
+    def a_copy(r):
+        return remote(send_a.at[r], recv_a.at[r], a_s.at[r], a_r.at[r], other)
+
 
     shift = scale * (off + slope * (local_mean - mean))
     turn = scale * slope
@@ -506,10 +523,25 @@
             )
         return pieces
 
-    for r in range(3):
+    def for_other(r, carry):
         for c, piece in enumerate(kernel_grad(r, 1 - core)):
             send_a[r, c] = piece.astype(BF16)
-        a_copies[r].start()
+        a_copy(r).start()
+        return carry
+
+    lax.fori_loop(0, 3, for_other, 0)
+
+    def for_own(r, carry):
+        pieces = kernel_grad(r, core)
+        a_copy(r).wait_recv()
+        for c, piece in enumerate(pieces):
+            with_conv[r, c * 128 : (c + 1) * 128] = piece + recv_a[r, c].astype(F32)
+        return carry
+
+    def store_g(line, b, left, value, right):
+        gl[line, b] = left
+        gc[line, b] = value
+        gr[line, b] = right
 
     def conv_grad(i, carry):
         b = lax.rem(i, B)
@@ -578,9 +610,6 @@
         ]
 
     def ring1(r):
-        a_copies[r].wait_recv()
-        for c, piece in enumerate(kernel_grad(r, core)):
-            with_conv[r, c * 128 : (c + 1) * 128] = piece + recv_a[r, c].astype(F32)
         here, half = coords[ORDERS[r][0]], halves(r)
         ring1_send[r][0] = block(r, here + 2, 0, half).astype(BF16)
         ring1_send[r][1] = block(r, here + 2, half, 2 * half).astype(BF16)
@@ -685,28 +714,26 @@
         o_copies[r].wait_recv()
         unpack(r, gat_other, 1 - core)
 
-    gi_copies = [
-        [
+    def gi_copies(h):
+        return [
             pltpu.make_async_copy(
                 pgs.at[h, pl.ds(b * W, W), pl.ds(0, CI)], gi_out.at[b, h], gi_sem.at[h, b]
             )
             for b in range(B)
         ]
-        for h in range(H)
-    ]
 
     def back(h):
-        lhs = jnp.concatenate(
-            [
-                ref[h + r].reshape(PIX, CO)
-                for r in range(3)
-                for ref in (gl, gc, gr)
-            ],
-            axis=1,
-        )
-        value = jnp.dot(lhs, wgt_t[...], preferred_element_type=F32)
-        pgs[h, :, 0:CI] = value
-        for copy in gi_copies[h]:
+        def kernel_row(r, total):
+            lhs = jnp.concatenate(
+                [ref[h + r].reshape(PIX, CO) for ref in (gl, gc, gr)], axis=1
+            )
+            rows = pl.ds(pl.multiple_of(r * 3 * CO, 3 * CO), 3 * CO)
+            pgs[h, :, 0:CI] += jnp.dot(lhs, wgt_t[rows, :], preferred_element_type=F32)
+            return total
+
+        pgs[h, :, 0:CI] = jnp.zeros((PIX, CI), F32)
+        lax.fori_loop(0, 3, kernel_row, 0)
+        for copy in gi_copies(h):
             copy.start()
 
     def set_edges(i, carry):
@@ -725,14 +752,15 @@
     grow_copies = row_sends(gc.at[1], gc.at[H], grow, grow_s, grow_r)
     for copy in grow_copies:
         copy.start()
+    lax.fori_loop(0, 3, for_own, 0)
     ring1(0)
+    ring1(1)
+    ring1(2)
     lax.fori_loop(2 * B, 4 * B, conv_grad, 0)
     gedge_out[...] = gedge_f[...].astype(BF16)
     gedge_copies = edge_sends(gedge_out, gedge_in, gedge_s, gedge_r)
     for copy in gedge_copies:
         copy.start()
-    ring1(1)
-    ring1(2)
     hd2_copy.wait_recv()
     head_pair = hd2[0] + hd2[1]
     for q in range(4):
@@ -750,45 +778,56 @@
         head_line = head_line + hdz[flip(z, k)]
     hdy[y] = head_line
     hdy_x[0]()
-    back(1)
-    stage2(0)
-    stage2(1)
-    stage2(2)
-    hdy_x[1]()
-    hdx[x] = add_up(hdy, 4)
-    hdx_x[0]()
-    back(2)
-    stage3(0)
-    stage3(1)
-    stage3(2)
-    for copy in grow_copies:
-        copy.wait_recv()
-    build_halo(grow, gedge_in, gl, gc, gr)
-    hdx_x[1]()
-    gh_out[...] = add_up(hdx, 4)
-    collect3(0)
-    collect3(1)
-    collect3(2)
-    back(0)
+
+    def back_rows(i, carry):
+        @pl.when(i == 1)
+        def _():
+            stage2(0)
+            stage2(1)
+            stage2(2)
+            hdy_x[1]()
+            hdx[x] = add_up(hdy, 4)
+            hdx_x[0]()
+
+        @pl.when(i == 2)
+        def _():
+            stage3(0)
+            stage3(1)
+            stage3(2)
+            for copy in grow_copies:
+                copy.wait_recv()
+            build_halo(grow, gedge_in, store_g)
+
+        @pl.when(i == 3)
+        def _():
+            collect3(0)
+            collect3(1)
+            collect3(2)
+            hdx_x[1]()
+            gh_out[...] = add_up(hdx, 4)
+
+        back(lax.rem(i + 1, 4))
+        return carry
+
+    lax.fori_loop(0, H, back_rows, 0)
     collect2(0)
     collect2(1)
     collect2(2)
-    back(3)
     swap(0)
     swap(1)
     swap(2)
     unpack_other(0)
     unpack_other(1)
 
-    for copy in [hd2_copy] + grow_copies + gedge_copies + a_copies:
+    for copy in [hd2_copy] + grow_copies + gedge_copies + [a_copy(r) for r in range(3)]:
         copy.wait_send()
     for exchanged in [tot8_x, tot16_x, hdz_x, hdy_x, hdx_x] + second + third + gather3 + gather2:
         exchanged[2]()
     for r in range(3):
         for copy in ring1_copies(r) + ring2_copies(r):
             copy.wait_send()
-    for line in gi_copies:
-        for copy in line:
+    for h in range(H):
+        for copy in gi_copies(h):
             copy.wait()
     unpack_other(2)
     for copy in o_copies:
@@ -846,9 +885,7 @@
         scratch_shapes=[
             vmem((TAPS * CI, CO), BF16),
             vmem((TAPS * CO, CI), BF16),
-            vmem((H + 2, B, W, CI), BF16),
-            vmem((H + 2, B, W, CI), BF16),
-            vmem((H + 2, B, W, CI), BF16),
+            vmem((3, H + 2, B, W, CI), BF16),
             vmem((H + 2, 3 * CI, PIX), BF16),
             vmem((H, PIX, CO), F32),
             vmem((H, PIX, CO), F32),

time: 87 us -> 89.1 us (1.024)
  Pallas kernels: 86.1 us -> 88.3 us
    pallas_call x1, Pallas kernels: 82.6 us -> 84.8 us  [per_device(): pl.pallas_call(kernel, out_shape=(jax.ShapeDtypeStruct((TAPS, CI, 128), F...]
where the time goes in v5:
time: 89.1 us; the launch traced here: 88.9 us
  Pallas kernels  88.3 us (99%)
    pallas_call x1, Pallas kernels, per_device(): pl.pallas_call(kernel, out_shape=(jax.ShapeDtypeStruct((TAPS, CI, 128), F...  84.8 us
    pallas_call x1, Pallas kernels, move_out(): pl.pallas_call(move_kernel, out_shape=tuple((jax.ShapeDtypeStruct(a.shape...  3.49 us

profile of v5, /device:TPU:1, one launch (start us, length us, event | category | flops | bytes accessed | tf_op | source)
XLA Modules:
  0.0 88.9 jit_solution(4703704424618412187)
XLA Ops:
  0.6 84.8 %shard_map.110 = (f32[9,256,128]{2,1,0:T(8,128)}, f32[1,128]{1,0:T(1,128)}, f32[1,128]{1,0:T(1,128)}, f32[4,128]{1,0:T(4,128)}, f32[4,4,128,256]{3,2,1,0:T(8,128)}) custom-call(bf16[4,4,128,256]{3,2,1,0:T(8,128)(2,1)} %feat.1, bf16[2304,512]{1,0:T(8,128)(2,1)} %bitcast.8, f32[1,512]{1,0:T(1,128)} %bitcast.11, f32[1,512]{1,0:T(1,128)} %bitcast.12, ...), custom_call_target="tpu_custom_call" | custom-call | flops 15000000512 | bytes 8000000 | tf_op jit(solution)/shard_map/pallas_call | solution.py:874
  85.4 3.5 %shard_map.111 = (f32[9,256,128]{2,1,0:T(8,128)}, f32[1,128]{1,0:T(1,128)}, f32[1,128]{1,0:T(1,128)}, f32[4,128]{1,0:T(4,128)}, f32[4,4,128,256]{3,2,1,0:T(8,128)}) custom-call(f32[9,256,128]{2,1,0:T(8,128)} %get-tuple-element.15.refs_0_, f32[1,128]{1,0:T(1,128)} %get-tuple-element.16.refs_1_, f32[1,128]{1,0:T(1,128)} %get-tuple-element.17.refs_2_, ...), custom_call_target="tpu_custom_call" | custom-call | tf_op jit(solution)/shard_map/pallas_call | solution.py:859

commit v6 on v4

--- a/solution.py
+++ b/solution.py
@@ -60,9 +60,11 @@
     gedge_in,
     st_local,
     st8,
-    st16,
+    sty,
+    stx,
     tot8,
-    tot16,
+    toty,
+    totx,
     hd2,
     hdz_send,
     hdz,
@@ -131,9 +133,6 @@
     def dev8(k):
         return (flip(me, k % 2), flip(z, k // 2))
 
-    def dev16(k):
-        return (flip(me, 2 * k), z)
-
     def on_axis(axis, k):
         return (me, flip(z, k)) if axis == "z" else (flip(me, (2 if axis == "y" else 8) * k), z)
 
@@ -153,8 +152,9 @@
         greet(dev8(k))
     for col in (west, z, east):
         greet((beyond, col))
-    for k in range(1, 16):
-        greet(dev16(k))
+    for k in range(1, 4):
+        greet(on_axis("y", k))
+        greet(on_axis("x", k))
 
     wcopies = []
     for t in range(TAPS):
@@ -176,7 +176,7 @@
     xedge_out[0] = right_edge.astype(BF16)
     xedge_out[1] = left_edge.astype(BF16)
 
-    pl.semaphore_wait(barrier, 25)
+    pl.semaphore_wait(barrier, 16)
 
     def remote(src, dst, ssem, rsem, device):
         return pltpu.make_async_remote_copy(
@@ -375,9 +375,11 @@
         return along(axis, lambda j: land.at[coords[axis]], land, ssem, rsem)
 
     st8_x = share(8, dev8, st8, rank8, st_s.at[0], st_r.at[0])
-    st16_x = share(16, dev16, st16, chip, st_s.at[1], st_r.at[1])
-    tot8_x = share(8, dev8, tot8, rank8, st_s.at[2], st_r.at[2])
-    tot16_x = share(16, dev16, tot16, chip, st_s.at[3], st_r.at[3])
+    sty_x = share_along("y", sty, st_s.at[1], st_r.at[1])
+    stx_x = share_along("x", stx, st_s.at[2], st_r.at[2])
+    tot8_x = share(8, dev8, tot8, rank8, st_s.at[3], st_r.at[3])
+    toty_x = share_along("y", toty, st_s.at[4], st_r.at[4])
+    totx_x = share_along("x", totx, st_s.at[5], st_r.at[5])
     hd2_copy = remote(hd2.at[core], hd2.at[core], hd_s.at[0], hd_r.at[0], other)
     hdz_x = along("z", lambda j: hdz_send.at[j], hdz, hd_s.at[1], hd_r.at[1])
     hdy_x = share_along("y", hdy, hd_s.at[2], hd_r.at[2])
@@ -410,13 +412,19 @@
     lax.fori_loop(0, 1, cross_conv, 0)
     st8_x[1]()
     mid, m2 = combine([st8[j] for j in range(8)], float(B * PIX))
-    st16[chip, 0:1] = mid
-    st16[chip, 1:2] = m2
-    st16_x[0]()
-    lax.fori_loop(1, 3, cross_conv, 0)
+    sty[y, 0:1] = mid
+    sty[y, 1:2] = m2
+    sty_x[0]()
+    lax.fori_loop(1, 2, cross_conv, 0)
+    sty_x[1]()
+    mid, m2 = combine([sty[j] for j in range(4)], float(8 * B * PIX))
+    stx[x, 0:1] = mid
+    stx[x, 1:2] = m2
+    stx_x[0]()
+    lax.fori_loop(2, 3, cross_conv, 0)
     transpose_w(TAPS - 1)
-    st16_x[1]()
-    mean, m2 = combine([st16[j] for j in range(16)], float(8 * B * PIX))
+    stx_x[1]()
+    mean, m2 = combine([stx[j] for j in range(4)], float(32 * B * PIX))
     rstd = lax.rsqrt(m2 * (1.0 / COUNT) + EPS)
     gain = gain_ref[...]
     bias = bias_ref[...]
@@ -470,18 +478,23 @@
 
     lax.fori_loop(0, 1, cross_grad, 0)
     tot8_x[1]()
-    tot16[chip] = add_up(tot8, 8)
-    tot16_x[0]()
-    lax.fori_loop(1, 3, cross_grad, 0)
+    toty[y] = add_up(tot8, 8)
+    toty_x[0]()
+    lax.fori_loop(1, 2, cross_grad, 0)
+    toty_x[1]()
+    totx[x] = add_up(toty, 4)
+    totx_x[0]()
+    lax.fori_loop(2, 3, cross_grad, 0)
     head_sum = lax.fori_loop(0, B, head_part, jnp.zeros((128, CO), F32))
     hd2[core] = head_sum[0:4, :]
     hd2_copy.start()
     st8_x[2]()
-    st16_x[2]()
+    sty_x[2]()
+    stx_x[2]()
     for copy in xrow_copies + xedge_copies:
         copy.wait_send()
-    tot16_x[1]()
-    totals = add_up(tot16, 16)
+    totx_x[1]()
+    totals = add_up(totx, 4)
     off = totals[0:1] * (1.0 / COUNT)
     slope = rstd * totals[1:2] * (1.0 / COUNT)
     st_local[0] = totals
@@ -782,7 +795,7 @@
 
     for copy in [hd2_copy] + grow_copies + gedge_copies + a_copies:
         copy.wait_send()
-    for exchanged in [tot8_x, tot16_x, hdz_x, hdy_x, hdx_x] + second + third + gather3 + gather2:
+    for exchanged in [tot8_x, toty_x, totx_x, hdz_x, hdy_x, hdx_x] + second + third + gather3 + gather2:
         exchanged[2]()
     for r in range(3):
         for copy in ring1_copies(r) + ring2_copies(r):
@@ -871,9 +884,11 @@
             vmem((6, 16, CO), BF16),
             vmem((B, 2, CO), F32),
             vmem((8, 2, CO), F32),
-            vmem((16, 2, CO), F32),
+            vmem((4, 2, CO), F32),
+            vmem((4, 2, CO), F32),
             vmem((8, 2, CO), F32),
-            vmem((16, 2, CO), F32),
+            vmem((4, 2, CO), F32),
+            vmem((4, 2, CO), F32),
             vmem((2, 4, CO), F32),
             vmem((4, 4, 128), F32),
             vmem((4, 4, 128), F32),
@@ -914,7 +929,8 @@
             dma((6,)),
             dma((6,)),
         ]
-        + [dma((4,))] * 4
+        + [dma((6,))] * 2
+        + [dma((4,))] * 2
         + [
             dma((3,)),
             dma((3,)),

time: 87 us -> 89.5 us (1.029)
  Pallas kernels: 86.1 us -> 88.6 us
    pallas_call x1, Pallas kernels: 82.6 us -> 85.1 us  [per_device(): pl.pallas_call(kernel, out_shape=(jax.ShapeDtypeStruct((TAPS, CI, 128), F...]
where the time goes in v6:
time: 89.5 us; the launch traced here: 89.4 us
  Pallas kernels  88.6 us (99%)
    pallas_call x1, Pallas kernels, per_device(): pl.pallas_call(kernel, out_shape=(jax.ShapeDtypeStruct((TAPS, CI, 128), F...  85.1 us
    pallas_call x1, Pallas kernels, move_out(): pl.pallas_call(move_kernel, out_shape=tuple((jax.ShapeDtypeStruct(a.shape...  3.49 us

profile of v6, /device:TPU:1, one launch (start us, length us, event | category | flops | bytes accessed | tf_op | source)
XLA Modules:
  0.0 89.4 jit_solution(8653443882635576528)
XLA Ops:
  0.6 85.1 %shard_map.110 = (f32[9,256,128]{2,1,0:T(8,128)}, f32[1,128]{1,0:T(1,128)}, f32[1,128]{1,0:T(1,128)}, f32[4,128]{1,0:T(4,128)}, f32[4,4,128,256]{3,2,1,0:T(8,128)}) custom-call(bf16[4,4,128,256]{3,2,1,0:T(8,128)(2,1)} %feat.1, bf16[2304,512]{1,0:T(8,128)(2,1)} %bitcast.8, f32[1,512]{1,0:T(1,128)} %bitcast.11, f32[1,512]{1,0:T(1,128)} %bitcast.12, ...), custom_call_target="tpu_custom_call" | custom-call | flops 15000000512 | bytes 8000000 | tf_op jit(solution)/shard_map/pallas_call | solution.py:848
  85.7 3.5 %shard_map.111 = (f32[9,256,128]{2,1,0:T(8,128)}, f32[1,128]{1,0:T(1,128)}, f32[1,128]{1,0:T(1,128)}, f32[4,128]{1,0:T(4,128)}, f32[4,4,128,256]{3,2,1,0:T(8,128)}) custom-call(f32[9,256,128]{2,1,0:T(8,128)} %get-tuple-element.15.refs_0_, f32[1,128]{1,0:T(1,128)} %get-tuple-element.16.refs_1_, f32[1,128]{1,0:T(1,128)} %get-tuple-element.17.refs_2_, ...), custom_call_target="tpu_custom_call" | custom-call | tf_op jit(solution)/shard_map/pallas_call | solution.py:833

commit v7 on v4

--- a/solution.py
+++ b/solution.py
@@ -32,9 +32,9 @@
     gg_out,
     gb_out,
     gh_out,
-    gi_out,
+    gc,
+    edges_to,
     wgt,
-    wgt_t,
     xl,
     xc,
     xr,
@@ -48,9 +48,6 @@
     head_pad,
     head_tile,
     head_t,
-    gl,
-    gc,
-    gr,
     xrow,
     xedge_out,
     xedge_in,
@@ -114,7 +111,6 @@
     dir_r,
     o_s,
     o_r,
-    gi_sem,
 ):
     me = lax.axis_index("rows")
     z = lax.axis_index("cols")
@@ -306,11 +302,6 @@
         for c, ref in enumerate((xl, xc, xr)):
             xt[line, c * CI : (c + 1) * CI, :] = jnp.transpose(ref[line].reshape(PIX, CI))
 
-    def transpose_w(t):
-        wgt_t[pl.ds(pl.multiple_of(t * CO, CO), CO), :] = jnp.transpose(
-            wgt[pl.ds(pl.multiple_of((TAPS - 1 - t) * CI, CI), CI), :]
-        )
-
     def inner_rows(i, carry):
         value = conv_rows(1 + i, 0, 3)
         conv[1 + i] = value
@@ -323,8 +314,6 @@
 
     def outer_rows(i, carry):
         conv[3 * i] = conv_rows(3 * i, 1 - i, 2)
-        for t in range(4):
-            transpose_w(4 * i + t)
         return carry
 
     lax.fori_loop(0, 2, outer_rows, 0)
@@ -414,7 +403,6 @@
     st16[chip, 1:2] = m2
     st16_x[0]()
     lax.fori_loop(1, 3, cross_conv, 0)
-    transpose_w(TAPS - 1)
     st16_x[1]()
     mean, m2 = combine([st16[j] for j in range(16)], float(8 * B * PIX))
     rstd = lax.rsqrt(m2 * (1.0 / COUNT) + EPS)
@@ -518,7 +506,6 @@
         away = conv[h, spot] - mean
         value = scale * (pgs[h, spot] - off - away * slope)
         gc[h + 1, b] = value.astype(BF16)
-        gl[h + 1, b], gr[h + 1, b] = shifted(value, 0.0, 0.0)
         gedge_f[0, pl.ds(h * B + b, 1)] = value[W - 1 : W, :]
         gedge_f[1, pl.ds(h * B + b, 1)] = value[0:1, :]
         return carry
@@ -685,42 +672,6 @@
         o_copies[r].wait_recv()
         unpack(r, gat_other, 1 - core)
 
-    gi_copies = [
-        [
-            pltpu.make_async_copy(
-                pgs.at[h, pl.ds(b * W, W), pl.ds(0, CI)], gi_out.at[b, h], gi_sem.at[h, b]
-            )
-            for b in range(B)
-        ]
-        for h in range(H)
-    ]
-
-    def back(h):
-        lhs = jnp.concatenate(
-            [
-                ref[h + r].reshape(PIX, CO)
-                for r in range(3)
-                for ref in (gl, gc, gr)
-            ],
-            axis=1,
-        )
-        value = jnp.dot(lhs, wgt_t[...], preferred_element_type=F32)
-        pgs[h, :, 0:CI] = value
-        for copy in gi_copies[h]:
-            copy.start()
-
-    def set_edges(i, carry):
-        h = i // B
-        b = lax.rem(i, B)
-        ids = lax.broadcasted_iota(jnp.int32, (16, CO), 0)
-        low = pick_row(gedge_in, 1, i) * west_ok
-        top = pick_row(gedge_in, 4, i) * east_ok
-        block16 = gl[h + 1, b, 0:16].astype(F32)
-        gl[h + 1, b, 0:16] = jnp.where(ids == 0, low, block16).astype(BF16)
-        block16 = gr[h + 1, b, W - 16 : W].astype(F32)
-        gr[h + 1, b, W - 16 : W] = jnp.where(ids == 15, top, block16).astype(BF16)
-        return carry
-
     lax.fori_loop(0, 2 * B, conv_grad, 0)
     grow_copies = row_sends(gc.at[1], gc.at[H], grow, grow_s, grow_r)
     for copy in grow_copies:
@@ -741,39 +692,36 @@
     ring2(0)
     ring2(1)
     ring2(2)
-    for copy in gedge_copies:
-        copy.wait_recv()
-    lax.fori_loop(0, B * H, set_edges, 0)
     hdz_x[1]()
     head_line = hdz_send[z]
     for k in range(1, 4):
         head_line = head_line + hdz[flip(z, k)]
     hdy[y] = head_line
     hdy_x[0]()
-    back(1)
     stage2(0)
     stage2(1)
     stage2(2)
+    for copy in gedge_copies:
+        copy.wait_recv()
+    edges_to[...] = gedge_in[...]
     hdy_x[1]()
     hdx[x] = add_up(hdy, 4)
     hdx_x[0]()
-    back(2)
     stage3(0)
     stage3(1)
     stage3(2)
     for copy in grow_copies:
         copy.wait_recv()
-    build_halo(grow, gedge_in, gl, gc, gr)
-    hdx_x[1]()
-    gh_out[...] = add_up(hdx, 4)
+    gc[0] = (grow[0].astype(F32) * up_ok).astype(BF16)
+    gc[H + 1] = (grow[1].astype(F32) * down_ok).astype(BF16)
     collect3(0)
     collect3(1)
     collect3(2)
-    back(0)
+    hdx_x[1]()
+    gh_out[...] = add_up(hdx, 4)
     collect2(0)
     collect2(1)
     collect2(2)
-    back(3)
     swap(0)
     swap(1)
     swap(2)
@@ -787,45 +735,105 @@
     for r in range(3):
         for copy in ring1_copies(r) + ring2_copies(r):
             copy.wait_send()
-    for line in gi_copies:
-        for copy in line:
-            copy.wait()
     unpack_other(2)
     for copy in o_copies:
         copy.wait_send()
 
 
-def move_kernel(*refs):
-    count = (len(refs) - 2) // 3
-    in_sem, out_sem = refs[-2:]
-    arrivals, leaves = [], []
-    for src, dst, held in zip(refs[:count], refs[count : 2 * count], refs[2 * count : 3 * count]):
-        size = src.shape[0] if len(src.shape) > 2 else 1
-        for i in range(size):
-            here, there, hold = (src.at[i], dst.at[i], held.at[i]) if size > 1 else (src, dst, held)
-            slot = len(arrivals)
-            arrivals.append(pltpu.make_async_copy(here, hold, in_sem.at[slot]))
-            leaves.append(pltpu.make_async_copy(hold, there, out_sem.at[slot]))
+def back_kernel(gc, edges, wgt, *refs):
+    small_in, small_out, gi_out = refs[0:4], refs[4:8], refs[8]
+    held = refs[9:13]
+    gl, gr, wgt_t, gi_buf, in_sem, out_sem, gi_sem = refs[13:]
+    me = lax.axis_index("rows")
+    z = lax.axis_index("cols")
+    west_ok = jnp.where(z > 0, 1.0, 0.0).astype(F32)
+    east_ok = jnp.where(z < 3, 1.0, 0.0).astype(F32)
+    up_ok = jnp.where(me > 0, 1.0, 0.0).astype(F32)
+    down_ok = jnp.where(me < 31, 1.0, 0.0).astype(F32)
+    arrivals = [pltpu.make_async_copy(a, b, in_sem.at[i]) for i, (a, b) in enumerate(zip(small_in, held))]
+    leaves = [pltpu.make_async_copy(a, b, out_sem.at[i]) for i, (a, b) in enumerate(zip(held, small_out))]
     for copy in arrivals:
         copy.start()
+
+    def transpose_w(t, carry):
+        wgt_t[pl.ds(pl.multiple_of(t * CO, CO), CO), :] = jnp.transpose(
+            wgt[pl.ds(pl.multiple_of((TAPS - 1 - t) * CI, CI), CI), :]
+        )
+        return carry
+
+    lax.fori_loop(0, TAPS, transpose_w, 0)
     for arrival, leave in zip(arrivals, leaves):
         arrival.wait()
         leave.start()
+
+    def pick_row(slot, index):
+        block = edges[slot].astype(F32)
+        ids = lax.broadcasted_iota(jnp.int32, block.shape, 0)
+        return jnp.sum(jnp.where(ids == index, block, 0.0), axis=0, keepdims=True)
+
+    def build(line, b, slot, index, ok):
+        value = gc[line, b].astype(F32)
+        ids = lax.broadcasted_iota(jnp.int32, value.shape, 0)
+        before = pick_row(slot, index) * (west_ok * ok)
+        after = pick_row(slot + 3, index) * (east_ok * ok)
+        left = jnp.where(ids == 0, before, pltpu.roll(value, 1, 0))
+        right = jnp.where(ids == W - 1, after, pltpu.roll(value, W - 1, 0))
+        gl[line, b] = left.astype(BF16)
+        gr[line, b] = right.astype(BF16)
+
+    def build_inner(i, carry):
+        build(1 + i // B, lax.rem(i, B), 1, i, 1.0)
+        return carry
+
+    def build_outer(b, carry):
+        build(0, b, 0, (H - 1) * B + b, up_ok)
+        build(H + 1, b, 2, b, down_ok)
+        return carry
+
+    lax.fori_loop(0, B * H, build_inner, 0)
+    lax.fori_loop(0, B, build_outer, 0)
+
+    def gi_copy(h):
+        return pltpu.make_async_copy(gi_buf.at[h], gi_out.at[:, h], gi_sem.at[h])
+
+    def back(h, carry):
+        lhs = jnp.concatenate(
+            [ref[h + r].reshape(PIX, CO) for r in range(3) for ref in (gl, gc, gr)], axis=1
+        )
+        value = jnp.dot(lhs, wgt_t[...], preferred_element_type=F32)
+        gi_buf[h] = value.reshape(B, W, CI)
+        gi_copy(h).start()
+        return carry
+
+    lax.fori_loop(0, H, back, 0)
     for leave in leaves:
         leave.wait()
-
-
-def move_out(arrays):
+    for h in range(H):
+        gi_copy(h).wait()
+
+
+def back_convolution(grad, edges, weights, arrays):
     anywhere = pl.BlockSpec(memory_space=pl.ANY)
+    whole = pl.BlockSpec(memory_space=pltpu.VMEM)
+    dma = pltpu.SemaphoreType.DMA
     return pl.pallas_call(
-        move_kernel,
-        out_shape=tuple(jax.ShapeDtypeStruct(a.shape, a.dtype) for a in arrays),
-        in_specs=[anywhere] * len(arrays),
-        out_specs=(anywhere,) * len(arrays),
+        back_kernel,
+        out_shape=tuple(jax.ShapeDtypeStruct(a.shape, a.dtype) for a in arrays)
+        + (jax.ShapeDtypeStruct((B, H, W, CI), F32),),
+        in_specs=[whole] * 3 + [anywhere] * 4,
+        out_specs=(anywhere,) * 5,
         scratch_shapes=[pltpu.VMEM(a.shape, a.dtype) for a in arrays]
-        + [pltpu.SemaphoreType.DMA((16,)), pltpu.SemaphoreType.DMA((16,))],
+        + [
+            pltpu.VMEM((H + 2, B, W, CO), BF16),
+            pltpu.VMEM((H + 2, B, W, CO), BF16),
+            pltpu.VMEM((TAPS * CO, CI), BF16),
+            pltpu.VMEM((H, B, W, CI), F32),
+            dma((4,)),
+            dma((4,)),
+            dma((H,)),
+        ],
         compiler_params=pltpu.CompilerParams(vmem_limit_bytes=60 * 1024 * 1024),
-    )(*arrays)
+    )(grad, edges, weights, *arrays)
 
 
 def per_device(features, conv_weight, bn_gain, bn_bias, head_weight, labels, raster):
@@ -839,13 +847,13 @@
             jax.ShapeDtypeStruct((1, 128), F32),
             jax.ShapeDtypeStruct((1, 128), F32),
             jax.ShapeDtypeStruct((4, 128), F32),
-            jax.ShapeDtypeStruct((B, H, W, CI), F32),
+            jax.ShapeDtypeStruct((H + 2, B, W, CO), BF16),
+            jax.ShapeDtypeStruct((6, 16, CO), BF16),
         ),
         in_specs=[whole, pl.BlockSpec(memory_space=pl.ANY)] + [whole] * 5,
-        out_specs=(whole,) * 4 + (pl.BlockSpec(memory_space=pl.ANY),),
+        out_specs=(whole,) * 6,
         scratch_shapes=[
             vmem((TAPS * CI, CO), BF16),
-            vmem((TAPS * CO, CI), BF16),
             vmem((H + 2, B, W, CI), BF16),
             vmem((H + 2, B, W, CI), BF16),
             vmem((H + 2, B, W, CI), BF16),
@@ -859,9 +867,6 @@
             vmem((128, CO), F32),
             vmem((CO, 128), BF16),
             vmem((128, CO), BF16),
-            vmem((H + 2, B, W, CO), BF16),
-            vmem((H + 2, B, W, CO), BF16),
-            vmem((H + 2, B, W, CO), BF16),
             vmem((2, B, W, CI), BF16),
             vmem((2, 16, CI), BF16),
             vmem((6, 16, CI), BF16),
@@ -924,7 +929,6 @@
             dma((4, 3)),
             dma((3,)),
             dma((3,)),
-            dma((H, B)),
         ],
         compiler_params=pltpu.CompilerParams(
             collective_id=0, has_side_effects=True, vmem_limit_bytes=60 * 1024 * 1024
@@ -941,7 +945,9 @@
         labels,
         raster,
     )
-    grad_weight, grad_gain, grad_bias, grad_head, grad_input = move_out(outs)
+    grad_weight, grad_gain, grad_bias, grad_head, grad_input = back_convolution(
+        outs[4], outs[5], conv_weight.reshape(TAPS * CI, CO), outs[:4]
+    )
     return (
         grad_weight.reshape(3, 3, CI, 128),
         grad_gain.reshape(128),

time: 87 us -> 95.3 us (1.095)
  Pallas kernels: 86.1 us -> 94.5 us
    pallas_call x1, Pallas kernels: 3.49 us -> 12.3 us  [back_convolution(): pl.pallas_call(back_kernel, out_shape=tuple((jax.ShapeDtypeStruct(a.shape...]
where the time goes in v7:
time: 95.3 us; the launch traced here: 95.1 us
  Pallas kernels  94.5 us (99%)
    pallas_call x1, Pallas kernels, per_device(): pl.pallas_call(kernel, out_shape=(jax.ShapeDtypeStruct((TAPS, CI, 128), F...  82.2 us
    pallas_call x1, Pallas kernels, back_convolution(): pl.pallas_call(back_kernel, out_shape=tuple((jax.ShapeDtypeStruct(a.shape...  12.3 us

profile of v7, /device:TPU:1, one launch (start us, length us, event | category | flops | bytes accessed | tf_op | source)
XLA Modules:
  0.0 95.1 jit_solution(17181184015415730151)
XLA Ops:
  0.6 82.2 %shard_map.110 = (f32[9,256,128]{2,1,0:T(8,128)}, f32[1,128]{1,0:T(1,128)}, f32[1,128]{1,0:T(1,128)}, f32[4,128]{1,0:T(4,128)}, bf16[6,4,128,512]{3,2,1,0:T(8,128)(2,1)}, /*index=5*/bf16[6,16,512]{2,1,0:T(8,128)(2,1)}) custom-call(bf16[4,4,128,256]{3,2,1,0:T(8,128)(2,1)} %feat.1, bf16[2304,512]{1,0:T(8,128)(2,1)} %bitcast.8, f32[1,512]{1,0:T(1,128)} %bitcast.12, ...), custom_call_target="tpu_custom_call" | custom-call | flops 15000000512 | bytes 8000000 | tf_op jit(solution)/shard_map/pallas_call | solution.py:843
  82.8 12.3 %shard_map.111 = (f32[9,256,128]{2,1,0:T(8,128)}, f32[1,128]{1,0:T(1,128)}, f32[1,128]{1,0:T(1,128)}, f32[4,128]{1,0:T(4,128)}, f32[4,4,128,256]{3,2,1,0:T(8,128)}) custom-call(bf16[6,4,128,512]{3,2,1,0:T(8,128)(2,1)} %get-tuple-element.16.gc, bf16[6,16,512]{2,1,0:T(8,128)(2,1)} %get-tuple-element.17.edges, bf16[2304,512]{1,0:T(8,128)(2,1)} %bitcast.9, ...), custom_call_target="tpu_custom_call" | custom-call | tf_op jit(solution)/shard_map/pallas_call | solution.py:819

commit v8 on v4

--- a/solution.py
+++ b/solution.py
@@ -34,7 +34,7 @@
     gh_out,
     gi_out,
     wgt,
-    wgt_t,
+    identity,
     xl,
     xc,
     xr,
@@ -220,15 +220,35 @@
     head_tile[...] = jnp.transpose(jnp.concatenate([head_pad[0:8]] * 16, axis=0)).astype(BF16)
 
     lane_class = lax.rem(lax.broadcasted_iota(jnp.int32, (W, 128), 1), 4).astype(F32)
-    for b in range(B):
-        for h in range(H):
-            label = labels_ref[b, h : h + 1, :].astype(F32)
-            weight = raster_ref[b, h : h + 1, :].astype(F32)
-            label_t = jnp.transpose(jnp.broadcast_to(label, (128, W)))
-            weight_t = jnp.transpose(jnp.broadcast_to(weight, (128, W)))
-            marks = jnp.where(label_t == lane_class, 1.0, 0.0)
-            onehot[h, b * W : (b + 1) * W] = marks.astype(BF16)
-            pixw[h, b * W : (b + 1) * W] = ((1.0 + weight_t) * 0.25).astype(BF16)
+    identity[...] = jnp.where(
+        lax.broadcasted_iota(jnp.int32, (256, 256), 0)
+        == lax.broadcasted_iota(jnp.int32, (256, 256), 1),
+        1.0,
+        0.0,
+    ).astype(BF16)
+
+    def turned(value):
+        size = value.shape[1]
+        return lax.dot_general(
+            identity[0:size, 0:size],
+            value,
+            (((1,), (1,)), ((), ())),
+            preferred_element_type=F32,
+        )
+
+    def class_marks(i, carry):
+        b = i // H
+        h = lax.rem(i, H)
+        spot = pl.ds(pl.multiple_of(b * W, W), W)
+        code = labels_ref[b, pl.ds(h, 1), :] + 4 * raster_ref[b, pl.ds(h, 1), :]
+        code = turned(jnp.broadcast_to(code.astype(F32), (128, W)).astype(BF16))
+        weight = jnp.where(code > 3.5, 1.0, 0.0)
+        marks = jnp.where(code - 4.0 * weight == lane_class, 1.0, 0.0)
+        onehot[h, spot] = marks.astype(BF16)
+        pixw[h, spot] = ((1.0 + weight) * 0.25).astype(BF16)
+        return carry
+
+    lax.fori_loop(0, B * H, class_marks, 0)
 
     west_ok = jnp.where(z > 0, 1.0, 0.0).astype(F32)
     east_ok = jnp.where(z < 3, 1.0, 0.0).astype(F32)
@@ -304,12 +324,7 @@
 
     def transpose_x(line):
         for c, ref in enumerate((xl, xc, xr)):
-            xt[line, c * CI : (c + 1) * CI, :] = jnp.transpose(ref[line].reshape(PIX, CI))
-
-    def transpose_w(t):
-        wgt_t[pl.ds(pl.multiple_of(t * CO, CO), CO), :] = jnp.transpose(
-            wgt[pl.ds(pl.multiple_of((TAPS - 1 - t) * CI, CI), CI), :]
-        )
+            xt[line, c * CI : (c + 1) * CI, :] = turned(ref[line].reshape(PIX, CI)).astype(BF16)
 
     def inner_rows(i, carry):
         value = conv_rows(1 + i, 0, 3)
@@ -323,8 +338,6 @@
 
     def outer_rows(i, carry):
         conv[3 * i] = conv_rows(3 * i, 1 - i, 2)
-        for t in range(4):
-            transpose_w(4 * i + t)
         return carry
 
     lax.fori_loop(0, 2, outer_rows, 0)
@@ -414,7 +427,6 @@
     st16[chip, 1:2] = m2
     st16_x[0]()
     lax.fori_loop(1, 3, cross_conv, 0)
-    transpose_w(TAPS - 1)
     st16_x[1]()
     mean, m2 = combine([st16[j] for j in range(16)], float(8 * B * PIX))
     rstd = lax.rsqrt(m2 * (1.0 / COUNT) + EPS)
@@ -704,7 +716,12 @@
             ],
             axis=1,
         )
-        value = jnp.dot(lhs, wgt_t[...], preferred_element_type=F32)
+        flipped = jnp.concatenate(
+            [wgt[(TAPS - 1 - t) * CI : (TAPS - t) * CI, :] for t in range(TAPS)], axis=1
+        )
+        value = lax.dot_general(
+            lhs, flipped, (((1,), (1,)), ((), ())), preferred_element_type=F32
+        )
         pgs[h, :, 0:CI] = value
         for copy in gi_copies[h]:
             copy.start()
@@ -845,7 +862,7 @@
         out_specs=(whole,) * 4 + (pl.BlockSpec(memory_space=pl.ANY),),
         scratch_shapes=[
             vmem((TAPS * CI, CO), BF16),
-            vmem((TAPS * CO, CI), BF16),
+            vmem((256, 256), BF16),
             vmem((H + 2, B, W, CI), BF16),
             vmem((H + 2, B, W, CI), BF16),
             vmem((H + 2, B, W, CI), BF16),

time: 87 us -> 87.4 us (level)
  no operation moved by 1% of the time
where the time goes in v8:
time: 87.4 us; the launch traced here: 87.3 us
  Pallas kernels  86.5 us (99%)
    pallas_call x1, Pallas kernels, per_device(): pl.pallas_call(kernel, out_shape=(jax.ShapeDtypeStruct((TAPS, CI, 128), F...  83 us
    pallas_call x1, Pallas kernels, move_out(): pl.pallas_call(move_kernel, out_shape=tuple((jax.ShapeDtypeStruct(a.shape...  3.49 us

profile of v8, /device:TPU:1, one launch (start us, length us, event | category | flops | bytes accessed | tf_op | source)
XLA Modules:
  0.0 87.3 jit_solution(16018298541927685771)
XLA Ops:
  0.6 83.0 %shard_map.110 = (f32[9,256,128]{2,1,0:T(8,128)}, f32[1,128]{1,0:T(1,128)}, f32[1,128]{1,0:T(1,128)}, f32[4,128]{1,0:T(4,128)}, f32[4,4,128,256]{3,2,1,0:T(8,128)}) custom-call(bf16[4,4,128,256]{3,2,1,0:T(8,128)(2,1)} %feat.1, bf16[2304,512]{1,0:T(8,128)(2,1)} %bitcast.8, f32[1,512]{1,0:T(1,128)} %bitcast.11, f32[1,512]{1,0:T(1,128)} %bitcast.12, ...), custom_call_target="tpu_custom_call" | custom-call | flops 15000000512 | bytes 8000000 | tf_op jit(solution)/shard_map/pallas_call | solution.py:852
  83.6 3.5 %shard_map.111 = (f32[9,256,128]{2,1,0:T(8,128)}, f32[1,128]{1,0:T(1,128)}, f32[1,128]{1,0:T(1,128)}, f32[4,128]{1,0:T(4,128)}, f32[4,4,128,256]{3,2,1,0:T(8,128)}) custom-call(f32[9,256,128]{2,1,0:T(8,128)} %get-tuple-element.15.refs_0_, f32[1,128]{1,0:T(1,128)} %get-tuple-element.16.refs_1_, f32[1,128]{1,0:T(1,128)} %get-tuple-element.17.refs_2_, ...), custom_call_target="tpu_custom_call" | custom-call | tf_op jit(solution)/shard_map/pallas_call | solution.py:837

commit v9 on v8

--- a/solution.py
+++ b/solution.py
@@ -35,6 +35,9 @@
     gi_out,
     wgt,
     identity,
+    line_one,
+    edge_f,
+    edge_part,
     xl,
     xc,
     xr,
@@ -176,6 +179,28 @@
     xedge_out[0] = right_edge.astype(BF16)
     xedge_out[1] = left_edge.astype(BF16)
 
+    def pick_row(ref, slot, index):
+        block = ref[slot].astype(F32)
+        ids = lax.broadcasted_iota(jnp.int32, block.shape, 0)
+        return jnp.sum(jnp.where(ids == index, block, 0.0), axis=0, keepdims=True)
+
+    def shifted(value, before, after):
+        ids = lax.broadcasted_iota(jnp.int32, value.shape, 0)
+        left = jnp.where(ids == 0, before, pltpu.roll(value, 1, 0))
+        right = jnp.where(ids == W - 1, after, pltpu.roll(value, W - 1, 0))
+        return left.astype(BF16), right.astype(BF16)
+
+    def build_x(i, carry):
+        b = i // H
+        h = lax.rem(i, H)
+        left, right = shifted(feat[b, h].astype(F32), 0.0, 0.0)
+        xl[h + 1, b] = left
+        xc[h + 1, b] = feat[b, h]
+        xr[h + 1, b] = right
+        return carry
+
+    lax.fori_loop(0, B * H, build_x, 0)
+
     pl.semaphore_wait(barrier, 25)
 
     def remote(src, dst, ssem, rsem, device):
@@ -254,36 +279,6 @@
     east_ok = jnp.where(z < 3, 1.0, 0.0).astype(F32)
     up_ok = jnp.where(me > 0, 1.0, 0.0).astype(F32)
     down_ok = jnp.where(me < 31, 1.0, 0.0).astype(F32)
-
-    def pick_row(ref, slot, index):
-        block = ref[slot].astype(F32)
-        ids = lax.broadcasted_iota(jnp.int32, block.shape, 0)
-        return jnp.sum(jnp.where(ids == index, block, 0.0), axis=0, keepdims=True)
-
-    def shifted(value, before, after):
-        ids = lax.broadcasted_iota(jnp.int32, value.shape, 0)
-        left = jnp.where(ids == 0, before, pltpu.roll(value, 1, 0))
-        right = jnp.where(ids == W - 1, after, pltpu.roll(value, W - 1, 0))
-        return left.astype(BF16), right.astype(BF16)
-
-    for copy in xedge_copies:
-        copy.wait_recv()
-
-    def build_x(i, carry):
-        h = i // B
-        b = lax.rem(i, B)
-        value = feat[b, h].astype(F32)
-        left, right = shifted(
-            value,
-            pick_row(xedge_in, 1, i) * west_ok,
-            pick_row(xedge_in, 4, i) * east_ok,
-        )
-        xl[h + 1, b] = left
-        xc[h + 1, b] = feat[b, h]
-        xr[h + 1, b] = right
-        return carry
-
-    lax.fori_loop(0, B * H, build_x, 0)
 
     def build_halo(land, edge_in, left_ref, mid_ref, right_ref):
         def body(b, carry):
@@ -317,21 +312,37 @@
         start = pl.multiple_of(first * 3 * CI, 3 * CI)
         return jnp.dot(lhs, wgt[pl.ds(start, count * 3 * CI), :], preferred_element_type=F32)
 
-    def statistics(h, value):
+    def statistics(h, carry):
+        value = conv[h]
         mid = jnp.sum(value, axis=0, keepdims=True) * (1.0 / PIX)
         st_local[h, 0:1] = mid
         st_local[h, 1:2] = jnp.sum((value - mid) ** 2, axis=0, keepdims=True)
+        return carry
 
     def transpose_x(line):
         for c, ref in enumerate((xl, xc, xr)):
             xt[line, c * CI : (c + 1) * CI, :] = turned(ref[line].reshape(PIX, CI)).astype(BF16)
+        line_one[line] = jnp.dot(
+            xt[line], jnp.ones((PIX, 128), BF16), preferred_element_type=F32
+        )
+
+    def set_edges_of(left_ref, right_ref, edge_in, channels):
+        def body(i, carry):
+            h = i // B
+            b = lax.rem(i, B)
+            ids = lax.broadcasted_iota(jnp.int32, (16, channels), 0)
+            low = pick_row(edge_in, 1, i) * west_ok
+            top = pick_row(edge_in, 4, i) * east_ok
+            block16 = left_ref[h + 1, b, 0:16].astype(F32)
+            left_ref[h + 1, b, 0:16] = jnp.where(ids == 0, low, block16).astype(BF16)
+            block16 = right_ref[h + 1, b, W - 16 : W].astype(F32)
+            right_ref[h + 1, b, W - 16 : W] = jnp.where(ids == 15, top, block16).astype(BF16)
+            return carry
+
+        lax.fori_loop(0, B * H, body, 0)
 
     def inner_rows(i, carry):
-        value = conv_rows(1 + i, 0, 3)
-        conv[1 + i] = value
-        transpose_x(1 + i)
-        transpose_x(3 + i)
-        statistics(1 + i, value)
+        conv[1 + i] = conv_rows(1 + i, 0, 3)
         return carry
 
     lax.fori_loop(0, 2, inner_rows, 0)
@@ -342,17 +353,41 @@
 
     lax.fori_loop(0, 2, outer_rows, 0)
 
+    for copy in xedge_copies:
+        copy.wait_recv()
+    set_edges_of(xl, xr, xedge_in, CI)
+    for side, ok, c, spot in ((0, west_ok, 0, 0), (1, east_ok, 2, W - 1)):
+        edge_f[...] = jnp.zeros((24, CI), F32)
+        edge_f[B : B + 16] = xedge_in[3 * side + 1].astype(F32) * ok
+        lhs = jnp.concatenate([edge_f[B * r : B * r + 16] for r in range(3)], axis=1)
+        taps = jnp.concatenate(
+            [wgt[(3 * r + c) * CI : (3 * r + c + 1) * CI, :] for r in range(3)], axis=0
+        )
+        edge_part[...] = jnp.dot(lhs.astype(BF16), taps, preferred_element_type=F32)
+
+        def add_edges(i, carry, spot=spot):
+            h = i // B
+            place = pl.ds(lax.rem(i, B) * W + spot, 1)
+            conv[h, place] += edge_part[pl.ds(i, 1)]
+            return carry
+
+        lax.fori_loop(0, B * H, add_edges, 0)
+
+    def transpose_inner(line, carry):
+        transpose_x(line)
+        return carry
+
+    lax.fori_loop(1, H + 1, transpose_inner, 0)
     for copy in xrow_copies:
         copy.wait_recv()
     build_halo(xrow, xedge_in, xl, xc, xr)
 
     def halo_rows(i, carry):
-        value = conv[3 * i] + conv_rows(3 * i, 2 * i, 1)
-        conv[3 * i] = value
-        statistics(3 * i, value)
+        conv[3 * i] += conv_rows(3 * i, 2 * i, 1)
         return carry
 
     lax.fori_loop(0, 2, halo_rows, 0)
+    lax.fori_loop(0, H, statistics, 0)
 
     def combine(parts, count):
         total = parts[0][0:1]
@@ -417,7 +452,7 @@
     def cross_conv(r, carry):
         lhs = features_of(r)
         with_conv[r] = jnp.dot(lhs, act[...].reshape(B * PIX, CO), preferred_element_type=F32)
-        with_one[r] = jnp.dot(lhs, jnp.ones((B * PIX, 128), BF16), preferred_element_type=F32)
+        with_one[r] = line_one[r] + line_one[r + 1] + line_one[r + 2] + line_one[r + 3]
         return carry
 
     lax.fori_loop(0, 1, cross_conv, 0)
@@ -725,18 +760,6 @@
         pgs[h, :, 0:CI] = value
         for copy in gi_copies[h]:
             copy.start()
-
-    def set_edges(i, carry):
-        h = i // B
-        b = lax.rem(i, B)
-        ids = lax.broadcasted_iota(jnp.int32, (16, CO), 0)
-        low = pick_row(gedge_in, 1, i) * west_ok
-        top = pick_row(gedge_in, 4, i) * east_ok
-        block16 = gl[h + 1, b, 0:16].astype(F32)
-        gl[h + 1, b, 0:16] = jnp.where(ids == 0, low, block16).astype(BF16)
-        block16 = gr[h + 1, b, W - 16 : W].astype(F32)
-        gr[h + 1, b, W - 16 : W] = jnp.where(ids == 15, top, block16).astype(BF16)
-        return carry
 
     lax.fori_loop(0, 2 * B, conv_grad, 0)
     grow_copies = row_sends(gc.at[1], gc.at[H], grow, grow_s, grow_r)
@@ -760,7 +783,7 @@
     ring2(2)
     for copy in gedge_copies:
         copy.wait_recv()
-    lax.fori_loop(0, B * H, set_edges, 0)
+    set_edges_of(gl, gr, gedge_in, CO)
     hdz_x[1]()
     head_line = hdz_send[z]
     for k in range(1, 4):
@@ -863,6 +886,9 @@
         scratch_shapes=[
             vmem((TAPS * CI, CO), BF16),
             vmem((256, 256), BF16),
+            vmem((H + 2, 3 * CI, 128), F32),
+            vmem((24, CI), F32),
+            vmem((16, CO), F32),
             vmem((H + 2, B, W, CI), BF16),
             vmem((H + 2, B, W, CI), BF16),
             vmem((H + 2, B, W, CI), BF16),

time: 87.4 us -> 84.6 us (0.968)
  Pallas kernels: 86.5 us -> 83.6 us
    pallas_call x1, Pallas kernels: 83 us -> 80.1 us  [per_device(): pl.pallas_call(kernel, out_shape=(jax.ShapeDtypeStruct((TAPS, CI, 128), F...]
where the time goes in v9:
time: 84.6 us; the launch traced here: 84.4 us
  Pallas kernels  83.6 us (99%)
    pallas_call x1, Pallas kernels, per_device(): pl.pallas_call(kernel, out_shape=(jax.ShapeDtypeStruct((TAPS, CI, 128), F...  80.1 us
    pallas_call x1, Pallas kernels, move_out(): pl.pallas_call(move_kernel, out_shape=tuple((jax.ShapeDtypeStruct(a.shape...  3.49 us

profile of v9, /device:TPU:1, one launch (start us, length us, event | category | flops | bytes accessed | tf_op | source)
XLA Modules:
  0.0 84.4 jit_solution(8285705319720447151)
XLA Ops:
  0.6 80.1 %shard_map.110 = (f32[9,256,128]{2,1,0:T(8,128)}, f32[1,128]{1,0:T(1,128)}, f32[1,128]{1,0:T(1,128)}, f32[4,128]{1,0:T(4,128)}, f32[4,4,128,256]{3,2,1,0:T(8,128)}) custom-call(bf16[4,4,128,256]{3,2,1,0:T(8,128)(2,1)} %feat.1, bf16[2304,512]{1,0:T(8,128)(2,1)} %bitcast.8, f32[1,512]{1,0:T(1,128)} %bitcast.11, f32[1,512]{1,0:T(1,128)} %bitcast.12, ...), custom_call_target="tpu_custom_call" | custom-call | flops 15000000512 | bytes 8000000 | tf_op jit(solution)/shard_map/pallas_call | solution.py:875
  80.8 3.5 %shard_map.111 = (f32[9,256,128]{2,1,0:T(8,128)}, f32[1,128]{1,0:T(1,128)}, f32[1,128]{1,0:T(1,128)}, f32[4,128]{1,0:T(4,128)}, f32[4,4,128,256]{3,2,1,0:T(8,128)}) custom-call(f32[9,256,128]{2,1,0:T(8,128)} %get-tuple-element.15.refs_0_, f32[1,128]{1,0:T(1,128)} %get-tuple-element.16.refs_1_, f32[1,128]{1,0:T(1,128)} %get-tuple-element.17.refs_2_, ...), custom_call_target="tpu_custom_call" | custom-call | tf_op jit(solution)/shard_map/pallas_call | solution.py:860

commit v10 on v9

--- a/solution.py
+++ b/solution.py
@@ -762,57 +762,57 @@
             copy.start()
 
     lax.fori_loop(0, 2 * B, conv_grad, 0)
-    grow_copies = row_sends(gc.at[1], gc.at[H], grow, grow_s, grow_r)
-    for copy in grow_copies:
-        copy.start()
     ring1(0)
+    ring1(1)
+    ring1(2)
     lax.fori_loop(2 * B, 4 * B, conv_grad, 0)
     gedge_out[...] = gedge_f[...].astype(BF16)
     gedge_copies = edge_sends(gedge_out, gedge_in, gedge_s, gedge_r)
     for copy in gedge_copies:
         copy.start()
-    ring1(1)
-    ring1(2)
+    ring2(0)
+    ring2(1)
+    ring2(2)
+    grow_copies = row_sends(gc.at[1], gc.at[H], grow, grow_s, grow_r)
+    for copy in grow_copies:
+        copy.start()
     hd2_copy.wait_recv()
     head_pair = hd2[0] + hd2[1]
     for q in range(4):
         hdz_send[q] = head_pair[:, q * 128 : (q + 1) * 128]
     hdz_x[0]()
-    ring2(0)
-    ring2(1)
-    ring2(2)
     for copy in gedge_copies:
         copy.wait_recv()
     set_edges_of(gl, gr, gedge_in, CO)
+    back(1)
+    stage2(0)
+    stage2(1)
+    stage2(2)
     hdz_x[1]()
     head_line = hdz_send[z]
     for k in range(1, 4):
         head_line = head_line + hdz[flip(z, k)]
     hdy[y] = head_line
     hdy_x[0]()
-    back(1)
-    stage2(0)
-    stage2(1)
-    stage2(2)
-    hdy_x[1]()
-    hdx[x] = add_up(hdy, 4)
-    hdx_x[0]()
     back(2)
     stage3(0)
     stage3(1)
     stage3(2)
+    hdy_x[1]()
+    hdx[x] = add_up(hdy, 4)
+    hdx_x[0]()
+    collect3(0)
+    collect3(1)
+    collect3(2)
     for copy in grow_copies:
         copy.wait_recv()
     build_halo(grow, gedge_in, gl, gc, gr)
-    hdx_x[1]()
-    gh_out[...] = add_up(hdx, 4)
-    collect3(0)
-    collect3(1)
-    collect3(2)
     back(0)
     collect2(0)
     collect2(1)
     collect2(2)
+    hdx_x[1]()
+    gh_out[...] = add_up(hdx, 4)
     back(3)
     swap(0)
     swap(1)

time: 84.6 us -> 85.1 us (level)
  no operation moved by 1% of the time
where the time goes in v10:
time: 85.1 us; the launch traced here: 85 us
  Pallas kernels  84.2 us (99%)
    pallas_call x1, Pallas kernels, per_device(): pl.pallas_call(kernel, out_shape=(jax.ShapeDtypeStruct((TAPS, CI, 128), F...  80.7 us
    pallas_call x1, Pallas kernels, move_out(): pl.pallas_call(move_kernel, out_shape=tuple((jax.ShapeDtypeStruct(a.shape...  3.49 us

profile of v10, /device:TPU:1, one launch (start us, length us, event | category | flops | bytes accessed | tf_op | source)
XLA Modules:
  0.0 85.0 jit_solution(12370090214199192274)
XLA Ops:
  0.6 80.7 %shard_map.110 = (f32[9,256,128]{2,1,0:T(8,128)}, f32[1,128]{1,0:T(1,128)}, f32[1,128]{1,0:T(1,128)}, f32[4,128]{1,0:T(4,128)}, f32[4,4,128,256]{3,2,1,0:T(8,128)}) custom-call(bf16[4,4,128,256]{3,2,1,0:T(8,128)(2,1)} %feat.1, bf16[2304,512]{1,0:T(8,128)(2,1)} %bitcast.8, f32[1,512]{1,0:T(1,128)} %bitcast.11, f32[1,512]{1,0:T(1,128)} %bitcast.12, ...), custom_call_target="tpu_custom_call" | custom-call | flops 15000000512 | bytes 8000000 | tf_op jit(solution)/shard_map/pallas_call | solution.py:875
  81.3 3.5 %shard_map.111 = (f32[9,256,128]{2,1,0:T(8,128)}, f32[1,128]{1,0:T(1,128)}, f32[1,128]{1,0:T(1,128)}, f32[4,128]{1,0:T(4,128)}, f32[4,4,128,256]{3,2,1,0:T(8,128)}) custom-call(f32[9,256,128]{2,1,0:T(8,128)} %get-tuple-element.15.refs_0_, f32[1,128]{1,0:T(1,128)} %get-tuple-element.16.refs_1_, f32[1,128]{1,0:T(1,128)} %get-tuple-element.17.refs_2_, ...), custom_call_target="tpu_custom_call" | custom-call | tf_op jit(solution)/shard_map/pallas_call | solution.py:860

commit v11 on v10

--- a/solution.py
+++ b/solution.py
@@ -28,7 +28,8 @@
     head_ref,
     labels_ref,
     raster_ref,
-    gw_out,
+    gat2,
+    gat_other,
     gg_out,
     gb_out,
     gh_out,
@@ -94,8 +95,6 @@
     three_send,
     three_recv,
     gat3,
-    gat2,
-    gat_other,
     wsem,
     xrow_s,
     xrow_r,
@@ -720,17 +719,6 @@
     def swap(r):
         gather2[r][1]()
         o_copies[r].start()
-        unpack(r, gat2, core)
-
-    def unpack(r, src, half):
-        rows = src[r].reshape(384, 128)
-        spot = pl.ds(pl.multiple_of(half * 128, 128), 128)
-        for c in range(3):
-            gw_out[3 * r + c, spot, :] = rows[c * 128 : (c + 1) * 128].astype(F32)
-
-    def unpack_other(r):
-        o_copies[r].wait_recv()
-        unpack(r, gat_other, 1 - core)
 
     gi_copies = [
         [
@@ -817,8 +805,6 @@
     swap(0)
     swap(1)
     swap(2)
-    unpack_other(0)
-    unpack_other(1)
 
     for copy in [hd2_copy] + grow_copies + gedge_copies + a_copies:
         copy.wait_send()
@@ -830,40 +816,58 @@
     for line in gi_copies:
         for copy in line:
             copy.wait()
-    unpack_other(2)
     for copy in o_copies:
-        copy.wait_send()
-
-
-def move_kernel(*refs):
-    count = (len(refs) - 2) // 3
-    in_sem, out_sem = refs[-2:]
-    arrivals, leaves = [], []
-    for src, dst, held in zip(refs[:count], refs[count : 2 * count], refs[2 * count : 3 * count]):
-        size = src.shape[0] if len(src.shape) > 2 else 1
-        for i in range(size):
-            here, there, hold = (src.at[i], dst.at[i], held.at[i]) if size > 1 else (src, dst, held)
-            slot = len(arrivals)
-            arrivals.append(pltpu.make_async_copy(here, hold, in_sem.at[slot]))
-            leaves.append(pltpu.make_async_copy(hold, there, out_sem.at[slot]))
-    for copy in arrivals:
+        copy.wait()
+
+
+def finish_kernel(own, far, gg, gb, gh, gi, *refs):
+    gw_out, gg_out, gb_out, gh_out, gi_out = refs[0:5]
+    own_in, far_in, gg_in, gb_in, gh_in, gi_in, gw_in, in_sem, out_sem = refs[5:]
+    core = lax.rem(lax.axis_index("rows"), 2)
+    moves = [(gg, gg_in, gg_out), (gb, gb_in, gb_out), (gh, gh_in, gh_out)]
+    moves += [(gi.at[b], gi_in.at[b], gi_out.at[b]) for b in range(B)]
+    blocks = [pltpu.make_async_copy(a, b, in_sem.at[i]) for i, (a, b) in enumerate(((own, own_in), (far, far_in)))]
+    arrivals = [pltpu.make_async_copy(a, b, in_sem.at[2 + i]) for i, (a, b, _) in enumerate(moves)]
+    leaves = [pltpu.make_async_copy(b, c, out_sem.at[3 + i]) for i, (_, b, c) in enumerate(moves)]
+    wide = [
+        pltpu.make_async_copy(
+            gw_in.at[pl.ds(3 * r, 3)], gw_out.at[pl.ds(3 * r, 3)], out_sem.at[r]
+        )
+        for r in range(3)
+    ]
+    for copy in blocks + arrivals:
         copy.start()
+    for copy in blocks:
+        copy.wait()
+
+    for r in range(3):
+        for src, half in ((own_in, core), (far_in, 1 - core)):
+            rows = src[r].reshape(384, 128)
+            spot = pl.ds(pl.multiple_of(half * 128, 128), 128)
+            for c in range(3):
+                gw_in[3 * r + c, spot, :] = rows[c * 128 : (c + 1) * 128].astype(F32)
+        wide[r].start()
     for arrival, leave in zip(arrivals, leaves):
         arrival.wait()
         leave.start()
-    for leave in leaves:
-        leave.wait()
-
-
-def move_out(arrays):
+    for copy in wide + leaves:
+        copy.wait()
+
+
+def finish(arrays):
     anywhere = pl.BlockSpec(memory_space=pl.ANY)
+    wide = jax.ShapeDtypeStruct((TAPS, CI, 128), F32)
     return pl.pallas_call(
-        move_kernel,
-        out_shape=tuple(jax.ShapeDtypeStruct(a.shape, a.dtype) for a in arrays),
-        in_specs=[anywhere] * len(arrays),
-        out_specs=(anywhere,) * len(arrays),
+        finish_kernel,
+        out_shape=(wide,) + tuple(jax.ShapeDtypeStruct(a.shape, a.dtype) for a in arrays[2:]),
+        in_specs=[anywhere] * 6,
+        out_specs=(anywhere,) * 5,
         scratch_shapes=[pltpu.VMEM(a.shape, a.dtype) for a in arrays]
-        + [pltpu.SemaphoreType.DMA((16,)), pltpu.SemaphoreType.DMA((16,))],
+        + [
+            pltpu.VMEM(wide.shape, F32),
+            pltpu.SemaphoreType.DMA((9,)),
+            pltpu.SemaphoreType.DMA((10,)),
+        ],
         compiler_params=pltpu.CompilerParams(vmem_limit_bytes=60 * 1024 * 1024),
     )(*arrays)
 
@@ -875,14 +879,15 @@
     outs = pl.pallas_call(
         kernel,
         out_shape=(
-            jax.ShapeDtypeStruct((TAPS, CI, 128), F32),
+            jax.ShapeDtypeStruct((3, 4, 96, 128), BF16),
+            jax.ShapeDtypeStruct((3, 4, 96, 128), BF16),
             jax.ShapeDtypeStruct((1, 128), F32),
             jax.ShapeDtypeStruct((1, 128), F32),
             jax.ShapeDtypeStruct((4, 128), F32),
             jax.ShapeDtypeStruct((B, H, W, CI), F32),
         ),
         in_specs=[whole, pl.BlockSpec(memory_space=pl.ANY)] + [whole] * 5,
-        out_specs=(whole,) * 4 + (pl.BlockSpec(memory_space=pl.ANY),),
+        out_specs=(whole,) * 5 + (pl.BlockSpec(memory_space=pl.ANY),),
         scratch_shapes=[
             vmem((TAPS * CI, CO), BF16),
             vmem((256, 256), BF16),
@@ -945,8 +950,6 @@
             vmem((3, 4, 24, 128), F32),
             vmem((3, 4, 24, 128), F32),
             vmem((3, 4, 24, 128), F32),
-            vmem((3, 4, 96, 128), BF16),
-            vmem((3, 4, 96, 128), BF16),
             dma((TAPS,)),
             dma((2,)),
             dma((2,)),
@@ -984,7 +987,7 @@
         labels,
         raster,
     )
-    grad_weight, grad_gain, grad_bias, grad_head, grad_input = move_out(outs)
+    grad_weight, grad_gain, grad_bias, grad_head, grad_input = finish(outs)
     return (
         grad_weight.reshape(3, 3, CI, 128),
         grad_gain.reshape(128),

time: 85.1 us -> 84.4 us (level)
  no operation moved by 1% of the time
where the time goes in v11:
time: 84.4 us; the launch traced here: 84.2 us
  Pallas kernels  83.4 us (99%)
    pallas_call x1, Pallas kernels, per_device(): pl.pallas_call(kernel, out_shape=(jax.ShapeDtypeStruct((3, 4, 96, 128), B...  80.5 us
    pallas_call x1, Pallas kernels, finish(): pl.pallas_call(finish_kernel, out_shape=(wide,) + tuple((jax.ShapeDtypeSt...  2.96 us

profile of v11, /device:TPU:1, one launch (start us, length us, event | category | flops | bytes accessed | tf_op | source)
XLA Modules:
  0.0 84.2 jit_solution(7792666631178738497)
XLA Ops:
  0.6 80.5 %shard_map.110 = (bf16[3,4,96,128]{3,2,1,0:T(8,128)(2,1)}, bf16[3,4,96,128]{3,2,1,0:T(8,128)(2,1)}, f32[1,128]{1,0:T(1,128)}, f32[1,128]{1,0:T(1,128)}, f32[4,128]{1,0:T(4,128)}, /*index=5*/f32[4,4,128,256]{3,2,1,0:T(8,128)}) custom-call(bf16[4,4,128,256]{3,2,1,0:T(8,128)(2,1)} %feat.1, bf16[2304,512]{1,0:T(8,128)(2,1)} %bitcast.8, f32[1,512]{1,0:T(1,128)} %bitcast.11, ...), custom_call_target="tpu_custom_call" | custom-call | flops 15000000512 | bytes 8000000 | tf_op jit(solution)/shard_map/pallas_call | solution.py:879
  81.1 3.0 %shard_map.111 = (f32[9,256,128]{2,1,0:T(8,128)}, f32[1,128]{1,0:T(1,128)}, f32[1,128]{1,0:T(1,128)}, f32[4,128]{1,0:T(4,128)}, f32[4,4,128,256]{3,2,1,0:T(8,128)}) custom-call(bf16[3,4,96,128]{3,2,1,0:T(8,128)(2,1)} %get-tuple-element.16.own, bf16[3,4,96,128]{3,2,1,0:T(8,128)(2,1)} %get-tuple-element.17.far, f32[1,128]{1,0:T(1,128)} %get-tuple-element.18.gg, ...), custom_call_target="tpu_custom_call" | custom-call | tf_op jit(solution)/shard_map/pallas_call | solution.py:860

commit v12 on v11

--- a/solution.py
+++ b/solution.py
@@ -140,6 +140,15 @@
         return (me, flip(z, k)) if axis == "z" else (flip(me, (2 if axis == "y" else 8) * k), z)
 
     other = (flip(me, 1), z)
+
+    def around(axis, way, cross=0):
+        step = 1 if way == 0 else 3
+        if axis == "z":
+            return (flip(me, cross), lax.rem(z + step, 4))
+        stride = 2 if axis == "y" else 8
+        here = coords[axis]
+        return (flip(me + stride * (lax.rem(here + step, 4) - here), cross), z)
+
     up = lax.rem(me + 31, 32)
     down = lax.rem(me + 1, 32)
     west = lax.rem(z + 3, 4)
@@ -157,6 +166,10 @@
         greet((beyond, col))
     for k in range(1, 16):
         greet(dev16(k))
+
+    for axis in ("x", "y"):
+        for way in range(2):
+            greet(around(axis, way, 1))
 
     wcopies = []
     for t in range(TAPS):
@@ -200,7 +213,7 @@
 
     lax.fori_loop(0, B * H, build_x, 0)
 
-    pl.semaphore_wait(barrier, 25)
+    pl.semaphore_wait(barrier, 29)
 
     def remote(src, dst, ssem, rsem, device):
         return pltpu.make_async_remote_copy(
@@ -554,7 +567,7 @@
 
     for r in range(3):
         for c, piece in enumerate(kernel_grad(r, 1 - core)):
-            send_a[r, c] = piece.astype(BF16)
+            send_a[r, c * 128 : (c + 1) * 128] = piece.astype(BF16)
         a_copies[r].start()
 
     def conv_grad(i, carry):
@@ -589,26 +602,28 @@
             return with_conv[r, low:high, pl.ds(pl.multiple_of(q * 128, 128), 128)]
         return with_conv[r, pl.ds(pl.multiple_of(q * 96 + low, 16), high - low), :]
 
-    def around(axis, way):
-        step = 1 if way == 0 else 3
-        if axis == "z":
-            return (me, lax.rem(z + step, 4))
-        stride = 2 if axis == "y" else 8
-        here = coords[axis]
-        return (me + stride * (lax.rem(here + step, 4) - here), z)
+    def first_block(r, way):
+        q, half = lax.rem(coords[ORDERS[r][0]] + 2, 4), halves(r)
+        if r == 0:
+            cols = pl.ds(pl.multiple_of(q * 128, 128), 128)
+            return send_a.at[r, pl.ds(way * half, half), cols]
+        return send_a.at[r, pl.ds(pl.multiple_of(q * 96 + way * half, 16), half)]
 
     def ring1_copies(r):
         axis = ORDERS[r][0]
-        return [
-            remote(
-                ring1_send[r].at[way],
-                ring1_recv[r].at[way],
-                ring_s.at[r, way],
-                ring_r.at[r, way],
-                around(axis, way),
-            )
-            for way in range(2)
-        ]
+        copies = []
+        for way in range(2):
+            for cross in range(2):
+                copies.append(
+                    remote(
+                        first_block(r, way) if cross else ring1_send[r].at[way],
+                        ring1_recv[r].at[way, cross],
+                        ring_s.at[r, 4 * cross + way],
+                        ring_r.at[r, 4 * cross + way],
+                        around(axis, way, cross),
+                    )
+                )
+        return copies
 
     def ring2_copies(r):
         axis = ORDERS[r][0]
@@ -624,9 +639,8 @@
         ]
 
     def ring1(r):
-        a_copies[r].wait_recv()
         for c, piece in enumerate(kernel_grad(r, core)):
-            with_conv[r, c * 128 : (c + 1) * 128] = piece + recv_a[r, c].astype(F32)
+            with_conv[r, c * 128 : (c + 1) * 128] = piece
         here, half = coords[ORDERS[r][0]], halves(r)
         ring1_send[r][0] = block(r, here + 2, 0, half).astype(BF16)
         ring1_send[r][1] = block(r, here + 2, half, 2 * half).astype(BF16)
@@ -634,11 +648,13 @@
             copy.start()
 
     def ring2(r):
+        a_copies[r].wait_recv()
+        with_conv[r, 0:384] += recv_a[r].astype(F32)
         for copy in ring1_copies(r):
             copy.wait_recv()
         here, half = coords[ORDERS[r][0]], halves(r)
-        low = ring1_recv[r][0].astype(F32)
-        high = ring1_recv[r][1].astype(F32)
+        low = ring1_recv[r][0, 0].astype(F32) + ring1_recv[r][0, 1].astype(F32)
+        high = ring1_recv[r][1, 0].astype(F32) + ring1_recv[r][1, 1].astype(F32)
         ring2_send[r][0, 0:half] = (block(r, here + 1, 0, half) + low).astype(BF16)
         ring2_send[r][0, half : 2 * half] = block(r, here + 1, half, 2 * half).astype(BF16)
         ring2_send[r][1, 0:half] = block(r, here + 3, 0, half).astype(BF16)
@@ -749,10 +765,10 @@
         for copy in gi_copies[h]:
             copy.start()
 
-    lax.fori_loop(0, 2 * B, conv_grad, 0)
     ring1(0)
     ring1(1)
     ring1(2)
+    lax.fori_loop(0, 2 * B, conv_grad, 0)
     lax.fori_loop(2 * B, 4 * B, conv_grad, 0)
     gedge_out[...] = gedge_f[...].astype(BF16)
     gedge_copies = edge_sends(gedge_out, gedge_in, gedge_s, gedge_r)
@@ -930,14 +946,14 @@
             vmem((3, 3, CI, CO), F32),
             vmem((3, 3 * CI, CO), F32),
             vmem((3, 3 * CI, 128), F32),
-            vmem((3, 3, 128, CO), BF16),
-            vmem((3, 3, 128, CO), BF16),
+            vmem((3, 384, CO), BF16),
+            vmem((3, 384, CO), BF16),
             vmem((2, 192, 128), BF16),
             vmem((2, 48, CO), BF16),
             vmem((2, 48, CO), BF16),
-            vmem((2, 192, 128), BF16),
-            vmem((2, 48, CO), BF16),
-            vmem((2, 48, CO), BF16),
+            vmem((2, 2, 192, 128), BF16),
+            vmem((2, 2, 48, CO), BF16),
+            vmem((2, 2, 48, CO), BF16),
             vmem((2, 384, 128), BF16),
             vmem((2, 96, CO), BF16),
             vmem((2, 96, CO), BF16),
@@ -964,8 +980,8 @@
         + [
             dma((3,)),
             dma((3,)),
-            dma((3, 4)),
-            dma((3, 4)),
+            dma((3, 6)),
+            dma((3, 6)),
             dma((4, 3)),
             dma((4, 3)),
             dma((3,)),

time: 84.4 us -> 82.2 us (0.974)
  Pallas kernels: 83.4 us -> 81.2 us
    pallas_call x1, Pallas kernels: 80.5 us -> 78.3 us  [per_device(): pl.pallas_call(kernel, out_shape=(jax.ShapeDtypeStruct((3, 4, 96, 128), B...]
where the time goes in v12:
time: 82.2 us; the launch traced here: 82 us
  Pallas kernels  81.2 us (99%)
    pallas_call x1, Pallas kernels, per_device(): pl.pallas_call(kernel, out_shape=(jax.ShapeDtypeStruct((3, 4, 96, 128), B...  78.3 us
    pallas_call x1, Pallas kernels, finish(): pl.pallas_call(finish_kernel, out_shape=(wide,) + tuple((jax.ShapeDtypeSt...  2.96 us

profile of v12, /device:TPU:1, one launch (start us, length us, event | category | flops | bytes accessed | tf_op | source)
XLA Modules:
  0.0 82.0 jit_solution(6975130447344252376)
XLA Ops:
  0.6 78.3 %shard_map.110 = (bf16[3,4,96,128]{3,2,1,0:T(8,128)(2,1)}, bf16[3,4,96,128]{3,2,1,0:T(8,128)(2,1)}, f32[1,128]{1,0:T(1,128)}, f32[1,128]{1,0:T(1,128)}, f32[4,128]{1,0:T(4,128)}, /*index=5*/f32[4,4,128,256]{3,2,1,0:T(8,128)}) custom-call(bf16[4,4,128,256]{3,2,1,0:T(8,128)(2,1)} %feat.1, bf16[2304,512]{1,0:T(8,128)(2,1)} %bitcast.8, f32[1,512]{1,0:T(1,128)} %bitcast.11, ...), custom_call_target="tpu_custom_call" | custom-call | flops 15000000512 | bytes 8000000 | tf_op jit(solution)/shard_map/pallas_call | solution.py:895
  78.9 3.0 %shard_map.111 = (f32[9,256,128]{2,1,0:T(8,128)}, f32[1,128]{1,0:T(1,128)}, f32[1,128]{1,0:T(1,128)}, f32[4,128]{1,0:T(4,128)}, f32[4,4,128,256]{3,2,1,0:T(8,128)}) custom-call(bf16[3,4,96,128]{3,2,1,0:T(8,128)(2,1)} %get-tuple-element.16.own, bf16[3,4,96,128]{3,2,1,0:T(8,128)(2,1)} %get-tuple-element.17.far, f32[1,128]{1,0:T(1,128)} %get-tuple-element.18.gg, ...), custom_call_target="tpu_custom_call" | custom-call | tf_op jit(solution)/shard_map/pallas_call | solution.py:876
